TPU v7x, 512 devices: a whole 4x4x16 slice. The times are simulated.
512 devices in a mesh: blk: 16 (over z_hi, y, core), fsdp: 32 (over z_lo, x).
Axes of the slice: x: 4, y: 4, z: 16 (z_hi: 2, z_lo: 8; z = z_hi * 8 + z_lo), core: 2. Of those that a mesh axis runs over, the one named last changes fastest.
Arguments:
- tokens: bfloat16 [16, 4096, 8192], P('blk', 'fsdp'), may hold values from -6 to 6
- norm_gain: float32 [8192], replicated, may hold values from 0.1 to 1.9
- adapt_in: float32 [16, 8192, 64], P('blk', 'fsdp'), may hold values from -6 to 6
- adapt_out: float32 [16, 8192, 64], P('blk', 'fsdp'), may hold values from -6 to 6
- upstream: bfloat16 [16, 4096, 8192], P('blk', 'fsdp'), may hold values from -6 to 6
Outputs:
- mixed_in: float32 [16, 8192, 64], P('blk', 'fsdp')
- mixed_out: float32 [16, 8192, 64], P('blk', 'fsdp')
All inputs are finite; a program needn't handle non-finite values.
Results may differ from a plain program's by a relative error of at most 0.0029.
Values may be sent and summed in bfloat16 or wider, within the bound.
No kernel may reach another device: no remote copies, remote signals or barrier semaphores. Data moves between devices by JAX's collectives and lax.ppermute only.
A program may use at most 64 MiB of HBM per device.

v0:
```python
import jax
import jax.numpy as jnp
from jax import lax
from jax.sharding import PartitionSpec as P

D = 8192
R = 64


learning_rate = 4.0
epsilon = 1e-05


def shifted(array, axis, by):
    count = lax.axis_size(axis)
    return lax.ppermute(array, axis, [(i, (i + by) % count) for i in range(count)])


def local(tokens, norm_gain, adapt_in, adapt_out, upstream):
    inv_width = D ** (-0.5)
    inv_rank = R ** (-0.5)
    hidden = tokens[0]
    cotangent = upstream[0]
    master_in = adapt_in[0]
    master_out = adapt_out[0]
    tok_count = hidden.shape[0]
    group_size = lax.axis_size("fsdp")
    step_size = learning_rate / (tok_count * group_size) ** 0.5
    wide = hidden.astype(jnp.float32)
    normed = (
        wide * lax.rsqrt(jnp.mean(wide * wide, axis=-1, keepdims=True) + epsilon) * norm_gain
    ).astype(jnp.bfloat16)
    low_in = master_in.astype(jnp.bfloat16)
    low_out = master_out.astype(jnp.bfloat16)
    factor_acc = jnp.dot(
        normed,
        lax.all_gather(low_in, "fsdp", axis=0, tiled=True),
        preferred_element_type=jnp.float32,
    )
    pulled_acc = jnp.dot(
        cotangent,
        lax.all_gather(low_out, "fsdp", axis=0, tiled=True),
        preferred_element_type=jnp.float32,
    )
    factor = (factor_acc * inv_width).astype(jnp.bfloat16)
    pulled = (pulled_acc * inv_rank).astype(jnp.bfloat16)
    contract = (((0,), (0,)), ((), ()))
    term_in = (
        lax.dot_general(normed, pulled, contract, preferred_element_type=jnp.float32) * inv_width
    )
    term_out = (
        lax.dot_general(cotangent, factor, contract, preferred_element_type=jnp.float32) * inv_rank
    )
    summed = lax.psum_scatter(
        jnp.concatenate([term_in, term_out], axis=1), "fsdp", scatter_dimension=0, tiled=True
    )
    grad_in = summed[:, :R]
    grad_out = summed[:, R:]
    stepped_in = master_in - step_size * grad_in
    stepped_out = master_out - step_size * grad_out
    lower_in, lower_out = shifted((stepped_in, stepped_out), "blk", 1)
    upper_in, upper_out = shifted((stepped_in, stepped_out), "blk", -1)
    mixed_in = (lower_in + stepped_in + upper_in) / 3.0
    mixed_out = (lower_out + stepped_out + upper_out) / 3.0
    return (mixed_in[None], mixed_out[None])


def solution(mesh):
    in_specs = (
        P("blk", "fsdp", None),
        P(),
        P("blk", "fsdp", None),
        P("blk", "fsdp", None),
        P("blk", "fsdp", None),
    )
    out_specs = (P("blk", "fsdp", None), P("blk", "fsdp", None))
    return jax.shard_map(local, mesh=mesh, in_specs=in_specs, out_specs=out_specs, check_vma=False)
```

profile of v0, /device:TPU:25, one launch (start us, length us, event | category | flops | bytes accessed | tf_op | source)
XLA Modules:
  0.0 648.0 jit_solution(17724820712778504849)
XLA Ops:
  7.2 0.0 copy-start
  7.2 0.0 copy-start.3
  7.2 0.0 all-gather.3.cloned.1.call-start
  7.2 1.6 bitcast_convert_fusion
  8.8 0.0 all-gather.3.cloned.1.call-update
  8.9 0.0 all-gather.5.cloned.1.call-start
  8.9 1.5 bitcast_convert_fusion.1
  10.4 0.0 all-gather.5.cloned.1.call-update
  10.4 0.0 reduce-scatter.2.cloned.1.call-start
  10.4 2.1 fusion.1
  12.5 163.1 %all-gather.3.cloned.1.call-done = bf16[8192,64]{0,1:T(8,128)(2,1)} async-done(((bf16[256,64]{0,1:T(8,128)(2,1)}), bf16[8192,64]{0,1:T(8,128)(2,1)}) %all-gather.3.cloned.1.call-update) | async-done | bytes 1048592 | tf_op jit(solution)/shard_map/all_gather | solution.py:42
  175.7 0.0 copy-done
  175.7 0.0 copy-done.3
  175.7 4.8 convolution_multiply_fusion.1
  180.5 167.7 %all-gather.5.cloned.1.call-done = bf16[8192,64]{0,1:T(8,128)(2,1)} async-done(((bf16[256,64]{0,1:T(8,128)(2,1)}), bf16[8192,64]{0,1:T(8,128)(2,1)}) %all-gather.5.cloned.1.call-update) | async-done | bytes 1048592 | tf_op jit(solution)/shard_map/all_gather | solution.py:37
  348.2 4.9 fusion
  353.1 4.6 pad_maximum_fusion
  357.7 0.0 copy-start.1
  357.7 0.0 copy-start.2
  357.7 0.0 reduce-scatter.2.cloned.1.call-update
  357.8 232.5 %reduce-scatter.2.cloned.1.call-done = f32[256,128]{0,1:T(8,128)} async-done(((f32[8192,128]{0,1:T(8,128)}), f32[256,128]{0,1:T(8,128)}) %reduce-scatter.2.cloned.1.call-update) | async-done | bytes 131088 | tf_op jit(solution)/shard_map/reduce_scatter | solution.py:54
  590.3 0.0 copy-done.1
  590.3 0.0 copy-done.2
  590.3 0.9 fusion.19
  591.2 28.8 %collective-permute-start.3 = (f32[256,64]{0,1:T(8,128)S(1)}, f32[256,64]{0,1:T(8,128)S(1)}, u32[]{:S(2)}, u32[]{:S(2)}) collective-permute-start(f32[256,64]{0,1:T(8,128)S(1)} %get-tuple-element.2), channel_id=1, source_target_pairs={{0,480},{32,0},{64,32},{96,64},{128,96},{160,128},{192,160},{224,1... | collective-permute-start | bytes 196616 | tf_op jit(solution)/shard_map/ppermute | solution.py:16
  620.0 3.1 collective-permute-start.2
  623.1 1.9 collective-permute-start.1
  625.0 14.5 %collective-permute-start = (f32[256,64]{0,1:T(8,128)S(1)}, f32[256,64]{0,1:T(8,128)S(1)}, u32[]{:S(2)}, u32[]{:S(2)}) collective-permute-start(f32[256,64]{0,1:T(8,128)S(1)} %get-tuple-element.3), channel_id=1, source_target_pairs={{0,32},{32,64},{64,96},{96,128},{128,160},{160,192},{192,224},{224... | collective-permute-start | bytes 196616 | tf_op jit(solution)/shard_map/ppermute | solution.py:16
  639.5 0.0 collective-permute-done.3
  639.5 0.0 collective-permute-done.2
  639.5 0.6 multiply_bitcast_fusion
  640.2 0.0 collective-permute-done.1
  640.2 0.6 collective-permute-done
  640.8 0.6 multiply_bitcast_fusion.1
  (1 shorter events, 0.0 us)
Async XLA Ops:
  7.2 168.5 %copy-start = (bf16[1,128,8192]{2,1,0:T(8,128)(2,1)S(1)}, bf16[1,128,8192]{2,1,0:T(8,128)(2,1)}, u32[]{:S(2)}) copy-start(bf16[1,128,8192]{2,1,0:T(8,128)(2,1)} %param.9) | copy-start | bytes 6291460
  7.2 168.5 %copy-start.3 = (f32[8192]{0:T(1024)S(1)}, f32[8192]{0:T(1024)}, u32[]{:S(2)}) copy-start(f32[8192]{0:T(1024)} %param.6) | copy-start | bytes 98308
  7.2 168.5 %all-gather.3.cloned.1.call-start = ((), (), s32[]{:S(2)}) async-start(), calls=%async_computation.1 | async-start | bytes 1081344 | tf_op jit(solution)/shard_map/all_gather | solution.py:42
  8.9 339.4 %all-gather.5.cloned.1.call-start = ((), (), s32[]{:S(2)}) async-start(), calls=%async_computation.2 | async-start | bytes 1081344 | tf_op jit(solution)/shard_map/all_gather | solution.py:37
  10.4 579.9 %reduce-scatter.2.cloned.1.call-start = ((), (), s32[]{:S(2)}) async-start(), calls=%async_computation.3 | async-start | bytes 4325376 | tf_op jit(solution)/shard_map/reduce_scatter | solution.py:54
  357.7 232.6 %copy-start.1 = (f32[1,256,64]{1,2,0:T(8,128)S(1)}, f32[1,256,64]{1,2,0:T(8,128)}, u32[]{:S(2)}) copy-start(f32[1,256,64]{1,2,0:T(8,128)} %param.8) | copy-start | bytes 196612
  357.7 232.6 %copy-start.2 = (f32[1,256,64]{1,2,0:T(8,128)S(1)}, f32[1,256,64]{1,2,0:T(8,128)}, u32[]{:S(2)}) copy-start(f32[1,256,64]{1,2,0:T(8,128)} %param.7) | copy-start | bytes 196612
  591.2 48.3 %collective-permute-start.3 = (f32[256,64]{0,1:T(8,128)S(1)}, f32[256,64]{0,1:T(8,128)S(1)}, u32[]{:S(2)}, u32[]{:S(2)}) collective-permute-start(f32[256,64]{0,1:T(8,128)S(1)} %get-tuple-element.2), channel_id=1, source_target_pairs={{0,480},{32,0},{64,32},{96,64},{128,96},{160,128},{192,160},{224,1... | collective-permute-start | bytes 196616 | tf_op jit(solution)/shard_map/ppermute | solution.py:16
  620.0 19.5 %collective-permute-start.2 = (f32[256,64]{0,1:T(8,128)S(1)}, f32[256,64]{0,1:T(8,128)S(1)}, u32[]{:S(2)}, u32[]{:S(2)}) collective-permute-start(f32[256,64]{0,1:T(8,128)S(1)} %get-tuple-element.2), channel_id=1, source_target_pairs={{0,32},{32,64},{64,96},{96,128},{128,160},{160,192},{192,224},{224... | collective-permute-start | bytes 196616 | tf_op jit(solution)/shard_map/ppermute | solution.py:16
  623.1 17.1 %collective-permute-start.1 = (f32[256,64]{0,1:T(8,128)S(1)}, f32[256,64]{0,1:T(8,128)S(1)}, u32[]{:S(2)}, u32[]{:S(2)}) collective-permute-start(f32[256,64]{0,1:T(8,128)S(1)} %get-tuple-element.3), channel_id=1, source_target_pairs={{0,480},{32,0},{64,32},{96,64},{128,96},{160,128},{192,160},{224,1... | collective-permute-start | bytes 196616 | tf_op jit(solution)/shard_map/ppermute | solution.py:16
  625.0 15.8 %collective-permute-start = (f32[256,64]{0,1:T(8,128)S(1)}, f32[256,64]{0,1:T(8,128)S(1)}, u32[]{:S(2)}, u32[]{:S(2)}) collective-permute-start(f32[256,64]{0,1:T(8,128)S(1)} %get-tuple-element.3), channel_id=1, source_target_pairs={{0,32},{32,64},{64,96},{96,128},{128,160},{160,192},{192,224},{224... | collective-permute-start | bytes 196616 | tf_op jit(solution)/shard_map/ppermute | solution.py:16
Sparse Core Ops, SparseCore 0:
  10.6 165.0 all-gather.2
  178.3 169.9 all-gather.4
  357.9 232.3 reduce-scatter.1
where the time goes:
time: 654 us; the launch traced here: 648 us
  waiting for transfers between devices  564 us (86%)
  starting transfers between devices  48.4 us (7%)
  between operations  13.8 us (2%)
  other arithmetic  11.9 us (2%)
  matrix products  9.74 us (1%)
    reduce_scatter x1, waiting for transfers between devices, local(): lax.psum_scatter(jnp.concatenate([term_in, term_out], axis=1), 'fsdp', sc...  233 us
    all_gather x1, waiting for transfers between devices, local(): lax.all_gather(low_in, 'fsdp', axis=0, tiled=True)  168 us
    all_gather x1, waiting for transfers between devices, local(): lax.all_gather(low_out, 'fsdp', axis=0, tiled=True)  163 us
    ppermute x4, starting transfers between devices, shifted(): lax.ppermute(array, axis, [(i, (i + by) % count) for i in range(count)])  48.3 us
  transfers between devices with their start and end apart: 7, of which 4 were waited for; matrix products, arithmetic and copies ran while one was open for 1% of the time, Pallas kernels for 0%

commit v1 on v0

v1 whole, which is shorter than its diff:
```python
import jax
import jax.numpy as jnp
from jax import lax
from jax.experimental import pallas as pl
from jax.experimental.pallas import tpu as pltpu
from jax.sharding import Mesh
from jax.sharding import PartitionSpec as P

D = 8192
R = 64
TOKENS = 4096
GROUPS = 16
NX = 4
NZ = 8
TOK = TOKENS // (NX * NZ)
OWN = D // (NX * NZ)
FEAT = D // NX

learning_rate = 4.0
epsilon = 1e-05

inv_width = D ** (-0.5)
inv_rank = R ** (-0.5)
step_size = learning_rate / TOKENS**0.5

LAST = (((1,), (1,)), ((), ()))
VMEM_LIMIT = 40 * 1024 * 1024


def prep_kernel(tok_ref, gain_ref, up_ref, out_ref):
    wide = tok_ref[...].astype(jnp.float32)
    scale = lax.rsqrt(jnp.mean(wide * wide, axis=-1, keepdims=True) + epsilon)
    for x in range(NX):
        for z in range(NZ):
            src = slice((z * NX + x) * OWN, (z * NX + x + 1) * OWN)
            dst = slice(z * OWN, (z + 1) * OWN)
            part = tok_ref[:, src].astype(jnp.float32) * scale * gain_ref[:, src]
            out_ref[x, 0, :, dst] = part.astype(jnp.bfloat16)
            out_ref[x, 1, :, dst] = up_ref[:, src]


def prep(tokens, gain, upstream):
    rows = 32
    return pl.pallas_call(
        prep_kernel,
        grid=(TOK // rows,),
        in_specs=[
            pl.BlockSpec((rows, D), lambda i: (i, 0)),
            pl.BlockSpec((1, D), lambda i: (0, 0)),
            pl.BlockSpec((rows, D), lambda i: (i, 0)),
        ],
        out_specs=pl.BlockSpec((NX, 2, rows, FEAT), lambda i: (0, 0, i, 0)),
        out_shape=jax.ShapeDtypeStruct((NX, 2, TOK, FEAT), jnp.bfloat16),
        compiler_params=pltpu.CompilerParams(vmem_limit_bytes=VMEM_LIMIT),
        cost_estimate=pl.CostEstimate(
            flops=6 * TOK * D, bytes_accessed=8 * TOK * D, transcendentals=TOK
        ),
    )(tokens, gain, upstream)


def project_kernel(feat_ref, low_ref, out_ref):
    low = jnp.concatenate([low_ref[z] for z in range(NZ)], axis=1).astype(jnp.bfloat16)
    fac = lax.dot_general(low[:R], feat_ref[0, 0], LAST, preferred_element_type=jnp.float32)
    pul = lax.dot_general(low[R:], feat_ref[0, 1], LAST, preferred_element_type=jnp.float32)
    for x in range(NX):
        out_ref[x, 0, :R, :] = fac
        out_ref[x, 0, R:, :] = pul


def project(feat, low):
    return pl.pallas_call(
        project_kernel,
        grid=(NX,),
        in_specs=[
            pl.BlockSpec((1, 2, TOK, FEAT), lambda i: (i, 0, 0, 0)),
            pl.BlockSpec((NZ, 2 * R, OWN), lambda i: (0, 0, 0)),
        ],
        out_specs=pl.BlockSpec((NX, 1, 2 * R, TOK), lambda i: (0, i, 0, 0)),
        out_shape=jax.ShapeDtypeStruct((NX, NX, 2 * R, TOK), jnp.float32),
        compiler_params=pltpu.CompilerParams(vmem_limit_bytes=VMEM_LIMIT),
        cost_estimate=pl.CostEstimate(
            flops=4 * NX * TOK * FEAT * R, bytes_accessed=6 * 1024 * 1024, transcendentals=0
        ),
    )(feat, low)


def grads_kernel(part_ref, feat_ref, out_ref):
    total = part_ref[0]
    for x in range(1, NX):
        total = total + part_ref[x]
    fac = jnp.concatenate([total[s, :R] for s in range(NX)], axis=1) * inv_width
    pul = jnp.concatenate([total[s, R:] for s in range(NX)], axis=1) * inv_rank
    normed = feat_ref[:, 0].reshape(NX * TOK, OWN)
    cotangent = feat_ref[:, 1].reshape(NX * TOK, OWN)
    g_in = jnp.dot(pul.astype(jnp.bfloat16), normed, preferred_element_type=jnp.float32)
    g_out = jnp.dot(fac.astype(jnp.bfloat16), cotangent, preferred_element_type=jnp.float32)
    out_ref[0, :R, :] = (g_in * inv_width).astype(jnp.bfloat16)
    out_ref[0, R:, :] = (g_out * inv_rank).astype(jnp.bfloat16)


def grads(part, feat):
    return pl.pallas_call(
        grads_kernel,
        grid=(NZ,),
        in_specs=[
            pl.BlockSpec((NX, NX, 2 * R, TOK), lambda i: (0, 0, 0, 0)),
            pl.BlockSpec((NX, 2, TOK, OWN), lambda i: (0, 0, 0, i)),
        ],
        out_specs=pl.BlockSpec((1, 2 * R, OWN), lambda i: (i, 0, 0)),
        out_shape=jax.ShapeDtypeStruct((NZ, 2 * R, OWN), jnp.bfloat16),
        compiler_params=pltpu.CompilerParams(vmem_limit_bytes=VMEM_LIMIT),
        cost_estimate=pl.CostEstimate(
            flops=4 * NX * TOK * FEAT * R, bytes_accessed=6 * 1024 * 1024, transcendentals=0
        ),
    )(part, feat)


def shifted(array, by):
    return lax.ppermute(array, "blk", [(i, (i + by) % GROUPS) for i in range(GROUPS)])


def local(tokens, norm_gain, adapt_in, adapt_out, upstream):
    master = jnp.concatenate([adapt_in[0].T, adapt_out[0].T], axis=0)
    low = lax.all_gather(master[None], "z", axis=0, tiled=True)
    base = shifted(master, 1) + master + shifted(master, -1)

    feat = prep(tokens[0], norm_gain[None], upstream[0])
    feat = lax.all_to_all(feat, "x", 0, 0, tiled=True)
    part = project(feat, low)
    part = lax.all_to_all(part, "x", 0, 0, tiled=True)
    pieces = grads(part, feat)
    pieces = lax.all_to_all(pieces, "z", 0, 0, tiled=True)
    grad = jnp.sum(pieces.astype(jnp.float32), axis=0)
    sent = grad.astype(jnp.bfloat16)
    lower, upper = shifted(sent, 1), shifted(sent, -1)
    around = lower.astype(jnp.float32) + grad + upper.astype(jnp.float32)
    mixed = (base - step_size * around) / 3.0
    return (mixed[:R].T[None], mixed[R:].T[None])


def solution(mesh):
    mesh = Mesh(mesh.devices.reshape(GROUPS, NZ, NX), ("blk", "z", "x"))
    split = P("blk", ("z", "x"), None)
    in_specs = (split, P(), split, split, split)
    return jax.shard_map(
        local, mesh=mesh, in_specs=in_specs, out_specs=(split, split), check_vma=False
    )
```

time: 654 us -> 183 us (0.28)
  the two profiles are of different devices: /device:TPU:25 before, /device:TPU:2 now
where the time goes in v1:
time: 183 us; the launch traced here: 182 us
  waiting for transfers between devices  109 us (60%)
  starting transfers between devices  24.7 us (13%)
  blocking collectives  14.2 us (8%)
  between operations  14.1 us (8%)
  Pallas kernels  12 us (7%)
  local copies, waits for them, and re-layouts  7.8 us (4%)
    all_gather x1, waiting for transfers between devices, local(): low = lax.all_gather(master[None], 'z', axis=0, tiled=True)  68.8 us
    all_to_all x1, waiting for transfers between devices, local(): pieces = lax.all_to_all(pieces, 'z', 0, 0, tiled=True)  24.3 us
    ppermute x4, waiting for transfers between devices, shifted(): lax.ppermute(array, 'blk', [(i, (i + by) % GROUPS) for i in range(GROUPS)])  15.4 us
    all_to_all x1, blocking collectives, local(): part = lax.all_to_all(part, 'x', 0, 0, tiled=True)  14.2 us
    all_to_all x1, starting transfers between devices, local(): feat = lax.all_to_all(feat, 'x', 0, 0, tiled=True)  10.8 us
    ppermute x4, starting transfers between devices, shifted(): lax.ppermute(array, 'blk', [(i, (i + by) % GROUPS) for i in range(GROUPS)])  10.3 us
    unnamed x16, local copies, waits for them, and re-layouts  7.14 us
    pallas_call x1, Pallas kernels, grads(): pl.pallas_call(grads_kernel, grid=(NZ,), in_specs=[pl.BlockSpec((NX, NX,...  6.41 us
  transfers between devices with their start and end apart: 7, of which 4 were waited for; matrix products, arithmetic and copies ran while one was open for 0% of the time, Pallas kernels for 0%

profile of v1, /device:TPU:2, one launch (start us, length us, event | category | flops | bytes accessed | tf_op | source)
XLA Modules:
  0.0 182.1 jit_solution(5897673471107692661)
XLA Ops:
  7.2 0.0 copy-start.1
  7.2 1.6 copy-done.1
  8.8 0.0 copy-start.2
  8.8 1.6 copy-done.2
  10.3 0.0 copy-start.4
  10.3 0.8 copy-done.4
  11.1 1.5 shard_map.68
  12.6 0.0 copy-start
  12.6 2.0 %copy-done = bf16[4,2,128,2048]{3,2,1,0:T(8,128)(2,1)} copy-done((bf16[4,2,128,2048]{3,2,1,0:T(8,128)(2,1)}, bf16[4,2,128,2048]{3,2,1,0:T(8,128)(2,1)S(1)}, u32[]{:S(2)}) %copy-start) | copy-done | bytes 4194328
  14.6 0.0 copy-start.6
  14.6 0.0 copy-start.7
  14.6 10.8 %all-to-all-start = ((bf16[4,2,128,2048]{3,2,1,0:T(8,128)(2,1)}), bf16[4,2,128,2048]{3,2,1,0:T(8,128)(2,1)}, u32[]{:S(2)}, u32[]{:S(2)}) async-start(bf16[4,2,128,2048]{3,2,1,0:T(8,128)(2,1)} %copy-done), calls=%async_computation | async-start | bytes 8388608 | tf_op jit(solution)/shard_map/all_to_all | solution.py:128
  25.4 0.0 all-gather.3.cloned.1.call-start
  25.4 0.0 copy-done.6
  25.4 0.0 copy-done.7
  25.4 0.7 pad_maximum_fusion
  26.1 0.0 all-gather.3.cloned.1.call-update
  26.2 68.8 %all-gather.3.cloned.1.call-done = f32[1024,256]{1,0:T(8,128)} async-done(((f32[128,256]{1,0:T(8,128)}), f32[1024,256]{1,0:T(8,128)}) %all-gather.3.cloned.1.call-update) | async-done | bytes 1048592 | tf_op jit(solution)/shard_map/all_gather | solution.py:124
  94.9 0.0 all-to-all-done.feat_ref
  94.9 0.0 copy-start.3
  94.9 1.2 copy-done.3
  96.2 4.1 %shard_map.69 = f32[4,4,128,128]{3,2,1,0:T(8,128)S(1)} custom-call(bf16[4,2,128,2048]{3,2,1,0:T(8,128)(2,1)} %all-to-all-done.feat_ref, f32[8,128,256]{2,1,0:T(8,128)S(1)} %bitcast.20), custom_call_target="tpu_custom_call" | custom-call | flops 268435456 | bytes 6291456 | tf_op jit(solution)/shard_map/pallas_call | solution.py:71
  100.3 0.0 copy-start.5
  100.3 14.2 %all_to_all.15.part_ref = f32[4,4,128,128]{3,2,1,0:T(8,128)S(1)} all-to-all(f32[4,4,128,128]{3,2,1,0:T(8,128)S(1)} %shard_map.69), channel_id=1, replica_groups=mesh['blk'=16,'z'=8,'x'=4] {'x'}, dimensions={0} | all-to-all | bytes 2097152 | tf_op jit(solution)/shard_map/all_to_all | solution.py:130
  114.4 6.4 %shard_map.70 = bf16[8,128,256]{2,1,0:T(8,128)(2,1)} custom-call(f32[4,4,128,128]{3,2,1,0:T(8,128)S(1)} %all_to_all.15.part_ref, bf16[4,2,128,2048]{3,2,1,0:T(8,128)(2,1)} %all-to-all-done.feat_ref), custom_call_target="tpu_custom_call" | custom-call | flops 268435456 | bytes 6291456 | tf_op jit(solution)/shard_map/pallas_call | solution.py:102
  120.9 3.5 %all-to-all-start.2 = ((bf16[8,128,256]{2,1,0:T(8,128)(2,1)}), bf16[8,128,256]{2,1,0:T(8,128)(2,1)S(1)}, u32[]{:S(2)}, u32[]{:S(2)}) async-start(bf16[8,128,256]{2,1,0:T(8,128)(2,1)} %shard_map.70), calls=%async_computation.2 | async-start | bytes 1048576 | tf_op jit(solution)/shard_map/all_to_all | solution.py:132
  124.4 0.0 copy-done.5
  124.4 4.1 %collective-permute-start.1 = (f32[128,256]{1,0:T(8,128)S(1)}, f32[128,256]{1,0:T(8,128)S(1)}, u32[]{:S(2)}, u32[]{:S(2)}) collective-permute-start(f32[128,256]{1,0:T(8,128)S(1)} %copy-done.5), channel_id=1, source_target_pairs={{0,480},{32,0},{64,32},{96,64},{128,96},{160,128},{192,160},{224,1... | collective-permute-start | bytes 393224 | tf_op jit(solution)/shard_map/ppermute | solution.py:119
  128.4 1.9 %collective-permute-start = (f32[128,256]{1,0:T(8,128)S(1)}, f32[128,256]{1,0:T(8,128)S(1)}, u32[]{:S(2)}, u32[]{:S(2)}) collective-permute-start(f32[128,256]{1,0:T(8,128)S(1)} %copy-done.5), channel_id=1, source_target_pairs={{0,32},{32,64},{64,96},{96,128},{128,160},{160,192},{192,224},{224... | collective-permute-start | bytes 393224 | tf_op jit(solution)/shard_map/ppermute | solution.py:119
  130.4 24.3 %all-to-all-done.2 = bf16[8,128,256]{2,1,0:T(8,128)(2,1)S(1)} async-done(((bf16[8,128,256]{2,1,0:T(8,128)(2,1)}), bf16[8,128,256]{2,1,0:T(8,128)(2,1)S(1)}, u32[]{:S(2)}, u32[]{:S(2)}) %all-to-all-start.2) | async-done | bytes 524320 | tf_op jit(solution)/shard_map/all_to_all | solution.py:132
  154.7 0.1 convert_reduce_fusion
  154.8 1.9 %collective-permute-start.3 = (bf16[128,256]{1,0:T(8,128)(2,1)S(1)}, bf16[128,256]{1,0:T(8,128)(2,1)S(1)}, u32[]{:S(2)}, u32[]{:S(2)}) collective-permute-start(bf16[128,256]{1,0:T(8,128)(2,1)S(1)} %convert_element_type.13), channel_id=1, source_target_pairs={{0,480},{32,0},{64,32},{96,64},{128,96},{160,128},{192,160},{224,1... | collective-permute-start | bytes 196616 | tf_op jit(solution)/shard_map/ppermute | solution.py:119
  156.7 2.4 %collective-permute-start.2 = (bf16[128,256]{1,0:T(8,128)(2,1)S(1)}, bf16[128,256]{1,0:T(8,128)(2,1)S(1)}, u32[]{:S(2)}, u32[]{:S(2)}) collective-permute-start(bf16[128,256]{1,0:T(8,128)(2,1)S(1)} %convert_element_type.13), channel_id=1, source_target_pairs={{0,32},{32,64},{64,96},{96,128},{128,160},{160,192},{192,224},{224... | collective-permute-start | bytes 196616 | tf_op jit(solution)/shard_map/ppermute | solution.py:119
  159.1 0.0 collective-permute-done.1
  159.1 0.0 collective-permute-done
  159.2 0.8 collective-permute-done.3
  159.9 14.6 %collective-permute-done.2 = bf16[128,256]{1,0:T(8,128)(2,1)S(1)} collective-permute-done((bf16[128,256]{1,0:T(8,128)(2,1)S(1)}, bf16[128,256]{1,0:T(8,128)(2,1)S(1)}, u32[]{:S(2)}, u32[]{:S(2)}) %collective-permute-start.2) | collective-permute-done | bytes 65568 | tf_op jit(solution)/shard_map/ppermute | solution.py:119
  174.5 0.1 subtract_multiply_fusion
  174.6 0.7 slice_bitcast_fusion
  (1 shorter events, 0.0 us)
Async XLA Ops:
  7.2 1.6 copy-start.1
  8.8 1.6 copy-start.2
  10.3 0.8 copy-start.4
  12.6 2.0 %copy-start = (bf16[4,2,128,2048]{3,2,1,0:T(8,128)(2,1)}, bf16[4,2,128,2048]{3,2,1,0:T(8,128)(2,1)S(1)}, u32[]{:S(2)}) copy-start(bf16[4,2,128,2048]{3,2,1,0:T(8,128)(2,1)S(1)} %shard_map.68) | copy-start | bytes 12582916
  14.6 10.9 %copy-start.6 = (f32[1,256,64]{1,2,0:T(8,128)S(1)}, f32[1,256,64]{1,2,0:T(8,128)}, u32[]{:S(2)}) copy-start(f32[1,256,64]{1,2,0:T(8,128)} %param.8) | copy-start | bytes 196612
  14.6 10.9 %copy-start.7 = (f32[1,256,64]{1,2,0:T(8,128)S(1)}, f32[1,256,64]{1,2,0:T(8,128)}, u32[]{:S(2)}) copy-start(f32[1,256,64]{1,2,0:T(8,128)} %param.7) | copy-start | bytes 196612
  14.6 80.4 %all-to-all-start = ((bf16[4,2,128,2048]{3,2,1,0:T(8,128)(2,1)}), bf16[4,2,128,2048]{3,2,1,0:T(8,128)(2,1)}, u32[]{:S(2)}, u32[]{:S(2)}) async-start(bf16[4,2,128,2048]{3,2,1,0:T(8,128)(2,1)} %copy-done), calls=%async_computation | async-start | bytes 8388608 | tf_op jit(solution)/shard_map/all_to_all | solution.py:128
  25.4 69.5 %all-gather.3.cloned.1.call-start = ((), (), s32[]{:S(2)}) async-start(), calls=%async_computation.3 | async-start | bytes 1179648 | tf_op jit(solution)/shard_map/all_gather | solution.py:124
  94.9 1.2 copy-start.3
  100.3 24.1 %copy-start.5 = (f32[128,256]{1,0:T(8,128)S(1)}, f32[128,256]{1,0:T(8,128)}, u32[]{:S(2)}) copy-start(f32[128,256]{1,0:T(8,128)} %pad_maximum_fusion) | copy-start | bytes 393220
  120.9 33.8 %all-to-all-start.2 = ((bf16[8,128,256]{2,1,0:T(8,128)(2,1)}), bf16[8,128,256]{2,1,0:T(8,128)(2,1)S(1)}, u32[]{:S(2)}, u32[]{:S(2)}) async-start(bf16[8,128,256]{2,1,0:T(8,128)(2,1)} %shard_map.70), calls=%async_computation.2 | async-start | bytes 1048576 | tf_op jit(solution)/shard_map/all_to_all | solution.py:132
  124.4 34.8 %collective-permute-start.1 = (f32[128,256]{1,0:T(8,128)S(1)}, f32[128,256]{1,0:T(8,128)S(1)}, u32[]{:S(2)}, u32[]{:S(2)}) collective-permute-start(f32[128,256]{1,0:T(8,128)S(1)} %copy-done.5), channel_id=1, source_target_pairs={{0,480},{32,0},{64,32},{96,64},{128,96},{160,128},{192,160},{224,1... | collective-permute-start | bytes 393224 | tf_op jit(solution)/shard_map/ppermute | solution.py:119
  128.4 30.7 %collective-permute-start = (f32[128,256]{1,0:T(8,128)S(1)}, f32[128,256]{1,0:T(8,128)S(1)}, u32[]{:S(2)}, u32[]{:S(2)}) collective-permute-start(f32[128,256]{1,0:T(8,128)S(1)} %copy-done.5), channel_id=1, source_target_pairs={{0,32},{32,64},{64,96},{96,128},{128,160},{160,192},{192,224},{224... | collective-permute-start | bytes 393224 | tf_op jit(solution)/shard_map/ppermute | solution.py:119
  154.8 5.1 %collective-permute-start.3 = (bf16[128,256]{1,0:T(8,128)(2,1)S(1)}, bf16[128,256]{1,0:T(8,128)(2,1)S(1)}, u32[]{:S(2)}, u32[]{:S(2)}) collective-permute-start(bf16[128,256]{1,0:T(8,128)(2,1)S(1)} %convert_element_type.13), channel_id=1, source_target_pairs={{0,480},{32,0},{64,32},{96,64},{128,96},{160,128},{192,160},{224,1... | collective-permute-start | bytes 196616 | tf_op jit(solution)/shard_map/ppermute | solution.py:119
  156.7 17.8 %collective-permute-start.2 = (bf16[128,256]{1,0:T(8,128)(2,1)S(1)}, bf16[128,256]{1,0:T(8,128)(2,1)S(1)}, u32[]{:S(2)}, u32[]{:S(2)}) collective-permute-start(bf16[128,256]{1,0:T(8,128)(2,1)S(1)} %convert_element_type.13), channel_id=1, source_target_pairs={{0,32},{32,64},{64,96},{96,128},{128,160},{160,192},{192,224},{224... | collective-permute-start | bytes 196616 | tf_op jit(solution)/shard_map/ppermute | solution.py:119
Sparse Core Ops, SparseCore 0:
  28.3 66.5 all-gather.2

commit v2 on v1

v2 whole, which is shorter than its diff:
```python
import functools

import jax
import jax.numpy as jnp
from jax import lax
from jax.experimental import pallas as pl
from jax.experimental.pallas import tpu as pltpu
from jax.sharding import Mesh
from jax.sharding import PartitionSpec as P

D = 8192
R = 64
TOKENS = 4096
GROUPS = 16
NX = 4
NZ = 8
TOK = TOKENS // (NX * NZ)
OWN = D // (NX * NZ)
QUAD = NZ // 2
FEAT = D // NX

learning_rate = 4.0
epsilon = 1e-05

inv_width = D ** (-0.5)
inv_rank = R ** (-0.5)
step_size = learning_rate / TOKENS**0.5

LAST = (((1,), (1,)), ((), ()))
VMEM_LIMIT = 40 * 1024 * 1024
DIRECT_LIMIT = 60 * 1024 * 1024


def norm_kernel(tok_ref, gain_ref, out_ref):
    wide = tok_ref[...].astype(jnp.float32)
    scale = lax.rsqrt(jnp.mean(wide * wide, axis=-1, keepdims=True) + epsilon)
    for x in range(NX):
        for z in range(NZ):
            src = slice((z * NX + x) * OWN, (z * NX + x + 1) * OWN)
            part = tok_ref[:, src].astype(jnp.float32) * scale * gain_ref[:, src]
            out_ref[x, :, z * OWN : (z + 1) * OWN] = part.astype(jnp.bfloat16)


def split_kernel(up_ref, out_ref):
    for x in range(NX):
        for z in range(NZ):
            src = slice((z * NX + x) * OWN, (z * NX + x + 1) * OWN)
            out_ref[x, :, z * OWN : (z + 1) * OWN] = up_ref[:, src]


def prep(kernel, array, *gain):
    rows = 32
    return pl.pallas_call(
        kernel,
        grid=(TOK // rows,),
        in_specs=[pl.BlockSpec((rows, D), lambda i: (i, 0))]
        + [pl.BlockSpec((1, D), lambda i: (0, 0)) for _ in gain],
        out_specs=pl.BlockSpec((NX, rows, FEAT), lambda i: (0, i, 0)),
        out_shape=jax.ShapeDtypeStruct((NX, TOK, FEAT), jnp.bfloat16),
        compiler_params=pltpu.CompilerParams(vmem_limit_bytes=DIRECT_LIMIT),
        cost_estimate=pl.CostEstimate(
            flops=4 * TOK * D, bytes_accessed=4 * TOK * D, transcendentals=0
        ),
    )(array, *gain)


def project_kernel(row, feat_ref, *refs):
    low_refs, out_ref, low_ref = refs[:QUAD], refs[QUAD], refs[QUAD + 1]
    me = lax.axis_index("z")

    @pl.when(pl.program_id(0) == 0)
    def _():
        for near in range(QUAD):
            for far in range(2):
                at = pl.multiple_of((me ^ (near + QUAD * far)) * OWN, OWN)
                low_ref[:, pl.ds(at, OWN)] = low_refs[near][far, row : row + R]

    for s in range(2):
        part = lax.dot_general(low_ref[...], feat_ref[s], LAST, preferred_element_type=jnp.float32)
        for x in range(out_ref.shape[0]):
            out_ref[x, s] = part


def project(feat, lows, row, copies):
    return pl.pallas_call(
        functools.partial(project_kernel, row),
        grid=(NX // 2,),
        in_specs=[pl.BlockSpec((2, TOK, FEAT), lambda i: (i, 0, 0))]
        + [pl.BlockSpec((2, 2 * R, OWN), lambda i: (0, 0, 0)) for _ in lows],
        out_specs=pl.BlockSpec((copies, 2, R, TOK), lambda i: (0, i, 0, 0)),
        out_shape=jax.ShapeDtypeStruct((copies, NX, R, TOK), jnp.float32),
        scratch_shapes=[pltpu.VMEM((R, FEAT), jnp.bfloat16)],
        compiler_params=pltpu.CompilerParams(vmem_limit_bytes=VMEM_LIMIT),
        cost_estimate=pl.CostEstimate(
            flops=2 * NX * TOK * FEAT * R, bytes_accessed=3 * 1024 * 1024, transcendentals=0
        ),
    )(feat, *lows)


def grads_kernel(relative, scale_part, scale_grad, feat_ref, *refs):
    part_refs, out_ref, low_ref = refs[:-2], refs[-2], refs[-1]
    step = pl.program_id(0)

    @pl.when(step == 0)
    def _():
        for s in range(NX):
            terms = [ref[x, s] for ref in part_refs for x in range(ref.shape[0])]
            total = sum(terms[1:], terms[0])
            low_ref[:, s * TOK : (s + 1) * TOK] = (total * scale_part).astype(jnp.bfloat16)

    grad = jnp.dot(
        low_ref[...],
        feat_ref[...].reshape(NX * TOK, 2 * OWN),
        preferred_element_type=jnp.float32,
    )
    grad = (grad * scale_grad).astype(jnp.bfloat16)
    me = lax.axis_index("z") if relative else 0
    for half in range(2):
        out_ref[me ^ (2 * step + half)] = grad[:, half * OWN : (half + 1) * OWN]


def grads(parts, feat, scale_part, scale_grad, relative):
    return pl.pallas_call(
        functools.partial(grads_kernel, relative, scale_part, scale_grad),
        grid=(NZ // 2,),
        in_specs=[pl.BlockSpec((NX, TOK, 2 * OWN), lambda i: (0, 0, i))]
        + [pl.BlockSpec(part.shape, lambda i: (0, 0, 0, 0)) for part in parts],
        out_specs=pl.BlockSpec((NZ, R, OWN), lambda i: (0, 0, 0)),
        out_shape=jax.ShapeDtypeStruct((NZ, R, OWN), jnp.bfloat16),
        scratch_shapes=[pltpu.VMEM((R, NX * TOK), jnp.bfloat16)],
        compiler_params=pltpu.CompilerParams(vmem_limit_bytes=VMEM_LIMIT),
        cost_estimate=pl.CostEstimate(
            flops=2 * NX * TOK * FEAT * R, bytes_accessed=3 * 1024 * 1024, transcendentals=0
        ),
    )(feat, *parts)


def shifted(array, axis, by):
    count = lax.axis_size(axis)
    return lax.ppermute(array, axis, [(i, (i + by) % count) for i in range(count)])


def swapped(array, by):
    return lax.ppermute(array, "z", [(i, i ^ by) for i in range(NZ)])


def exchange(array, axis):
    return lax.all_to_all(array, axis, 0, 0, tiled=True)


def mix(base, grad):
    sent = grad.astype(jnp.bfloat16)
    lower, upper = shifted(sent, "blk", 1), shifted(sent, "blk", -1)
    around = lower.astype(jnp.float32) + grad + upper.astype(jnp.float32)
    return ((base - step_size * around) / 3.0).T[None]


def local(tokens, norm_gain, adapt_in, adapt_out, upstream):
    wide = jnp.float32
    cotangent = prep(split_kernel, upstream[0])
    cotangent, adapt_in, adapt_out = lax.optimization_barrier((cotangent, adapt_in, adapt_out))
    cotangent = exchange(cotangent, "x")

    master = jnp.concatenate([adapt_in[0].T, adapt_out[0].T], axis=0)
    own = master.astype(jnp.bfloat16)
    pair = jnp.stack([own, swapped(own, QUAD)])
    lows = [pair] + [swapped(pair, k) for k in range(1, QUAD)]

    normed = prep(norm_kernel, tokens[0], norm_gain[None])
    cotangent, normed, lows = lax.optimization_barrier((cotangent, normed, lows))
    normed = exchange(normed, "x")
    base = shifted(master, "blk", 1) + master + shifted(master, "blk", -1)

    mine = project(cotangent, lows, R, 1)
    pulled = [mine, shifted(mine, "x", 1), shifted(mine, "x", -1), shifted(mine, "x", 2)]
    normed, base, pulled = lax.optimization_barrier((normed, base, pulled))

    factor = exchange(project(normed, lows, 0, NX), "x")
    near = grads(pulled, normed, inv_rank, inv_width, True)
    near = near.reshape(2, QUAD, R, OWN)
    quad = near[:, 0].astype(wide)
    for k in range(1, QUAD):
        quad = quad + swapped(near[:, k], k).astype(wide)
    grad_in = quad[0] + swapped(quad[1], QUAD)

    pieces = exchange(grads([factor], cotangent, inv_width, inv_rank, False), "z")
    grad_out = jnp.sum(pieces.astype(wide), axis=0)
    return (mix(base[:R], grad_in), mix(base[R:], grad_out))


def solution(mesh):
    mesh = Mesh(mesh.devices.reshape(GROUPS, NZ, NX), ("blk", "z", "x"))
    split = P("blk", ("z", "x"), None)
    in_specs = (split, P(), split, split, split)
    return jax.shard_map(
        local, mesh=mesh, in_specs=in_specs, out_specs=(split, split), check_vma=False
    )
```

time: 183 us -> 176 us (0.962)
  the two profiles are of different devices: /device:TPU:2 before, /device:TPU:96 now
where the time goes in v2:
time: 176 us; the launch traced here: 175 us
  starting transfers between devices  120 us (68%)
  waiting for transfers between devices  36.5 us (21%)
  Pallas kernels  16.7 us (9%)
    ppermute x9, starting transfers between devices, shifted(): lax.ppermute(array, axis, [(i, (i + by) % count) for i in range(count)])  57.3 us
    ppermute x8, starting transfers between devices, swapped(): return lax.ppermute(array, 'z', [(i, i ^ by) for i in range(NZ)])  36.9 us
    all_to_all x4, starting transfers between devices, exchange(): return lax.all_to_all(array, axis, 0, 0, tiled=True)  25.7 us
    ppermute x9, waiting for transfers between devices, shifted(): lax.ppermute(array, axis, [(i, (i + by) % count) for i in range(count)])  18.8 us
    ppermute x8, waiting for transfers between devices, swapped(): return lax.ppermute(array, 'z', [(i, i ^ by) for i in range(NZ)])  12.5 us
    pallas_call x2, Pallas kernels, prep(): pl.pallas_call(kernel, grid=(TOK // rows,), in_specs=[pl.BlockSpec((rows,...  8.09 us
    all_to_all x4, waiting for transfers between devices, exchange(): return lax.all_to_all(array, axis, 0, 0, tiled=True)  5.22 us
    pallas_call x2, Pallas kernels, grads(): pl.pallas_call(functools.partial(grads_kernel, relative, scale_part, scal...  4.58 us
  transfers between devices with their start and end apart: 21, of which 10 were waited for; matrix products, arithmetic and copies ran while one was open for 0% of the time, Pallas kernels for 5%

profile of v2, /device:TPU:96, one launch (start us, length us, event | category | flops | bytes accessed | tf_op | source)
XLA Modules:
  0.0 174.8 jit_solution(15049828610382470086)
XLA Ops:
  0.6 3.8 %shard_map.68 = bf16[4,128,2048]{2,1,0:T(8,128)(2,1)} custom-call(bf16[128,8192]{1,0:T(8,128)(2,1)} %bitcast.56), custom_call_target="tpu_custom_call" | custom-call | flops 4194304 | bytes 4194304 | tf_op jit(solution)/shard_map/pallas_call | solution.py:53
  4.4 0.0 copy-start
  4.4 0.0 copy-start.1
  4.4 4.4 %all-to-all-start = ((bf16[4,128,2048]{2,1,0:T(8,128)(2,1)}), bf16[4,128,2048]{2,1,0:T(8,128)(2,1)S(1)}, u32[]{:S(2)}, u32[]{:S(2)}) async-start(bf16[4,128,2048]{2,1,0:T(8,128)(2,1)} %shard_map.68), calls=%async_computation | async-start | bytes 4194304 | tf_op jit(solution)/shard_map/all_to_all | solution.py:148
  8.9 0.0 copy-done
  8.9 0.0 copy-done.1
  8.9 9.1 %collective-permute-start = (bf16[128,256]{1,0:T(8,128)(2,1)S(1)}, bf16[128,256]{1,0:T(8,128)(2,1)S(1)}, u32[]{:S(2)}, u32[]{:S(2)}) collective-permute-start(bf16[128,256]{1,0:T(8,128)(2,1)S(1)} %fusion.4), channel_id=1, source_target_pairs={{0,16},{4,20},{8,24},{12,28},{16,0},{20,4},{24,8},{28,12},{1,17},{... | collective-permute-start | bytes 196616 | tf_op jit(solution)/shard_map/ppermute | solution.py:144
  18.0 3.9 %collective-permute-done = bf16[128,256]{1,0:T(8,128)(2,1)S(1)} collective-permute-done((bf16[128,256]{1,0:T(8,128)(2,1)S(1)}, bf16[128,256]{1,0:T(8,128)(2,1)S(1)}, u32[]{:S(2)}, u32[]{:S(2)}) %collective-permute-start) | collective-permute-done | bytes 65568 | tf_op jit(solution)/shard_map/ppermute | solution.py:144
  21.9 1.9 %collective-permute-start.1 = (bf16[2,128,256]{2,1,0:T(8,128)(2,1)S(1)}, bf16[2,128,256]{2,1,0:T(8,128)(2,1)S(1)}, u32[]{:S(2)}, u32[]{:S(2)}) collective-permute-start(bf16[2,128,256]{2,1,0:T(8,128)(2,1)S(1)} %pad_maximum_fusion.1.refs_0_), channel_id=1, source_target_pairs={{0,4},{4,0},{8,12},{12,8},{16,20},{20,16},{24,28},{28,24},{1,5},{5... | collective-permute-start | bytes 393224 | tf_op jit(solution)/shard_map/ppermute | solution.py:144
  23.8 5.0 %collective-permute-start.2 = (bf16[2,128,256]{2,1,0:T(8,128)(2,1)S(1)}, bf16[2,128,256]{2,1,0:T(8,128)(2,1)S(1)}, u32[]{:S(2)}, u32[]{:S(2)}) collective-permute-start(bf16[2,128,256]{2,1,0:T(8,128)(2,1)S(1)} %pad_maximum_fusion.1.refs_0_), channel_id=1, source_target_pairs={{0,8},{4,12},{8,0},{12,4},{16,24},{20,28},{24,16},{28,20},{1,9},{5... | collective-permute-start | bytes 393224 | tf_op jit(solution)/shard_map/ppermute | solution.py:144
  28.8 3.2 %collective-permute-start.3 = (bf16[2,128,256]{2,1,0:T(8,128)(2,1)S(1)}, bf16[2,128,256]{2,1,0:T(8,128)(2,1)S(1)}, u32[]{:S(2)}, u32[]{:S(2)}) collective-permute-start(bf16[2,128,256]{2,1,0:T(8,128)(2,1)S(1)} %pad_maximum_fusion.1.refs_0_), channel_id=1, source_target_pairs={{0,12},{4,8},{8,4},{12,0},{16,28},{20,24},{24,20},{28,16},{1,13},{... | collective-permute-start | bytes 393224 | tf_op jit(solution)/shard_map/ppermute | solution.py:144
  32.0 4.3 %shard_map.69 = bf16[4,128,2048]{2,1,0:T(8,128)(2,1)} custom-call(bf16[128,8192]{1,0:T(8,128)(2,1)} %bitcast.57, f32[1,8192]{1,0:T(1,128)} %bitcast.65), custom_call_target="tpu_custom_call" | custom-call | flops 4194304 | bytes 4194304 | tf_op jit(solution)/shard_map/pallas_call | solution.py:53
  36.3 0.0 collective-permute-done.1.refs_1_
  36.3 2.5 %collective-permute-done.2.refs_2_ = bf16[2,128,256]{2,1,0:T(8,128)(2,1)S(1)} collective-permute-done((bf16[2,128,256]{2,1,0:T(8,128)(2,1)S(1)}, bf16[2,128,256]{2,1,0:T(8,128)(2,1)S(1)}, u32[]{:S(2)}, u32[]{:S(2)}) %collective-permute-start.2) | collective-permute-done | bytes 131104 | tf_op jit(solution)/shard_map/ppermute | solution.py:144
  38.8 0.0 collective-permute-done.3.refs_3_
  38.8 0.0 all-to-all-done.feat_ref
  38.8 4.6 %all-to-all-start.1 = ((bf16[4,128,2048]{2,1,0:T(8,128)(2,1)}), bf16[4,128,2048]{2,1,0:T(8,128)(2,1)}, u32[]{:S(2)}, u32[]{:S(2)}) async-start(bf16[4,128,2048]{2,1,0:T(8,128)(2,1)} %shard_map.69), calls=%async_computation.1 | async-start | bytes 4194304 | tf_op jit(solution)/shard_map/all_to_all | solution.py:148
  43.4 11.5 %collective-permute-start.5 = (f32[128,256]{1,0:T(8,128)S(1)}, f32[128,256]{1,0:T(8,128)S(1)}, u32[]{:S(2)}, u32[]{:S(2)}) collective-permute-start(f32[128,256]{1,0:T(8,128)S(1)} %pad_maximum_fusion), channel_id=1, source_target_pairs={{0,480},{32,0},{64,32},{96,64},{128,96},{160,128},{192,160},{224,1... | collective-permute-start | bytes 393224 | tf_op jit(solution)/shard_map/ppermute | solution.py:140
  54.9 1.9 %collective-permute-start.4 = (f32[128,256]{1,0:T(8,128)S(1)}, f32[128,256]{1,0:T(8,128)S(1)}, u32[]{:S(2)}, u32[]{:S(2)}) collective-permute-start(f32[128,256]{1,0:T(8,128)S(1)} %pad_maximum_fusion), channel_id=1, source_target_pairs={{0,32},{32,64},{64,96},{96,128},{128,160},{160,192},{192,224},{224... | collective-permute-start | bytes 393224 | tf_op jit(solution)/shard_map/ppermute | solution.py:140
  56.8 1.0 shard_map.70.refs_0_
  57.9 3.6 %collective-permute-start.6 = (f32[1,4,64,128]{3,2,1,0:T(8,128)S(1)}, f32[1,4,64,128]{3,2,1,0:T(8,128)S(1)}, u32[]{:S(2)}, u32[]{:S(2)}) collective-permute-start(f32[1,4,64,128]{3,2,1,0:T(8,128)S(1)} %shard_map.70.refs_0_), channel_id=1, source_target_pairs={{0,1},{1,2},{2,3},{3,0},{4,5},{5,6},{6,7},{7,4},{8,9},{9,10},{10,1... | collective-permute-start | bytes 393224 | tf_op jit(solution)/shard_map/ppermute | solution.py:140
  61.5 3.4 %collective-permute-start.7 = (f32[1,4,64,128]{3,2,1,0:T(8,128)S(1)}, f32[1,4,64,128]{3,2,1,0:T(8,128)S(1)}, u32[]{:S(2)}, u32[]{:S(2)}) collective-permute-start(f32[1,4,64,128]{3,2,1,0:T(8,128)S(1)} %shard_map.70.refs_0_), channel_id=1, source_target_pairs={{0,3},{1,0},{2,1},{3,2},{4,7},{5,4},{6,5},{7,6},{8,11},{9,8},{10,9... | collective-permute-start | bytes 393224 | tf_op jit(solution)/shard_map/ppermute | solution.py:140
  64.9 3.9 %collective-permute-start.8 = (f32[1,4,64,128]{3,2,1,0:T(8,128)S(1)}, f32[1,4,64,128]{3,2,1,0:T(8,128)S(1)}, u32[]{:S(2)}, u32[]{:S(2)}) collective-permute-start(f32[1,4,64,128]{3,2,1,0:T(8,128)S(1)} %shard_map.70.refs_0_), channel_id=1, source_target_pairs={{0,2},{1,3},{2,0},{3,1},{4,6},{5,7},{6,4},{7,5},{8,10},{9,11},{10,... | collective-permute-start | bytes 393224 | tf_op jit(solution)/shard_map/ppermute | solution.py:140
  68.9 0.0 collective-permute-done.5
  68.9 3.1 %collective-permute-done.4 = f32[128,256]{1,0:T(8,128)S(1)} collective-permute-done((f32[128,256]{1,0:T(8,128)S(1)}, f32[128,256]{1,0:T(8,128)S(1)}, u32[]{:S(2)}, u32[]{:S(2)}) %collective-permute-start.4) | collective-permute-done | bytes 131104 | tf_op jit(solution)/shard_map/ppermute | solution.py:140
  72.0 0.0 collective-permute-done.6.refs_1_
  72.0 0.0 collective-permute-done.7.refs_2_
  72.1 1.2 collective-permute-done.8.refs_3_
  73.3 0.0 all-to-all-done.1.feat_ref
  73.3 3.0 %shard_map.72 = f32[4,4,64,128]{3,2,1,0:T(8,128)} custom-call(bf16[4,128,2048]{2,1,0:T(8,128)(2,1)} %all-to-all-done.1.feat_ref, bf16[2,128,256]{2,1,0:T(8,128)(2,1)S(1)} %pad_maximum_fusion.1.refs_0_, bf16[2,128,256]{2,1,0:T(8,128)(2,1)S(1)} %collective-permute-done.1.refs_1_, bf16[2,128,256]{2,1,0:T(8,128)(2,1)S(1)} %collective-permute-done.2.refs_2_, ...), custom_call_target="tpu_custom_call" | custom-call | flops 134217728 | bytes 3145728 | tf_op jit(solution)/shard_map/pallas_call | solution.py:85
  76.3 3.5 %all-to-all-start.2 = ((f32[4,4,64,128]{3,2,1,0:T(8,128)}), f32[4,4,64,128]{3,2,1,0:T(8,128)S(1)}, u32[]{:S(2)}, u32[]{:S(2)}) async-start(f32[4,4,64,128]{3,2,1,0:T(8,128)} %shard_map.72), calls=%async_computation.2 | async-start | bytes 1048576 | tf_op jit(solution)/shard_map/all_to_all | solution.py:148
  79.8 2.8 %shard_map.71 = bf16[8,64,256]{2,1,0:T(8,128)(2,1)S(1)} custom-call(bf16[4,128,2048]{2,1,0:T(8,128)(2,1)} %all-to-all-done.1.feat_ref, f32[1,4,64,128]{3,2,1,0:T(8,128)S(1)} %shard_map.70.refs_0_, f32[1,4,64,128]{3,2,1,0:T(8,128)S(1)} %collective-permute-done.6.refs_1_, f32[1,4,64,128]{3,2,1,0:T(8,128)S(1)} %collective-permute-done.7.refs_2_, ...), custom_call_target="tpu_custom_call" | custom-call | flops 134217728 | bytes 3145728 | tf_op jit(solution)/shard_map/pallas_call | solution.py:123
  82.6 5.2 %all-to-all-done.2.refs_0_ = f32[4,4,64,128]{3,2,1,0:T(8,128)S(1)} async-done(((f32[4,4,64,128]{3,2,1,0:T(8,128)}), f32[4,4,64,128]{3,2,1,0:T(8,128)S(1)}, u32[]{:S(2)}, u32[]{:S(2)}) %all-to-all-start.2) | async-done | bytes 524320 | tf_op jit(solution)/shard_map/all_to_all | solution.py:148
  87.8 1.8 %shard_map.73 = bf16[8,64,256]{2,1,0:T(8,128)(2,1)} custom-call(bf16[4,128,2048]{2,1,0:T(8,128)(2,1)S(1)} %all-to-all-done.feat_ref, f32[4,4,64,128]{3,2,1,0:T(8,128)S(1)} %all-to-all-done.2.refs_0_), custom_call_target="tpu_custom_call" | custom-call | flops 134217728 | bytes 3145728 | tf_op jit(solution)/shard_map/pallas_call | solution.py:123
  89.6 13.2 %all-to-all-start.3 = ((bf16[8,64,256]{2,1,0:T(8,128)(2,1)}), bf16[8,64,256]{2,1,0:T(8,128)(2,1)S(1)}, u32[]{:S(2)}, u32[]{:S(2)}) async-start(bf16[8,64,256]{2,1,0:T(8,128)(2,1)} %shard_map.73), calls=%async_computation.3 | async-start | bytes 524288 | tf_op jit(solution)/shard_map/all_to_all | solution.py:148
  102.8 1.9 %collective-permute-start.11 = (bf16[2,64,256]{2,1,0:T(8,128)(2,1)S(1)}, bf16[2,64,256]{2,1,0:T(8,128)(2,1)S(1)}, u32[]{:S(2)}, u32[]{:S(2)}) collective-permute-start(bf16[2,64,256]{2,1,0:T(8,128)(2,1)S(1)} %get-tuple-element.34), channel_id=1, source_target_pairs={{0,12},{4,8},{8,4},{12,0},{16,28},{20,24},{24,20},{28,16},{1,13},{... | collective-permute-start | bytes 196616 | tf_op jit(solution)/shard_map/ppermute | solution.py:144
  104.7 3.9 %collective-permute-start.10 = (bf16[2,64,256]{2,1,0:T(8,128)(2,1)S(1)}, bf16[2,64,256]{2,1,0:T(8,128)(2,1)S(1)}, u32[]{:S(2)}, u32[]{:S(2)}) collective-permute-start(bf16[2,64,256]{2,1,0:T(8,128)(2,1)S(1)} %get-tuple-element.33), channel_id=1, source_target_pairs={{0,8},{4,12},{8,0},{12,4},{16,24},{20,28},{24,16},{28,20},{1,9},{5... | collective-permute-start | bytes 196616 | tf_op jit(solution)/shard_map/ppermute | solution.py:144
  108.7 4.3 %collective-permute-start.9 = (bf16[2,64,256]{2,1,0:T(8,128)(2,1)S(1)}, bf16[2,64,256]{2,1,0:T(8,128)(2,1)S(1)}, u32[]{:S(2)}, u32[]{:S(2)}) collective-permute-start(bf16[2,64,256]{2,1,0:T(8,128)(2,1)S(1)} %get-tuple-element.32), channel_id=1, source_target_pairs={{0,4},{4,0},{8,12},{12,8},{16,20},{20,16},{24,28},{28,24},{1,5},{5... | collective-permute-start | bytes 196616 | tf_op jit(solution)/shard_map/ppermute | solution.py:144
  112.9 0.2 collective-permute-done.11
  113.2 1.3 collective-permute-done.10
  114.5 0.7 collective-permute-done.9
  115.3 7.6 %collective-permute-start.12 = (f32[64,256]{1,0:T(8,128)S(1)}, f32[64,256]{1,0:T(8,128)S(1)}, u32[]{:S(2)}, u32[]{:S(2)}) collective-permute-start(f32[64,256]{1,0:T(8,128)S(1)} %slice_bitcast_fusion), channel_id=1, source_target_pairs={{0,16},{4,20},{8,24},{12,28},{16,0},{20,4},{24,8},{28,12},{1,17},{... | collective-permute-start | bytes 196616 | tf_op jit(solution)/shard_map/ppermute | solution.py:144
  122.8 3.9 %collective-permute-done.12 = f32[64,256]{1,0:T(8,128)S(1)} collective-permute-done((f32[64,256]{1,0:T(8,128)S(1)}, f32[64,256]{1,0:T(8,128)S(1)}, u32[]{:S(2)}, u32[]{:S(2)}) %collective-permute-start.12) | collective-permute-done | bytes 65568 | tf_op jit(solution)/shard_map/ppermute | solution.py:144
  126.7 14.6 %collective-permute-start.14 = (bf16[64,256]{1,0:T(8,128)(2,1)S(1)}, bf16[64,256]{1,0:T(8,128)(2,1)S(1)}, u32[]{:S(2)}, u32[]{:S(2)}) collective-permute-start(bf16[64,256]{1,0:T(8,128)(2,1)S(1)} %fusion.3), channel_id=1, source_target_pairs={{0,480},{32,0},{64,32},{96,64},{128,96},{160,128},{192,160},{224,1... | collective-permute-start | bytes 98312 | tf_op jit(solution)/shard_map/ppermute | solution.py:140
  141.3 1.9 %collective-permute-start.13 = (bf16[64,256]{1,0:T(8,128)(2,1)S(1)}, bf16[64,256]{1,0:T(8,128)(2,1)S(1)}, u32[]{:S(2)}, u32[]{:S(2)}) collective-permute-start(bf16[64,256]{1,0:T(8,128)(2,1)S(1)} %fusion.3), channel_id=1, source_target_pairs={{0,32},{32,64},{64,96},{96,128},{128,160},{160,192},{192,224},{224... | collective-permute-start | bytes 98312 | tf_op jit(solution)/shard_map/ppermute | solution.py:140
  143.2 0.0 all-to-all-done.3
  143.3 14.5 %collective-permute-start.16 = (bf16[64,256]{1,0:T(8,128)(2,1)S(1)}, bf16[64,256]{1,0:T(8,128)(2,1)S(1)}, u32[]{:S(2)}, u32[]{:S(2)}) collective-permute-start(bf16[64,256]{1,0:T(8,128)(2,1)S(1)} %convert_element_type.56), channel_id=1, source_target_pairs={{0,480},{32,0},{64,32},{96,64},{128,96},{160,128},{192,160},{224,1... | collective-permute-start | bytes 98312 | tf_op jit(solution)/shard_map/ppermute | solution.py:140
  157.8 1.9 %collective-permute-start.15 = (bf16[64,256]{1,0:T(8,128)(2,1)S(1)}, bf16[64,256]{1,0:T(8,128)(2,1)S(1)}, u32[]{:S(2)}, u32[]{:S(2)}) collective-permute-start(bf16[64,256]{1,0:T(8,128)(2,1)S(1)} %convert_element_type.56), channel_id=1, source_target_pairs={{0,32},{32,64},{64,96},{96,128},{128,160},{160,192},{192,224},{224... | collective-permute-start | bytes 98312 | tf_op jit(solution)/shard_map/ppermute | solution.py:140
  159.7 0.0 collective-permute-done.14
  159.7 0.0 collective-permute-done.13
  159.7 0.0 collective-permute-done.16
  159.8 14.4 %collective-permute-done.15 = bf16[64,256]{1,0:T(8,128)(2,1)S(1)} collective-permute-done((bf16[64,256]{1,0:T(8,128)(2,1)S(1)}, bf16[64,256]{1,0:T(8,128)(2,1)S(1)}, u32[]{:S(2)}, u32[]{:S(2)}) %collective-permute-start.15) | collective-permute-done | bytes 32800 | tf_op jit(solution)/shard_map/ppermute | solution.py:140
  174.1 0.7 multiply_bitcast_fusion
  (11 shorter events, 0.2 us)
Async XLA Ops:
  4.4 4.4 %copy-start = (f32[1,256,64]{1,2,0:T(8,128)S(1)}, f32[1,256,64]{1,2,0:T(8,128)}, u32[]{:S(2)}) copy-start(f32[1,256,64]{1,2,0:T(8,128)} %param.8) | copy-start | bytes 196612
  4.4 4.4 %copy-start.1 = (f32[1,256,64]{1,2,0:T(8,128)S(1)}, f32[1,256,64]{1,2,0:T(8,128)}, u32[]{:S(2)}) copy-start(f32[1,256,64]{1,2,0:T(8,128)} %param.7) | copy-start | bytes 196612
  4.4 34.3 %all-to-all-start = ((bf16[4,128,2048]{2,1,0:T(8,128)(2,1)}), bf16[4,128,2048]{2,1,0:T(8,128)(2,1)S(1)}, u32[]{:S(2)}, u32[]{:S(2)}) async-start(bf16[4,128,2048]{2,1,0:T(8,128)(2,1)} %shard_map.68), calls=%async_computation | async-start | bytes 4194304 | tf_op jit(solution)/shard_map/all_to_all | solution.py:148
  8.9 13.0 %collective-permute-start = (bf16[128,256]{1,0:T(8,128)(2,1)S(1)}, bf16[128,256]{1,0:T(8,128)(2,1)S(1)}, u32[]{:S(2)}, u32[]{:S(2)}) collective-permute-start(bf16[128,256]{1,0:T(8,128)(2,1)S(1)} %fusion.4), channel_id=1, source_target_pairs={{0,16},{4,20},{8,24},{12,28},{16,0},{20,4},{24,8},{28,12},{1,17},{... | collective-permute-start | bytes 196616 | tf_op jit(solution)/shard_map/ppermute | solution.py:144
  21.9 14.4 %collective-permute-start.1 = (bf16[2,128,256]{2,1,0:T(8,128)(2,1)S(1)}, bf16[2,128,256]{2,1,0:T(8,128)(2,1)S(1)}, u32[]{:S(2)}, u32[]{:S(2)}) collective-permute-start(bf16[2,128,256]{2,1,0:T(8,128)(2,1)S(1)} %pad_maximum_fusion.1.refs_0_), channel_id=1, source_target_pairs={{0,4},{4,0},{8,12},{12,8},{16,20},{20,16},{24,28},{28,24},{1,5},{5... | collective-permute-start | bytes 393224 | tf_op jit(solution)/shard_map/ppermute | solution.py:144
  23.8 14.9 %collective-permute-start.2 = (bf16[2,128,256]{2,1,0:T(8,128)(2,1)S(1)}, bf16[2,128,256]{2,1,0:T(8,128)(2,1)S(1)}, u32[]{:S(2)}, u32[]{:S(2)}) collective-permute-start(bf16[2,128,256]{2,1,0:T(8,128)(2,1)S(1)} %pad_maximum_fusion.1.refs_0_), channel_id=1, source_target_pairs={{0,8},{4,12},{8,0},{12,4},{16,24},{20,28},{24,16},{28,20},{1,9},{5... | collective-permute-start | bytes 393224 | tf_op jit(solution)/shard_map/ppermute | solution.py:144
  28.8 10.0 %collective-permute-start.3 = (bf16[2,128,256]{2,1,0:T(8,128)(2,1)S(1)}, bf16[2,128,256]{2,1,0:T(8,128)(2,1)S(1)}, u32[]{:S(2)}, u32[]{:S(2)}) collective-permute-start(bf16[2,128,256]{2,1,0:T(8,128)(2,1)S(1)} %pad_maximum_fusion.1.refs_0_), channel_id=1, source_target_pairs={{0,12},{4,8},{8,4},{12,0},{16,28},{20,24},{24,20},{28,16},{1,13},{... | collective-permute-start | bytes 393224 | tf_op jit(solution)/shard_map/ppermute | solution.py:144
  38.8 34.5 %all-to-all-start.1 = ((bf16[4,128,2048]{2,1,0:T(8,128)(2,1)}), bf16[4,128,2048]{2,1,0:T(8,128)(2,1)}, u32[]{:S(2)}, u32[]{:S(2)}) async-start(bf16[4,128,2048]{2,1,0:T(8,128)(2,1)} %shard_map.69), calls=%async_computation.1 | async-start | bytes 4194304 | tf_op jit(solution)/shard_map/all_to_all | solution.py:148
  43.4 25.5 %collective-permute-start.5 = (f32[128,256]{1,0:T(8,128)S(1)}, f32[128,256]{1,0:T(8,128)S(1)}, u32[]{:S(2)}, u32[]{:S(2)}) collective-permute-start(f32[128,256]{1,0:T(8,128)S(1)} %pad_maximum_fusion), channel_id=1, source_target_pairs={{0,480},{32,0},{64,32},{96,64},{128,96},{160,128},{192,160},{224,1... | collective-permute-start | bytes 393224 | tf_op jit(solution)/shard_map/ppermute | solution.py:140
  54.9 17.1 %collective-permute-start.4 = (f32[128,256]{1,0:T(8,128)S(1)}, f32[128,256]{1,0:T(8,128)S(1)}, u32[]{:S(2)}, u32[]{:S(2)}) collective-permute-start(f32[128,256]{1,0:T(8,128)S(1)} %pad_maximum_fusion), channel_id=1, source_target_pairs={{0,32},{32,64},{64,96},{96,128},{128,160},{160,192},{192,224},{224... | collective-permute-start | bytes 393224 | tf_op jit(solution)/shard_map/ppermute | solution.py:140
  57.9 14.2 %collective-permute-start.6 = (f32[1,4,64,128]{3,2,1,0:T(8,128)S(1)}, f32[1,4,64,128]{3,2,1,0:T(8,128)S(1)}, u32[]{:S(2)}, u32[]{:S(2)}) collective-permute-start(f32[1,4,64,128]{3,2,1,0:T(8,128)S(1)} %shard_map.70.refs_0_), channel_id=1, source_target_pairs={{0,1},{1,2},{2,3},{3,0},{4,5},{5,6},{6,7},{7,4},{8,9},{9,10},{10,1... | collective-permute-start | bytes 393224 | tf_op jit(solution)/shard_map/ppermute | solution.py:140
  61.5 10.5 %collective-permute-start.7 = (f32[1,4,64,128]{3,2,1,0:T(8,128)S(1)}, f32[1,4,64,128]{3,2,1,0:T(8,128)S(1)}, u32[]{:S(2)}, u32[]{:S(2)}) collective-permute-start(f32[1,4,64,128]{3,2,1,0:T(8,128)S(1)} %shard_map.70.refs_0_), channel_id=1, source_target_pairs={{0,3},{1,0},{2,1},{3,2},{4,7},{5,4},{6,5},{7,6},{8,11},{9,8},{10,9... | collective-permute-start | bytes 393224 | tf_op jit(solution)/shard_map/ppermute | solution.py:140
  64.9 8.4 %collective-permute-start.8 = (f32[1,4,64,128]{3,2,1,0:T(8,128)S(1)}, f32[1,4,64,128]{3,2,1,0:T(8,128)S(1)}, u32[]{:S(2)}, u32[]{:S(2)}) collective-permute-start(f32[1,4,64,128]{3,2,1,0:T(8,128)S(1)} %shard_map.70.refs_0_), channel_id=1, source_target_pairs={{0,2},{1,3},{2,0},{3,1},{4,6},{5,7},{6,4},{7,5},{8,10},{9,11},{10,... | collective-permute-start | bytes 393224 | tf_op jit(solution)/shard_map/ppermute | solution.py:140
  76.3 11.5 %all-to-all-start.2 = ((f32[4,4,64,128]{3,2,1,0:T(8,128)}), f32[4,4,64,128]{3,2,1,0:T(8,128)S(1)}, u32[]{:S(2)}, u32[]{:S(2)}) async-start(f32[4,4,64,128]{3,2,1,0:T(8,128)} %shard_map.72), calls=%async_computation.2 | async-start | bytes 1048576 | tf_op jit(solution)/shard_map/all_to_all | solution.py:148
  89.6 53.7 %all-to-all-start.3 = ((bf16[8,64,256]{2,1,0:T(8,128)(2,1)}), bf16[8,64,256]{2,1,0:T(8,128)(2,1)S(1)}, u32[]{:S(2)}, u32[]{:S(2)}) async-start(bf16[8,64,256]{2,1,0:T(8,128)(2,1)} %shard_map.73), calls=%async_computation.3 | async-start | bytes 524288 | tf_op jit(solution)/shard_map/all_to_all | solution.py:148
  102.8 10.4 %collective-permute-start.11 = (bf16[2,64,256]{2,1,0:T(8,128)(2,1)S(1)}, bf16[2,64,256]{2,1,0:T(8,128)(2,1)S(1)}, u32[]{:S(2)}, u32[]{:S(2)}) collective-permute-start(bf16[2,64,256]{2,1,0:T(8,128)(2,1)S(1)} %get-tuple-element.34), channel_id=1, source_target_pairs={{0,12},{4,8},{8,4},{12,0},{16,28},{20,24},{24,20},{28,16},{1,13},{... | collective-permute-start | bytes 196616 | tf_op jit(solution)/shard_map/ppermute | solution.py:144
  104.7 9.8 %collective-permute-start.10 = (bf16[2,64,256]{2,1,0:T(8,128)(2,1)S(1)}, bf16[2,64,256]{2,1,0:T(8,128)(2,1)S(1)}, u32[]{:S(2)}, u32[]{:S(2)}) collective-permute-start(bf16[2,64,256]{2,1,0:T(8,128)(2,1)S(1)} %get-tuple-element.33), channel_id=1, source_target_pairs={{0,8},{4,12},{8,0},{12,4},{16,24},{20,28},{24,16},{28,20},{1,9},{5... | collective-permute-start | bytes 196616 | tf_op jit(solution)/shard_map/ppermute | solution.py:144
  108.7 6.5 %collective-permute-start.9 = (bf16[2,64,256]{2,1,0:T(8,128)(2,1)S(1)}, bf16[2,64,256]{2,1,0:T(8,128)(2,1)S(1)}, u32[]{:S(2)}, u32[]{:S(2)}) collective-permute-start(bf16[2,64,256]{2,1,0:T(8,128)(2,1)S(1)} %get-tuple-element.32), channel_id=1, source_target_pairs={{0,4},{4,0},{8,12},{12,8},{16,20},{20,16},{24,28},{28,24},{1,5},{5... | collective-permute-start | bytes 196616 | tf_op jit(solution)/shard_map/ppermute | solution.py:144
  115.3 11.5 %collective-permute-start.12 = (f32[64,256]{1,0:T(8,128)S(1)}, f32[64,256]{1,0:T(8,128)S(1)}, u32[]{:S(2)}, u32[]{:S(2)}) collective-permute-start(f32[64,256]{1,0:T(8,128)S(1)} %slice_bitcast_fusion), channel_id=1, source_target_pairs={{0,16},{4,20},{8,24},{12,28},{16,0},{20,4},{24,8},{28,12},{1,17},{... | collective-permute-start | bytes 196616 | tf_op jit(solution)/shard_map/ppermute | solution.py:144
  126.7 33.0 %collective-permute-start.14 = (bf16[64,256]{1,0:T(8,128)(2,1)S(1)}, bf16[64,256]{1,0:T(8,128)(2,1)S(1)}, u32[]{:S(2)}, u32[]{:S(2)}) collective-permute-start(bf16[64,256]{1,0:T(8,128)(2,1)S(1)} %fusion.3), channel_id=1, source_target_pairs={{0,480},{32,0},{64,32},{96,64},{128,96},{160,128},{192,160},{224,1... | collective-permute-start | bytes 98312 | tf_op jit(solution)/shard_map/ppermute | solution.py:140
  141.3 18.4 %collective-permute-start.13 = (bf16[64,256]{1,0:T(8,128)(2,1)S(1)}, bf16[64,256]{1,0:T(8,128)(2,1)S(1)}, u32[]{:S(2)}, u32[]{:S(2)}) collective-permute-start(bf16[64,256]{1,0:T(8,128)(2,1)S(1)} %fusion.3), channel_id=1, source_target_pairs={{0,32},{32,64},{64,96},{96,128},{128,160},{160,192},{192,224},{224... | collective-permute-start | bytes 98312 | tf_op jit(solution)/shard_map/ppermute | solution.py:140
  143.3 16.4 %collective-permute-start.16 = (bf16[64,256]{1,0:T(8,128)(2,1)S(1)}, bf16[64,256]{1,0:T(8,128)(2,1)S(1)}, u32[]{:S(2)}, u32[]{:S(2)}) collective-permute-start(bf16[64,256]{1,0:T(8,128)(2,1)S(1)} %convert_element_type.56), channel_id=1, source_target_pairs={{0,480},{32,0},{64,32},{96,64},{128,96},{160,128},{192,160},{224,1... | collective-permute-start | bytes 98312 | tf_op jit(solution)/shard_map/ppermute | solution.py:140
  157.8 16.4 %collective-permute-start.15 = (bf16[64,256]{1,0:T(8,128)(2,1)S(1)}, bf16[64,256]{1,0:T(8,128)(2,1)S(1)}, u32[]{:S(2)}, u32[]{:S(2)}) collective-permute-start(bf16[64,256]{1,0:T(8,128)(2,1)S(1)} %convert_element_type.56), channel_id=1, source_target_pairs={{0,32},{32,64},{64,96},{96,128},{128,160},{160,192},{192,224},{224... | collective-permute-start | bytes 98312 | tf_op jit(solution)/shard_map/ppermute | solution.py:140

commit v3 on v1

v3 whole, which is shorter than its diff:
```python
import jax
import jax.numpy as jnp
from jax import lax
from jax.experimental import pallas as pl
from jax.experimental.pallas import tpu as pltpu
from jax.sharding import Mesh
from jax.sharding import PartitionSpec as P

D = 8192
R = 64
TOKENS = 4096
GROUPS = 16
NX = 4
NZ = 8
TOK = TOKENS // (NX * NZ)
OWN = D // (NX * NZ)
QUAD = NZ // 2
FEAT = D // NX

learning_rate = 4.0
epsilon = 1e-05

inv_width = D ** (-0.5)
inv_rank = R ** (-0.5)
step_size = learning_rate / TOKENS**0.5

ROWS = 32
CHUNKS = TOK // ROWS

LAST = (((1,), (1,)), ((), ()))
VMEM_LIMIT = 40 * 1024 * 1024
DIRECT_LIMIT = 60 * 1024 * 1024


def prep_kernel(tok_ref, gain_ref, up_ref, out_ref, raw_ref, done_ref, in_sem, out_sem, up_sem):
    loads = []
    for c in range(CHUNKS):
        rows = pl.ds(c * ROWS, ROWS)
        loads.append(pltpu.make_async_copy(tok_ref.at[rows], raw_ref.at[c], in_sem.at[c]))
        loads[-1].start()
    moves = []
    for b in range(NX * NZ):
        z, x = divmod(b, NX)
        src = up_ref.at[:, pl.ds(b * OWN, OWN)]
        dst = out_ref.at[x, 1, :, pl.ds(z * OWN, OWN)]
        moves.append(pltpu.make_async_copy(src, dst, up_sem.at[b]))
        moves[-1].start()
    stores = []
    for c in range(CHUNKS):
        loads[c].wait()
        wide = raw_ref[c].astype(jnp.float32)
        scale = lax.rsqrt(jnp.mean(wide * wide, axis=-1, keepdims=True) + epsilon)
        for b in range(NX * NZ):
            z, x = divmod(b, NX)
            src = slice(b * OWN, (b + 1) * OWN)
            part = raw_ref[c, :, src].astype(jnp.float32) * scale * gain_ref[:, src]
            done_ref[c, x, :, z * OWN : (z + 1) * OWN] = part.astype(jnp.bfloat16)
        for x in range(NX):
            dst = out_ref.at[x, 0, pl.ds(c * ROWS, ROWS)]
            stores.append(pltpu.make_async_copy(done_ref.at[c, x], dst, out_sem.at[c, x]))
            stores[-1].start()
    for copy in moves + stores:
        copy.wait()


def prep(tokens, gain, upstream):
    return pl.pallas_call(
        prep_kernel,
        in_specs=[
            pl.BlockSpec(memory_space=pl.ANY),
            pl.BlockSpec(memory_space=pltpu.VMEM),
            pl.BlockSpec(memory_space=pl.ANY),
        ],
        out_specs=pl.BlockSpec(memory_space=pl.ANY),
        out_shape=jax.ShapeDtypeStruct((NX, 2, TOK, FEAT), jnp.bfloat16),
        scratch_shapes=[
            pltpu.VMEM((CHUNKS, ROWS, D), jnp.bfloat16),
            pltpu.VMEM((CHUNKS, NX, ROWS, FEAT), jnp.bfloat16),
            pltpu.SemaphoreType.DMA((CHUNKS,)),
            pltpu.SemaphoreType.DMA((CHUNKS, NX)),
            pltpu.SemaphoreType.DMA((NX * NZ,)),
        ],
        compiler_params=pltpu.CompilerParams(vmem_limit_bytes=DIRECT_LIMIT),
        cost_estimate=pl.CostEstimate(
            flops=6 * TOK * D, bytes_accessed=8 * TOK * D, transcendentals=0
        ),
    )(tokens, gain, upstream)


def project_kernel(feat_ref, *refs):
    low_refs, out_ref, low_ref = refs[:QUAD], refs[QUAD], refs[QUAD + 1]
    me = lax.axis_index("z")

    @pl.when(pl.program_id(0) == 0)
    def _():
        for near in range(QUAD):
            for far in range(2):
                at = pl.multiple_of((me ^ (near + QUAD * far)) * OWN, OWN)
                low_ref[:, pl.ds(at, OWN)] = low_refs[near][far]

    for s in range(2):
        for half in range(2):
            rows = slice(half * R, (half + 1) * R)
            part = lax.dot_general(
                low_ref[rows], feat_ref[s, half], LAST, preferred_element_type=jnp.float32
            )
            for x in range(NX):
                out_ref[x, s, rows] = part


def project(feat, lows):
    return pl.pallas_call(
        project_kernel,
        grid=(NX // 2,),
        in_specs=[pl.BlockSpec((2, 2, TOK, FEAT), lambda i: (i, 0, 0, 0))]
        + [pl.BlockSpec((2, 2 * R, OWN), lambda i: (0, 0, 0)) for _ in lows],
        out_specs=pl.BlockSpec((NX, 2, 2 * R, TOK), lambda i: (0, i, 0, 0)),
        out_shape=jax.ShapeDtypeStruct((NX, NX, 2 * R, TOK), jnp.float32),
        scratch_shapes=[pltpu.VMEM((2 * R, FEAT), jnp.bfloat16)],
        compiler_params=pltpu.CompilerParams(vmem_limit_bytes=VMEM_LIMIT),
        cost_estimate=pl.CostEstimate(
            flops=4 * NX * TOK * FEAT * R, bytes_accessed=6 * 1024 * 1024, transcendentals=0
        ),
    )(feat, *lows)


def grads_kernel(part_ref, feat_ref, out_ref, low_ref):
    step = pl.program_id(0)

    @pl.when(step == 0)
    def _():
        for s in range(NX):
            total = part_ref[0, s]
            for x in range(1, NX):
                total = total + part_ref[x, s]
            at = slice(s * TOK, (s + 1) * TOK)
            low_ref[0, :, at] = (total[R:] * inv_rank).astype(jnp.bfloat16)
            low_ref[1, :, at] = (total[:R] * inv_width).astype(jnp.bfloat16)

    me = lax.axis_index("z")
    for half, scale in enumerate((inv_width, inv_rank)):
        rows = slice(half * R, (half + 1) * R)
        grad = jnp.dot(
            low_ref[half],
            feat_ref[:, half].reshape(NX * TOK, 2 * OWN),
            preferred_element_type=jnp.float32,
        )
        grad = (grad * scale).astype(jnp.bfloat16)
        for block in range(2):
            out_ref[me ^ (2 * step + block), rows] = grad[:, block * OWN : (block + 1) * OWN]


def grads(part, feat):
    return pl.pallas_call(
        grads_kernel,
        grid=(NZ // 2,),
        in_specs=[
            pl.BlockSpec(part.shape, lambda i: (0, 0, 0, 0)),
            pl.BlockSpec((NX, 2, TOK, 2 * OWN), lambda i: (0, 0, 0, i)),
        ],
        out_specs=pl.BlockSpec((NZ, 2 * R, OWN), lambda i: (0, 0, 0)),
        out_shape=jax.ShapeDtypeStruct((NZ, 2 * R, OWN), jnp.bfloat16),
        scratch_shapes=[pltpu.VMEM((2, R, NX * TOK), jnp.bfloat16)],
        compiler_params=pltpu.CompilerParams(vmem_limit_bytes=VMEM_LIMIT),
        cost_estimate=pl.CostEstimate(
            flops=4 * NX * TOK * FEAT * R, bytes_accessed=6 * 1024 * 1024, transcendentals=0
        ),
    )(part, feat)


def exchange(array, axis):
    return lax.all_to_all(array, axis, 0, 0, tiled=True)


def swapped(array, by):
    return lax.ppermute(array, "z", [(i, i ^ by) for i in range(NZ)])


def is_far(group):
    return group % (GROUPS // 2) in (0, GROUPS // 2 - 1)


def first_neighbour(array):
    return lax.ppermute(array, "blk", [(g, g ^ 1) for g in range(GROUPS)])


def second_neighbour(array):
    pairs = []
    for g in range(GROUPS):
        other = (g + 1 if g % 2 else g - 1) % GROUPS
        for z in range(NZ):
            pairs.append((g * NZ + z, other * NZ + (z ^ QUAD if is_far(g) else z)))
    return lax.ppermute(array, ("blk", "z"), pairs)


def local(tokens, norm_gain, adapt_in, adapt_out, upstream):
    wide, narrow = jnp.float32, jnp.bfloat16
    group = lax.axis_index("blk") % (GROUPS // 2)
    far = (group == 0) | (group == GROUPS // 2 - 1)

    feat = prep(tokens[0], norm_gain[None], upstream[0])
    feat, adapt_in, adapt_out = lax.optimization_barrier((feat, adapt_in, adapt_out))
    feat = exchange(feat, "x")

    master = jnp.concatenate([adapt_in[0].T, adapt_out[0].T], axis=0)
    opposite = swapped(master, QUAD)
    pair = jnp.stack([master, opposite]).astype(narrow)
    lows = [pair] + [swapped(pair, k) for k in range(1, QUAD)]
    base = second_neighbour(jnp.where(far, opposite, master)) + master + first_neighbour(master)
    feat, lows, base = lax.optimization_barrier((feat, lows, base))

    part = exchange(project(feat, lows), "x")
    pieces = grads(part, feat).reshape(2, QUAD, 2 * R, OWN)
    quad = pieces[:, 0].astype(wide)
    for k in range(1, QUAD):
        quad = quad + swapped(pieces[:, k], k).astype(wide)

    sent = quad.astype(narrow)
    second = second_neighbour(sent).astype(wide)
    second = jnp.where(far, second[::-1], second)
    around = quad + first_neighbour(sent).astype(wide) + second
    total = around[0] + swapped(around[1].astype(narrow), QUAD).astype(wide)
    mixed = (base - step_size * total) / 3.0
    return (mixed[:R].T[None], mixed[R:].T[None])


def solution(mesh):
    mesh = Mesh(mesh.devices.reshape(GROUPS, NZ, NX), ("blk", "z", "x"))
    split = P("blk", ("z", "x"), None)
    in_specs = (split, P(), split, split, split)
    return jax.shard_map(
        local, mesh=mesh, in_specs=in_specs, out_specs=(split, split), check_vma=False
    )
```

time: 183 us -> 191 us (1.044)
  the two profiles are of different devices: /device:TPU:2 before, /device:TPU:25 now
where the time goes in v3:
time: 191 us
  Pallas kernels  72.9 us (38%)
  starting transfers between devices  67.8 us (35%)
  waiting for transfers between devices  32.1 us (17%)
  blocking collectives  15.9 us (8%)
    pallas_call x1, Pallas kernels, prep(): pl.pallas_call(prep_kernel, in_specs=[pl.BlockSpec(memory_space=pl.ANY),...  65.9 us
    ppermute x8, starting transfers between devices, swapped(): return lax.ppermute(array, 'z', [(i, i ^ by) for i in range(NZ)])  36 us
    ppermute x8, waiting for transfers between devices, swapped(): return lax.ppermute(array, 'z', [(i, i ^ by) for i in range(NZ)])  26.4 us
    ppermute x2, starting transfers between devices, second_neighbour(): return lax.ppermute(array, ('blk', 'z'), pairs)  22.1 us
    all_to_all x1, blocking collectives, exchange(): return lax.all_to_all(array, axis, 0, 0, tiled=True)  15.9 us
    all_to_all x1, starting transfers between devices, exchange(): return lax.all_to_all(array, axis, 0, 0, tiled=True)  4.99 us
    ppermute x2, starting transfers between devices, first_neighbour(): return lax.ppermute(array, 'blk', [(g, g ^ 1) for g in range(GROUPS)])  4.78 us
  transfers between devices with their start and end apart: 13, of which 7 were waited for; matrix products, arithmetic and copies ran while one was open for 0% of the time, Pallas kernels for 0%

profile of v3, /device:TPU:25, one launch (start us, length us, event | category | flops | bytes accessed | tf_op | source)
XLA Modules:
  0.0 190.6 jit_solution(13686427959092883707)
XLA Ops:
  0.6 65.9 %shard_map.68 = bf16[4,2,128,2048]{3,2,1,0:T(8,128)(2,1)} custom-call(bf16[128,8192]{1,0:T(8,128)(2,1)} %bitcast.60, f32[1,8192]{1,0:T(1,128)} %bitcast.70, bf16[128,8192]{1,0:T(8,128)(2,1)} %bitcast.61), custom_call_target="tpu_custom_call" | custom-call | flops 6291456 | bytes 8388608 | tf_op jit(solution)/shard_map/pallas_call | solution.py:67
  66.5 0.0 copy-start
  66.5 0.0 copy-start.1
  66.5 5.0 %all-to-all-start = ((bf16[4,2,128,2048]{3,2,1,0:T(8,128)(2,1)}), bf16[4,2,128,2048]{3,2,1,0:T(8,128)(2,1)}, u32[]{:S(2)}, u32[]{:S(2)}) async-start(bf16[4,2,128,2048]{3,2,1,0:T(8,128)(2,1)} %shard_map.68), calls=%async_computation | async-start | bytes 8388608 | tf_op jit(solution)/shard_map/all_to_all | solution.py:172
  71.5 0.0 copy-done
  71.6 0.0 copy-done.1
  71.6 8.8 %collective-permute-start = (f32[128,256]{1,0:T(8,128)S(1)}, f32[128,256]{1,0:T(8,128)S(1)}, u32[]{:S(2)}, u32[]{:S(2)}) collective-permute-start(f32[128,256]{1,0:T(8,128)S(1)} %pad_maximum_fusion), channel_id=1, source_target_pairs={{0,16},{4,20},{8,24},{12,28},{16,0},{20,4},{24,8},{28,12},{1,17},{... | collective-permute-start | bytes 393224 | tf_op jit(solution)/shard_map/ppermute | solution.py:176
  80.4 2.9 %collective-permute-start.5 = (f32[128,256]{1,0:T(8,128)S(1)}, f32[128,256]{1,0:T(8,128)S(1)}, u32[]{:S(2)}, u32[]{:S(2)}) collective-permute-start(f32[128,256]{1,0:T(8,128)S(1)} %pad_maximum_fusion), channel_id=1, source_target_pairs={{0,32},{32,0},{64,96},{96,64},{128,160},{160,128},{192,224},{224,1... | collective-permute-start | bytes 393224 | tf_op jit(solution)/shard_map/ppermute | solution.py:184
  83.3 8.7 %collective-permute-done = f32[128,256]{1,0:T(8,128)S(1)} collective-permute-done((f32[128,256]{1,0:T(8,128)S(1)}, f32[128,256]{1,0:T(8,128)S(1)}, u32[]{:S(2)}, u32[]{:S(2)}) %collective-permute-start) | collective-permute-done | bytes 131104 | tf_op jit(solution)/shard_map/ppermute | solution.py:176
  92.1 8.8 %collective-permute-start.4 = (f32[128,256]{1,0:T(8,128)S(1)}, f32[128,256]{1,0:T(8,128)S(1)}, u32[]{:S(2)}, u32[]{:S(2)}) collective-permute-start(f32[128,256]{1,0:T(8,128)S(1)} %get-tuple-element.25), channel_id=1, source_target_pairs={{0,496},{4,500},{8,504},{12,508},{16,480},{20,484},{24,488},{28,49... | collective-permute-start | bytes 393224 | tf_op jit(solution)/shard_map/ppermute | solution.py:193
  101.0 1.9 %collective-permute-start.1 = (bf16[2,128,256]{2,1,0:T(8,128)(2,1)S(1)}, bf16[2,128,256]{2,1,0:T(8,128)(2,1)S(1)}, u32[]{:S(2)}, u32[]{:S(2)}) collective-permute-start(bf16[2,128,256]{2,1,0:T(8,128)(2,1)S(1)} %pad_maximum_fusion.1.refs_0_), channel_id=1, source_target_pairs={{0,4},{4,0},{8,12},{12,8},{16,20},{20,16},{24,28},{28,24},{1,5},{5... | collective-permute-start | bytes 393224 | tf_op jit(solution)/shard_map/ppermute | solution.py:176
  102.9 6.7 %collective-permute-start.2 = (bf16[2,128,256]{2,1,0:T(8,128)(2,1)S(1)}, bf16[2,128,256]{2,1,0:T(8,128)(2,1)S(1)}, u32[]{:S(2)}, u32[]{:S(2)}) collective-permute-start(bf16[2,128,256]{2,1,0:T(8,128)(2,1)S(1)} %pad_maximum_fusion.1.refs_0_), channel_id=1, source_target_pairs={{0,8},{4,12},{8,0},{12,4},{16,24},{20,28},{24,16},{28,20},{1,9},{5... | collective-permute-start | bytes 393224 | tf_op jit(solution)/shard_map/ppermute | solution.py:176
  109.6 1.9 %collective-permute-start.3 = (bf16[2,128,256]{2,1,0:T(8,128)(2,1)S(1)}, bf16[2,128,256]{2,1,0:T(8,128)(2,1)S(1)}, u32[]{:S(2)}, u32[]{:S(2)}) collective-permute-start(bf16[2,128,256]{2,1,0:T(8,128)(2,1)S(1)} %pad_maximum_fusion.1.refs_0_), channel_id=1, source_target_pairs={{0,12},{4,8},{8,4},{12,0},{16,28},{20,24},{24,20},{28,16},{1,13},{... | collective-permute-start | bytes 393224 | tf_op jit(solution)/shard_map/ppermute | solution.py:176
  111.5 0.0 collective-permute-done.5
  111.5 0.0 collective-permute-done.4
  111.5 0.0 collective-permute-done.1.refs_1_
  111.5 3.3 %collective-permute-done.2.refs_2_ = bf16[2,128,256]{2,1,0:T(8,128)(2,1)S(1)} collective-permute-done((bf16[2,128,256]{2,1,0:T(8,128)(2,1)S(1)}, bf16[2,128,256]{2,1,0:T(8,128)(2,1)S(1)}, u32[]{:S(2)}, u32[]{:S(2)}) %collective-permute-start.2) | collective-permute-done | bytes 131104 | tf_op jit(solution)/shard_map/ppermute | solution.py:176
  114.8 2.7 %collective-permute-done.3.refs_3_ = bf16[2,128,256]{2,1,0:T(8,128)(2,1)S(1)} collective-permute-done((bf16[2,128,256]{2,1,0:T(8,128)(2,1)S(1)}, bf16[2,128,256]{2,1,0:T(8,128)(2,1)S(1)}, u32[]{:S(2)}, u32[]{:S(2)}) %collective-permute-start.3) | collective-permute-done | bytes 131104 | tf_op jit(solution)/shard_map/ppermute | solution.py:176
  117.5 2.3 %all-to-all-done.feat_ref = bf16[4,2,128,2048]{3,2,1,0:T(8,128)(2,1)} async-done(((bf16[4,2,128,2048]{3,2,1,0:T(8,128)(2,1)}), bf16[4,2,128,2048]{3,2,1,0:T(8,128)(2,1)}, u32[]{:S(2)}, u32[]{:S(2)}) %all-to-all-start) | async-done | bytes 4194336 | tf_op jit(solution)/shard_map/all_to_all | solution.py:172
  119.8 3.5 %shard_map.69 = f32[4,4,128,128]{3,2,1,0:T(8,128)S(1)} custom-call(bf16[4,2,128,2048]{3,2,1,0:T(8,128)(2,1)} %all-to-all-done.feat_ref, bf16[2,128,256]{2,1,0:T(8,128)(2,1)S(1)} %pad_maximum_fusion.1.refs_0_, bf16[2,128,256]{2,1,0:T(8,128)(2,1)S(1)} %collective-permute-done.1.refs_1_, bf16[2,128,256]{2,1,0:T(8,128)(2,1)S(1)} %collective-permute-done.2.refs_2_, ...), custom_call_target="tpu_custom_call" | custom-call | flops 268435456 | bytes 6291456 | tf_op jit(solution)/shard_map/pallas_call | solution.py:112
  123.3 15.9 %all_to_all.10.part_ref = f32[4,4,128,128]{3,2,1,0:T(8,128)S(1)} all-to-all(f32[4,4,128,128]{3,2,1,0:T(8,128)S(1)} %shard_map.69), channel_id=1, replica_groups=mesh['blk'=16,'z'=8,'x'=4] {'x'}, dimensions={0} | all-to-all | bytes 2097152 | tf_op jit(solution)/shard_map/all_to_all | solution.py:172
  139.2 3.5 %shard_map.70 = bf16[8,128,256]{2,1,0:T(8,128)(2,1)S(1)} custom-call(f32[4,4,128,128]{3,2,1,0:T(8,128)S(1)} %all_to_all.10.part_ref, bf16[4,2,128,2048]{3,2,1,0:T(8,128)(2,1)} %all-to-all-done.feat_ref), custom_call_target="tpu_custom_call" | custom-call | flops 268435456 | bytes 6291456 | tf_op jit(solution)/shard_map/pallas_call | solution.py:154
  142.8 6.3 %collective-permute-start.8 = (bf16[2,128,256]{2,1,0:T(8,128)(2,1)S(1)}, bf16[2,128,256]{2,1,0:T(8,128)(2,1)S(1)}, u32[]{:S(2)}, u32[]{:S(2)}) collective-permute-start(bf16[2,128,256]{2,1,0:T(8,128)(2,1)S(1)} %get-tuple-element.22), channel_id=1, source_target_pairs={{0,12},{4,8},{8,4},{12,0},{16,28},{20,24},{24,20},{28,16},{1,13},{... | collective-permute-start | bytes 393224 | tf_op jit(solution)/shard_map/ppermute | solution.py:176
  149.0 1.9 %collective-permute-start.7 = (bf16[2,128,256]{2,1,0:T(8,128)(2,1)S(1)}, bf16[2,128,256]{2,1,0:T(8,128)(2,1)S(1)}, u32[]{:S(2)}, u32[]{:S(2)}) collective-permute-start(bf16[2,128,256]{2,1,0:T(8,128)(2,1)S(1)} %get-tuple-element.21), channel_id=1, source_target_pairs={{0,8},{4,12},{8,0},{12,4},{16,24},{20,28},{24,16},{28,20},{1,9},{5... | collective-permute-start | bytes 393224 | tf_op jit(solution)/shard_map/ppermute | solution.py:176
  151.0 2.2 %collective-permute-start.6 = (bf16[2,128,256]{2,1,0:T(8,128)(2,1)S(1)}, bf16[2,128,256]{2,1,0:T(8,128)(2,1)S(1)}, u32[]{:S(2)}, u32[]{:S(2)}) collective-permute-start(bf16[2,128,256]{2,1,0:T(8,128)(2,1)S(1)} %get-tuple-element.20), channel_id=1, source_target_pairs={{0,4},{4,0},{8,12},{12,8},{16,20},{20,16},{24,28},{28,24},{1,5},{5... | collective-permute-start | bytes 393224 | tf_op jit(solution)/shard_map/ppermute | solution.py:176
  153.2 0.0 collective-permute-done.8
  153.2 6.3 %collective-permute-done.7 = bf16[2,128,256]{2,1,0:T(8,128)(2,1)S(1)} collective-permute-done((bf16[2,128,256]{2,1,0:T(8,128)(2,1)S(1)}, bf16[2,128,256]{2,1,0:T(8,128)(2,1)S(1)}, u32[]{:S(2)}, u32[]{:S(2)}) %collective-permute-start.7) | collective-permute-done | bytes 131104 | tf_op jit(solution)/shard_map/ppermute | solution.py:176
  159.5 0.0 collective-permute-done.6
  159.5 0.1 fusion.7
  159.5 13.2 %collective-permute-start.10 = (bf16[2,128,256]{2,1,0:T(8,128)(2,1)S(1)}, bf16[2,128,256]{2,1,0:T(8,128)(2,1)S(1)}, u32[]{:S(2)}, u32[]{:S(2)}) collective-permute-start(bf16[2,128,256]{2,1,0:T(8,128)(2,1)S(1)} %fusion.7), channel_id=1, source_target_pairs={{0,496},{4,500},{8,504},{12,508},{16,480},{20,484},{24,488},{28,49... | collective-permute-start | bytes 393224 | tf_op jit(solution)/shard_map/ppermute | solution.py:193
  172.8 1.9 %collective-permute-start.9 = (bf16[2,128,256]{2,1,0:T(8,128)(2,1)S(1)}, bf16[2,128,256]{2,1,0:T(8,128)(2,1)S(1)}, u32[]{:S(2)}, u32[]{:S(2)}) collective-permute-start(bf16[2,128,256]{2,1,0:T(8,128)(2,1)S(1)} %fusion.7), channel_id=1, source_target_pairs={{0,32},{32,0},{64,96},{96,64},{128,160},{160,128},{192,224},{224,1... | collective-permute-start | bytes 393224 | tf_op jit(solution)/shard_map/ppermute | solution.py:184
  174.7 3.3 %collective-permute-done.10 = bf16[2,128,256]{2,1,0:T(8,128)(2,1)S(1)} collective-permute-done((bf16[2,128,256]{2,1,0:T(8,128)(2,1)S(1)}, bf16[2,128,256]{2,1,0:T(8,128)(2,1)S(1)}, u32[]{:S(2)}, u32[]{:S(2)}) %collective-permute-start.10) | collective-permute-done | bytes 131104 | tf_op jit(solution)/shard_map/ppermute | solution.py:193
  178.0 0.0 collective-permute-done.9
  178.1 0.1 fusion
  178.2 6.3 %collective-permute-start.11 = (bf16[128,256]{1,0:T(8,128)(2,1)S(1)}, bf16[128,256]{1,0:T(8,128)(2,1)S(1)}, u32[]{:S(2)}, u32[]{:S(2)}) collective-permute-start(bf16[128,256]{1,0:T(8,128)(2,1)S(1)} %fusion.8), channel_id=1, source_target_pairs={{0,16},{4,20},{8,24},{12,28},{16,0},{20,4},{24,8},{28,12},{1,17},{... | collective-permute-start | bytes 196616 | tf_op jit(solution)/shard_map/ppermute | solution.py:176
  184.5 5.5 %collective-permute-done.11 = bf16[128,256]{1,0:T(8,128)(2,1)S(1)} collective-permute-done((bf16[128,256]{1,0:T(8,128)(2,1)S(1)}, bf16[128,256]{1,0:T(8,128)(2,1)S(1)}, u32[]{:S(2)}, u32[]{:S(2)}) %collective-permute-start.11) | collective-permute-done | bytes 65568 | tf_op jit(solution)/shard_map/ppermute | solution.py:176
  190.0 0.7 slice_bitcast_fusion.5
  (9 shorter events, 0.2 us)
Async XLA Ops:
  66.5 5.0 %copy-start = (f32[1,256,64]{1,2,0:T(8,128)S(1)}, f32[1,256,64]{1,2,0:T(8,128)}, u32[]{:S(2)}) copy-start(f32[1,256,64]{1,2,0:T(8,128)} %param.8) | copy-start | bytes 196612
  66.5 5.0 %copy-start.1 = (f32[1,256,64]{1,2,0:T(8,128)S(1)}, f32[1,256,64]{1,2,0:T(8,128)}, u32[]{:S(2)}) copy-start(f32[1,256,64]{1,2,0:T(8,128)} %param.7) | copy-start | bytes 196612
  66.5 53.3 %all-to-all-start = ((bf16[4,2,128,2048]{3,2,1,0:T(8,128)(2,1)}), bf16[4,2,128,2048]{3,2,1,0:T(8,128)(2,1)}, u32[]{:S(2)}, u32[]{:S(2)}) async-start(bf16[4,2,128,2048]{3,2,1,0:T(8,128)(2,1)} %shard_map.68), calls=%async_computation | async-start | bytes 8388608 | tf_op jit(solution)/shard_map/all_to_all | solution.py:172
  71.6 20.5 %collective-permute-start = (f32[128,256]{1,0:T(8,128)S(1)}, f32[128,256]{1,0:T(8,128)S(1)}, u32[]{:S(2)}, u32[]{:S(2)}) collective-permute-start(f32[128,256]{1,0:T(8,128)S(1)} %pad_maximum_fusion), channel_id=1, source_target_pairs={{0,16},{4,20},{8,24},{12,28},{16,0},{20,4},{24,8},{28,12},{1,17},{... | collective-permute-start | bytes 393224 | tf_op jit(solution)/shard_map/ppermute | solution.py:176
  80.4 31.1 %collective-permute-start.5 = (f32[128,256]{1,0:T(8,128)S(1)}, f32[128,256]{1,0:T(8,128)S(1)}, u32[]{:S(2)}, u32[]{:S(2)}) collective-permute-start(f32[128,256]{1,0:T(8,128)S(1)} %pad_maximum_fusion), channel_id=1, source_target_pairs={{0,32},{32,0},{64,96},{96,64},{128,160},{160,128},{192,224},{224,1... | collective-permute-start | bytes 393224 | tf_op jit(solution)/shard_map/ppermute | solution.py:184
  92.1 19.4 %collective-permute-start.4 = (f32[128,256]{1,0:T(8,128)S(1)}, f32[128,256]{1,0:T(8,128)S(1)}, u32[]{:S(2)}, u32[]{:S(2)}) collective-permute-start(f32[128,256]{1,0:T(8,128)S(1)} %get-tuple-element.25), channel_id=1, source_target_pairs={{0,496},{4,500},{8,504},{12,508},{16,480},{20,484},{24,488},{28,49... | collective-permute-start | bytes 393224 | tf_op jit(solution)/shard_map/ppermute | solution.py:193
  101.0 10.6 %collective-permute-start.1 = (bf16[2,128,256]{2,1,0:T(8,128)(2,1)S(1)}, bf16[2,128,256]{2,1,0:T(8,128)(2,1)S(1)}, u32[]{:S(2)}, u32[]{:S(2)}) collective-permute-start(bf16[2,128,256]{2,1,0:T(8,128)(2,1)S(1)} %pad_maximum_fusion.1.refs_0_), channel_id=1, source_target_pairs={{0,4},{4,0},{8,12},{12,8},{16,20},{20,16},{24,28},{28,24},{1,5},{5... | collective-permute-start | bytes 393224 | tf_op jit(solution)/shard_map/ppermute | solution.py:176
  102.9 12.0 %collective-permute-start.2 = (bf16[2,128,256]{2,1,0:T(8,128)(2,1)S(1)}, bf16[2,128,256]{2,1,0:T(8,128)(2,1)S(1)}, u32[]{:S(2)}, u32[]{:S(2)}) collective-permute-start(bf16[2,128,256]{2,1,0:T(8,128)(2,1)S(1)} %pad_maximum_fusion.1.refs_0_), channel_id=1, source_target_pairs={{0,8},{4,12},{8,0},{12,4},{16,24},{20,28},{24,16},{28,20},{1,9},{5... | collective-permute-start | bytes 393224 | tf_op jit(solution)/shard_map/ppermute | solution.py:176
  109.6 8.0 %collective-permute-start.3 = (bf16[2,128,256]{2,1,0:T(8,128)(2,1)S(1)}, bf16[2,128,256]{2,1,0:T(8,128)(2,1)S(1)}, u32[]{:S(2)}, u32[]{:S(2)}) collective-permute-start(bf16[2,128,256]{2,1,0:T(8,128)(2,1)S(1)} %pad_maximum_fusion.1.refs_0_), channel_id=1, source_target_pairs={{0,12},{4,8},{8,4},{12,0},{16,28},{20,24},{24,20},{28,16},{1,13},{... | collective-permute-start | bytes 393224 | tf_op jit(solution)/shard_map/ppermute | solution.py:176
  142.8 10.4 %collective-permute-start.8 = (bf16[2,128,256]{2,1,0:T(8,128)(2,1)S(1)}, bf16[2,128,256]{2,1,0:T(8,128)(2,1)S(1)}, u32[]{:S(2)}, u32[]{:S(2)}) collective-permute-start(bf16[2,128,256]{2,1,0:T(8,128)(2,1)S(1)} %get-tuple-element.22), channel_id=1, source_target_pairs={{0,12},{4,8},{8,4},{12,0},{16,28},{20,24},{24,20},{28,16},{1,13},{... | collective-permute-start | bytes 393224 | tf_op jit(solution)/shard_map/ppermute | solution.py:176
  149.0 10.4 %collective-permute-start.7 = (bf16[2,128,256]{2,1,0:T(8,128)(2,1)S(1)}, bf16[2,128,256]{2,1,0:T(8,128)(2,1)S(1)}, u32[]{:S(2)}, u32[]{:S(2)}) collective-permute-start(bf16[2,128,256]{2,1,0:T(8,128)(2,1)S(1)} %get-tuple-element.21), channel_id=1, source_target_pairs={{0,8},{4,12},{8,0},{12,4},{16,24},{20,28},{24,16},{28,20},{1,9},{5... | collective-permute-start | bytes 393224 | tf_op jit(solution)/shard_map/ppermute | solution.py:176
  151.0 8.5 %collective-permute-start.6 = (bf16[2,128,256]{2,1,0:T(8,128)(2,1)S(1)}, bf16[2,128,256]{2,1,0:T(8,128)(2,1)S(1)}, u32[]{:S(2)}, u32[]{:S(2)}) collective-permute-start(bf16[2,128,256]{2,1,0:T(8,128)(2,1)S(1)} %get-tuple-element.20), channel_id=1, source_target_pairs={{0,4},{4,0},{8,12},{12,8},{16,20},{20,16},{24,28},{28,24},{1,5},{5... | collective-permute-start | bytes 393224 | tf_op jit(solution)/shard_map/ppermute | solution.py:176
  159.5 18.5 %collective-permute-start.10 = (bf16[2,128,256]{2,1,0:T(8,128)(2,1)S(1)}, bf16[2,128,256]{2,1,0:T(8,128)(2,1)S(1)}, u32[]{:S(2)}, u32[]{:S(2)}) collective-permute-start(bf16[2,128,256]{2,1,0:T(8,128)(2,1)S(1)} %fusion.7), channel_id=1, source_target_pairs={{0,496},{4,500},{8,504},{12,508},{16,480},{20,484},{24,488},{28,49... | collective-permute-start | bytes 393224 | tf_op jit(solution)/shard_map/ppermute | solution.py:193
  172.8 5.3 %collective-permute-start.9 = (bf16[2,128,256]{2,1,0:T(8,128)(2,1)S(1)}, bf16[2,128,256]{2,1,0:T(8,128)(2,1)S(1)}, u32[]{:S(2)}, u32[]{:S(2)}) collective-permute-start(bf16[2,128,256]{2,1,0:T(8,128)(2,1)S(1)} %fusion.7), channel_id=1, source_target_pairs={{0,32},{32,0},{64,96},{96,64},{128,160},{160,128},{192,224},{224,1... | collective-permute-start | bytes 393224 | tf_op jit(solution)/shard_map/ppermute | solution.py:184
  178.2 11.7 %collective-permute-start.11 = (bf16[128,256]{1,0:T(8,128)(2,1)S(1)}, bf16[128,256]{1,0:T(8,128)(2,1)S(1)}, u32[]{:S(2)}, u32[]{:S(2)}) collective-permute-start(bf16[128,256]{1,0:T(8,128)(2,1)S(1)} %fusion.8), channel_id=1, source_target_pairs={{0,16},{4,20},{8,24},{12,28},{16,0},{20,4},{24,8},{28,12},{1,17},{... | collective-permute-start | bytes 196616 | tf_op jit(solution)/shard_map/ppermute | solution.py:176

commit v4 on v3

--- a/solution.py
+++ b/solution.py
@@ -32,34 +32,38 @@
 DIRECT_LIMIT = 60 * 1024 * 1024
 
 
-def prep_kernel(tok_ref, gain_ref, up_ref, out_ref, raw_ref, done_ref, in_sem, out_sem, up_sem):
-    loads = []
+def prep_kernel(tok_ref, gain_ref, up_ref, out_ref, raw_ref, done_ref, in_sem, out_sem):
+    sources = (up_ref, tok_ref)
+    loads = {}
     for c in range(CHUNKS):
         rows = pl.ds(c * ROWS, ROWS)
-        loads.append(pltpu.make_async_copy(tok_ref.at[rows], raw_ref.at[c], in_sem.at[c]))
-        loads[-1].start()
-    moves = []
-    for b in range(NX * NZ):
-        z, x = divmod(b, NX)
-        src = up_ref.at[:, pl.ds(b * OWN, OWN)]
-        dst = out_ref.at[x, 1, :, pl.ds(z * OWN, OWN)]
-        moves.append(pltpu.make_async_copy(src, dst, up_sem.at[b]))
-        moves[-1].start()
+        for h in range(2):
+            loads[c, h] = pltpu.make_async_copy(
+                sources[h].at[rows], raw_ref.at[c, h], in_sem.at[c, h]
+            )
+            loads[c, h].start()
     stores = []
     for c in range(CHUNKS):
-        loads[c].wait()
-        wide = raw_ref[c].astype(jnp.float32)
-        scale = lax.rsqrt(jnp.mean(wide * wide, axis=-1, keepdims=True) + epsilon)
-        for b in range(NX * NZ):
-            z, x = divmod(b, NX)
-            src = slice(b * OWN, (b + 1) * OWN)
-            part = raw_ref[c, :, src].astype(jnp.float32) * scale * gain_ref[:, src]
-            done_ref[c, x, :, z * OWN : (z + 1) * OWN] = part.astype(jnp.bfloat16)
-        for x in range(NX):
-            dst = out_ref.at[x, 0, pl.ds(c * ROWS, ROWS)]
-            stores.append(pltpu.make_async_copy(done_ref.at[c, x], dst, out_sem.at[c, x]))
-            stores[-1].start()
-    for copy in moves + stores:
+        rows = pl.ds(c * ROWS, ROWS)
+        for h in range(2):
+            loads[c, h].wait()
+            if h == 1:
+                wide = raw_ref[c, h].astype(jnp.float32)
+                scale = lax.rsqrt(jnp.mean(wide * wide, axis=-1, keepdims=True) + epsilon)
+            for x in range(NX):
+                for z in range(NZ):
+                    at = slice((z * NX + x) * OWN, (z * NX + x + 1) * OWN)
+                    part = raw_ref[c, h, :, at]
+                    if h == 1:
+                        part = part.astype(jnp.float32) * scale * gain_ref[:, at]
+                    part = part.astype(jnp.bfloat16)
+                    done_ref[c, x, h, :, z * OWN : (z + 1) * OWN] = part
+                dst = out_ref.at[x, h, rows]
+                stores.append(
+                    pltpu.make_async_copy(done_ref.at[c, x, h], dst, out_sem.at[c, x, h])
+                )
+                stores[-1].start()
+    for copy in stores:
         copy.wait()
 
 
@@ -74,11 +78,10 @@
         out_specs=pl.BlockSpec(memory_space=pl.ANY),
         out_shape=jax.ShapeDtypeStruct((NX, 2, TOK, FEAT), jnp.bfloat16),
         scratch_shapes=[
-            pltpu.VMEM((CHUNKS, ROWS, D), jnp.bfloat16),
-            pltpu.VMEM((CHUNKS, NX, ROWS, FEAT), jnp.bfloat16),
-            pltpu.SemaphoreType.DMA((CHUNKS,)),
-            pltpu.SemaphoreType.DMA((CHUNKS, NX)),
-            pltpu.SemaphoreType.DMA((NX * NZ,)),
+            pltpu.VMEM((CHUNKS, 2, ROWS, D), jnp.bfloat16),
+            pltpu.VMEM((CHUNKS, NX, 2, ROWS, FEAT), jnp.bfloat16),
+            pltpu.SemaphoreType.DMA((CHUNKS, 2)),
+            pltpu.SemaphoreType.DMA((CHUNKS, NX, 2)),
         ],
         compiler_params=pltpu.CompilerParams(vmem_limit_bytes=DIRECT_LIMIT),
         cost_estimate=pl.CostEstimate(
@@ -102,7 +105,7 @@
         for half in range(2):
             rows = slice(half * R, (half + 1) * R)
             part = lax.dot_general(
-                low_ref[rows], feat_ref[s, half], LAST, preferred_element_type=jnp.float32
+                low_ref[rows], feat_ref[s, 1 - half], LAST, preferred_element_type=jnp.float32
             )
             for x in range(NX):
                 out_ref[x, s, rows] = part
@@ -142,7 +145,7 @@
         rows = slice(half * R, (half + 1) * R)
         grad = jnp.dot(
             low_ref[half],
-            feat_ref[:, half].reshape(NX * TOK, 2 * OWN),
+            feat_ref[:, 1 - half].reshape(NX * TOK, 2 * OWN),
             preferred_element_type=jnp.float32,
         )
         grad = (grad * scale).astype(jnp.bfloat16)
@@ -195,8 +198,7 @@
 
 def local(tokens, norm_gain, adapt_in, adapt_out, upstream):
     wide, narrow = jnp.float32, jnp.bfloat16
-    group = lax.axis_index("blk") % (GROUPS // 2)
-    far = (group == 0) | (group == GROUPS // 2 - 1)
+    far = ((lax.axis_index("blk") + 1) & (GROUPS // 2 - 1)) < 2
 
     feat = prep(tokens[0], norm_gain[None], upstream[0])
     feat, adapt_in, adapt_out = lax.optimization_barrier((feat, adapt_in, adapt_out))

time: 191 us -> 130 us (0.68)
  Pallas kernels: 72.9 us -> 11.5 us
    pallas_call x1, Pallas kernels: 65.9 us -> 4.53 us  [prep(): pl.pallas_call(prep_kernel, in_specs=[pl.BlockSpec(memory_space=pl.ANY),...]
where the time goes in v4:
time: 130 us; the launch traced here: 129 us
  starting transfers between devices  67.8 us (52%)
  waiting for transfers between devices  32.1 us (25%)
  blocking collectives  15.9 us (12%)
  Pallas kernels  11.5 us (9%)
    ppermute x8, starting transfers between devices, swapped(): return lax.ppermute(array, 'z', [(i, i ^ by) for i in range(NZ)])  36 us
    ppermute x8, waiting for transfers between devices, swapped(): return lax.ppermute(array, 'z', [(i, i ^ by) for i in range(NZ)])  26.5 us
    ppermute x2, starting transfers between devices, second_neighbour(): return lax.ppermute(array, ('blk', 'z'), pairs)  22.1 us
    all_to_all x1, blocking collectives, exchange(): return lax.all_to_all(array, axis, 0, 0, tiled=True)  15.9 us
    all_to_all x1, starting transfers between devices, exchange(): return lax.all_to_all(array, axis, 0, 0, tiled=True)  4.99 us
    ppermute x2, starting transfers between devices, first_neighbour(): return lax.ppermute(array, 'blk', [(g, g ^ 1) for g in range(GROUPS)])  4.78 us
    pallas_call x1, Pallas kernels, prep(): pl.pallas_call(prep_kernel, in_specs=[pl.BlockSpec(memory_space=pl.ANY),...  4.53 us
    pallas_call x1, Pallas kernels, grads(): pl.pallas_call(grads_kernel, grid=(NZ // 2,), in_specs=[pl.BlockSpec(part...  3.53 us
  transfers between devices with their start and end apart: 13, of which 7 were waited for; matrix products, arithmetic and copies ran while one was open for 0% of the time, Pallas kernels for 0%

profile of v4, /device:TPU:25, one launch (start us, length us, event | category | flops | bytes accessed | tf_op | source)
XLA Modules:
  0.0 129.3 jit_solution(1485820420005496425)
XLA Ops:
  0.6 4.5 %shard_map.68 = bf16[4,2,128,2048]{3,2,1,0:T(8,128)(2,1)} custom-call(bf16[128,8192]{1,0:T(8,128)(2,1)} %bitcast.60, f32[1,8192]{1,0:T(1,128)} %bitcast.70, bf16[128,8192]{1,0:T(8,128)(2,1)} %bitcast.61), custom_call_target="tpu_custom_call" | custom-call | flops 6291456 | bytes 8388608 | tf_op jit(solution)/shard_map/pallas_call | solution.py:71
  5.2 0.0 copy-start
  5.2 0.0 copy-start.1
  5.2 5.0 %all-to-all-start = ((bf16[4,2,128,2048]{3,2,1,0:T(8,128)(2,1)}), bf16[4,2,128,2048]{3,2,1,0:T(8,128)(2,1)}, u32[]{:S(2)}, u32[]{:S(2)}) async-start(bf16[4,2,128,2048]{3,2,1,0:T(8,128)(2,1)} %shard_map.68), calls=%async_computation | async-start | bytes 8388608 | tf_op jit(solution)/shard_map/all_to_all | solution.py:175
  10.2 0.0 copy-done
  10.2 0.0 copy-done.1
  10.2 8.8 %collective-permute-start = (f32[128,256]{1,0:T(8,128)S(1)}, f32[128,256]{1,0:T(8,128)S(1)}, u32[]{:S(2)}, u32[]{:S(2)}) collective-permute-start(f32[128,256]{1,0:T(8,128)S(1)} %pad_maximum_fusion), channel_id=1, source_target_pairs={{0,16},{4,20},{8,24},{12,28},{16,0},{20,4},{24,8},{28,12},{1,17},{... | collective-permute-start | bytes 393224 | tf_op jit(solution)/shard_map/ppermute | solution.py:179
  19.1 2.9 %collective-permute-start.5 = (f32[128,256]{1,0:T(8,128)S(1)}, f32[128,256]{1,0:T(8,128)S(1)}, u32[]{:S(2)}, u32[]{:S(2)}) collective-permute-start(f32[128,256]{1,0:T(8,128)S(1)} %pad_maximum_fusion), channel_id=1, source_target_pairs={{0,32},{32,0},{64,96},{96,64},{128,160},{160,128},{192,224},{224,1... | collective-permute-start | bytes 393224 | tf_op jit(solution)/shard_map/ppermute | solution.py:187
  21.9 8.8 %collective-permute-done = f32[128,256]{1,0:T(8,128)S(1)} collective-permute-done((f32[128,256]{1,0:T(8,128)S(1)}, f32[128,256]{1,0:T(8,128)S(1)}, u32[]{:S(2)}, u32[]{:S(2)}) %collective-permute-start) | collective-permute-done | bytes 131104 | tf_op jit(solution)/shard_map/ppermute | solution.py:179
  30.7 8.8 %collective-permute-start.4 = (f32[128,256]{1,0:T(8,128)S(1)}, f32[128,256]{1,0:T(8,128)S(1)}, u32[]{:S(2)}, u32[]{:S(2)}) collective-permute-start(f32[128,256]{1,0:T(8,128)S(1)} %get-tuple-element.25), channel_id=1, source_target_pairs={{0,496},{4,500},{8,504},{12,508},{16,480},{20,484},{24,488},{28,49... | collective-permute-start | bytes 393224 | tf_op jit(solution)/shard_map/ppermute | solution.py:196
  39.6 1.9 %collective-permute-start.1 = (bf16[2,128,256]{2,1,0:T(8,128)(2,1)S(1)}, bf16[2,128,256]{2,1,0:T(8,128)(2,1)S(1)}, u32[]{:S(2)}, u32[]{:S(2)}) collective-permute-start(bf16[2,128,256]{2,1,0:T(8,128)(2,1)S(1)} %pad_maximum_fusion.1.refs_0_), channel_id=1, source_target_pairs={{0,4},{4,0},{8,12},{12,8},{16,20},{20,16},{24,28},{28,24},{1,5},{5... | collective-permute-start | bytes 393224 | tf_op jit(solution)/shard_map/ppermute | solution.py:179
  41.5 6.7 %collective-permute-start.2 = (bf16[2,128,256]{2,1,0:T(8,128)(2,1)S(1)}, bf16[2,128,256]{2,1,0:T(8,128)(2,1)S(1)}, u32[]{:S(2)}, u32[]{:S(2)}) collective-permute-start(bf16[2,128,256]{2,1,0:T(8,128)(2,1)S(1)} %pad_maximum_fusion.1.refs_0_), channel_id=1, source_target_pairs={{0,8},{4,12},{8,0},{12,4},{16,24},{20,28},{24,16},{28,20},{1,9},{5... | collective-permute-start | bytes 393224 | tf_op jit(solution)/shard_map/ppermute | solution.py:179
  48.2 1.9 %collective-permute-start.3 = (bf16[2,128,256]{2,1,0:T(8,128)(2,1)S(1)}, bf16[2,128,256]{2,1,0:T(8,128)(2,1)S(1)}, u32[]{:S(2)}, u32[]{:S(2)}) collective-permute-start(bf16[2,128,256]{2,1,0:T(8,128)(2,1)S(1)} %pad_maximum_fusion.1.refs_0_), channel_id=1, source_target_pairs={{0,12},{4,8},{8,4},{12,0},{16,28},{20,24},{24,20},{28,16},{1,13},{... | collective-permute-start | bytes 393224 | tf_op jit(solution)/shard_map/ppermute | solution.py:179
  50.1 0.0 collective-permute-done.5
  50.1 0.0 collective-permute-done.4
  50.2 0.0 collective-permute-done.1.refs_1_
  50.2 3.3 %collective-permute-done.2.refs_2_ = bf16[2,128,256]{2,1,0:T(8,128)(2,1)S(1)} collective-permute-done((bf16[2,128,256]{2,1,0:T(8,128)(2,1)S(1)}, bf16[2,128,256]{2,1,0:T(8,128)(2,1)S(1)}, u32[]{:S(2)}, u32[]{:S(2)}) %collective-permute-start.2) | collective-permute-done | bytes 131104 | tf_op jit(solution)/shard_map/ppermute | solution.py:179
  53.5 2.7 %collective-permute-done.3.refs_3_ = bf16[2,128,256]{2,1,0:T(8,128)(2,1)S(1)} collective-permute-done((bf16[2,128,256]{2,1,0:T(8,128)(2,1)S(1)}, bf16[2,128,256]{2,1,0:T(8,128)(2,1)S(1)}, u32[]{:S(2)}, u32[]{:S(2)}) %collective-permute-start.3) | collective-permute-done | bytes 131104 | tf_op jit(solution)/shard_map/ppermute | solution.py:179
  56.2 2.3 %all-to-all-done.feat_ref = bf16[4,2,128,2048]{3,2,1,0:T(8,128)(2,1)} async-done(((bf16[4,2,128,2048]{3,2,1,0:T(8,128)(2,1)}), bf16[4,2,128,2048]{3,2,1,0:T(8,128)(2,1)}, u32[]{:S(2)}, u32[]{:S(2)}) %all-to-all-start) | async-done | bytes 4194336 | tf_op jit(solution)/shard_map/all_to_all | solution.py:175
  58.5 3.5 %shard_map.69 = f32[4,4,128,128]{3,2,1,0:T(8,128)S(1)} custom-call(bf16[4,2,128,2048]{3,2,1,0:T(8,128)(2,1)} %all-to-all-done.feat_ref, bf16[2,128,256]{2,1,0:T(8,128)(2,1)S(1)} %pad_maximum_fusion.1.refs_0_, bf16[2,128,256]{2,1,0:T(8,128)(2,1)S(1)} %collective-permute-done.1.refs_1_, bf16[2,128,256]{2,1,0:T(8,128)(2,1)S(1)} %collective-permute-done.2.refs_2_, ...), custom_call_target="tpu_custom_call" | custom-call | flops 268435456 | bytes 6291456 | tf_op jit(solution)/shard_map/pallas_call | solution.py:115
  61.9 15.9 %all_to_all.10.part_ref = f32[4,4,128,128]{3,2,1,0:T(8,128)S(1)} all-to-all(f32[4,4,128,128]{3,2,1,0:T(8,128)S(1)} %shard_map.69), channel_id=1, replica_groups=mesh['blk'=16,'z'=8,'x'=4] {'x'}, dimensions={0} | all-to-all | bytes 2097152 | tf_op jit(solution)/shard_map/all_to_all | solution.py:175
  77.9 3.5 %shard_map.70 = bf16[8,128,256]{2,1,0:T(8,128)(2,1)S(1)} custom-call(f32[4,4,128,128]{3,2,1,0:T(8,128)S(1)} %all_to_all.10.part_ref, bf16[4,2,128,2048]{3,2,1,0:T(8,128)(2,1)} %all-to-all-done.feat_ref), custom_call_target="tpu_custom_call" | custom-call | flops 268435456 | bytes 6291456 | tf_op jit(solution)/shard_map/pallas_call | solution.py:157
  81.4 6.3 %collective-permute-start.8 = (bf16[2,128,256]{2,1,0:T(8,128)(2,1)S(1)}, bf16[2,128,256]{2,1,0:T(8,128)(2,1)S(1)}, u32[]{:S(2)}, u32[]{:S(2)}) collective-permute-start(bf16[2,128,256]{2,1,0:T(8,128)(2,1)S(1)} %get-tuple-element.22), channel_id=1, source_target_pairs={{0,12},{4,8},{8,4},{12,0},{16,28},{20,24},{24,20},{28,16},{1,13},{... | collective-permute-start | bytes 393224 | tf_op jit(solution)/shard_map/ppermute | solution.py:179
  87.7 1.9 %collective-permute-start.7 = (bf16[2,128,256]{2,1,0:T(8,128)(2,1)S(1)}, bf16[2,128,256]{2,1,0:T(8,128)(2,1)S(1)}, u32[]{:S(2)}, u32[]{:S(2)}) collective-permute-start(bf16[2,128,256]{2,1,0:T(8,128)(2,1)S(1)} %get-tuple-element.21), channel_id=1, source_target_pairs={{0,8},{4,12},{8,0},{12,4},{16,24},{20,28},{24,16},{28,20},{1,9},{5... | collective-permute-start | bytes 393224 | tf_op jit(solution)/shard_map/ppermute | solution.py:179
  89.6 2.2 %collective-permute-start.6 = (bf16[2,128,256]{2,1,0:T(8,128)(2,1)S(1)}, bf16[2,128,256]{2,1,0:T(8,128)(2,1)S(1)}, u32[]{:S(2)}, u32[]{:S(2)}) collective-permute-start(bf16[2,128,256]{2,1,0:T(8,128)(2,1)S(1)} %get-tuple-element.20), channel_id=1, source_target_pairs={{0,4},{4,0},{8,12},{12,8},{16,20},{20,16},{24,28},{28,24},{1,5},{5... | collective-permute-start | bytes 393224 | tf_op jit(solution)/shard_map/ppermute | solution.py:179
  91.8 0.0 collective-permute-done.8
  91.8 6.3 %collective-permute-done.7 = bf16[2,128,256]{2,1,0:T(8,128)(2,1)S(1)} collective-permute-done((bf16[2,128,256]{2,1,0:T(8,128)(2,1)S(1)}, bf16[2,128,256]{2,1,0:T(8,128)(2,1)S(1)}, u32[]{:S(2)}, u32[]{:S(2)}) %collective-permute-start.7) | collective-permute-done | bytes 131104 | tf_op jit(solution)/shard_map/ppermute | solution.py:179
  98.1 0.0 collective-permute-done.6
  98.1 0.1 fusion.7
  98.2 13.2 %collective-permute-start.10 = (bf16[2,128,256]{2,1,0:T(8,128)(2,1)S(1)}, bf16[2,128,256]{2,1,0:T(8,128)(2,1)S(1)}, u32[]{:S(2)}, u32[]{:S(2)}) collective-permute-start(bf16[2,128,256]{2,1,0:T(8,128)(2,1)S(1)} %fusion.7), channel_id=1, source_target_pairs={{0,496},{4,500},{8,504},{12,508},{16,480},{20,484},{24,488},{28,49... | collective-permute-start | bytes 393224 | tf_op jit(solution)/shard_map/ppermute | solution.py:196
  111.4 1.9 %collective-permute-start.9 = (bf16[2,128,256]{2,1,0:T(8,128)(2,1)S(1)}, bf16[2,128,256]{2,1,0:T(8,128)(2,1)S(1)}, u32[]{:S(2)}, u32[]{:S(2)}) collective-permute-start(bf16[2,128,256]{2,1,0:T(8,128)(2,1)S(1)} %fusion.7), channel_id=1, source_target_pairs={{0,32},{32,0},{64,96},{96,64},{128,160},{160,128},{192,224},{224,1... | collective-permute-start | bytes 393224 | tf_op jit(solution)/shard_map/ppermute | solution.py:187
  113.3 3.3 %collective-permute-done.10 = bf16[2,128,256]{2,1,0:T(8,128)(2,1)S(1)} collective-permute-done((bf16[2,128,256]{2,1,0:T(8,128)(2,1)S(1)}, bf16[2,128,256]{2,1,0:T(8,128)(2,1)S(1)}, u32[]{:S(2)}, u32[]{:S(2)}) %collective-permute-start.10) | collective-permute-done | bytes 131104 | tf_op jit(solution)/shard_map/ppermute | solution.py:196
  116.7 0.0 collective-permute-done.9
  116.7 0.1 fusion
  116.8 6.3 %collective-permute-start.11 = (bf16[128,256]{1,0:T(8,128)(2,1)S(1)}, bf16[128,256]{1,0:T(8,128)(2,1)S(1)}, u32[]{:S(2)}, u32[]{:S(2)}) collective-permute-start(bf16[128,256]{1,0:T(8,128)(2,1)S(1)} %fusion.8), channel_id=1, source_target_pairs={{0,16},{4,20},{8,24},{12,28},{16,0},{20,4},{24,8},{28,12},{1,17},{... | collective-permute-start | bytes 196616 | tf_op jit(solution)/shard_map/ppermute | solution.py:179
  123.1 5.5 %collective-permute-done.11 = bf16[128,256]{1,0:T(8,128)(2,1)S(1)} collective-permute-done((bf16[128,256]{1,0:T(8,128)(2,1)S(1)}, bf16[128,256]{1,0:T(8,128)(2,1)S(1)}, u32[]{:S(2)}, u32[]{:S(2)}) %collective-permute-start.11) | collective-permute-done | bytes 65568 | tf_op jit(solution)/shard_map/ppermute | solution.py:179
  128.6 0.7 slice_bitcast_fusion.5
  (9 shorter events, 0.2 us)
Async XLA Ops:
  5.2 5.0 %copy-start = (f32[1,256,64]{1,2,0:T(8,128)S(1)}, f32[1,256,64]{1,2,0:T(8,128)}, u32[]{:S(2)}) copy-start(f32[1,256,64]{1,2,0:T(8,128)} %param.8) | copy-start | bytes 196612
  5.2 5.0 %copy-start.1 = (f32[1,256,64]{1,2,0:T(8,128)S(1)}, f32[1,256,64]{1,2,0:T(8,128)}, u32[]{:S(2)}) copy-start(f32[1,256,64]{1,2,0:T(8,128)} %param.7) | copy-start | bytes 196612
  5.2 53.3 %all-to-all-start = ((bf16[4,2,128,2048]{3,2,1,0:T(8,128)(2,1)}), bf16[4,2,128,2048]{3,2,1,0:T(8,128)(2,1)}, u32[]{:S(2)}, u32[]{:S(2)}) async-start(bf16[4,2,128,2048]{3,2,1,0:T(8,128)(2,1)} %shard_map.68), calls=%async_computation | async-start | bytes 8388608 | tf_op jit(solution)/shard_map/all_to_all | solution.py:175
  10.2 20.5 %collective-permute-start = (f32[128,256]{1,0:T(8,128)S(1)}, f32[128,256]{1,0:T(8,128)S(1)}, u32[]{:S(2)}, u32[]{:S(2)}) collective-permute-start(f32[128,256]{1,0:T(8,128)S(1)} %pad_maximum_fusion), channel_id=1, source_target_pairs={{0,16},{4,20},{8,24},{12,28},{16,0},{20,4},{24,8},{28,12},{1,17},{... | collective-permute-start | bytes 393224 | tf_op jit(solution)/shard_map/ppermute | solution.py:179
  19.1 31.1 %collective-permute-start.5 = (f32[128,256]{1,0:T(8,128)S(1)}, f32[128,256]{1,0:T(8,128)S(1)}, u32[]{:S(2)}, u32[]{:S(2)}) collective-permute-start(f32[128,256]{1,0:T(8,128)S(1)} %pad_maximum_fusion), channel_id=1, source_target_pairs={{0,32},{32,0},{64,96},{96,64},{128,160},{160,128},{192,224},{224,1... | collective-permute-start | bytes 393224 | tf_op jit(solution)/shard_map/ppermute | solution.py:187
  30.7 19.4 %collective-permute-start.4 = (f32[128,256]{1,0:T(8,128)S(1)}, f32[128,256]{1,0:T(8,128)S(1)}, u32[]{:S(2)}, u32[]{:S(2)}) collective-permute-start(f32[128,256]{1,0:T(8,128)S(1)} %get-tuple-element.25), channel_id=1, source_target_pairs={{0,496},{4,500},{8,504},{12,508},{16,480},{20,484},{24,488},{28,49... | collective-permute-start | bytes 393224 | tf_op jit(solution)/shard_map/ppermute | solution.py:196
  39.6 10.6 %collective-permute-start.1 = (bf16[2,128,256]{2,1,0:T(8,128)(2,1)S(1)}, bf16[2,128,256]{2,1,0:T(8,128)(2,1)S(1)}, u32[]{:S(2)}, u32[]{:S(2)}) collective-permute-start(bf16[2,128,256]{2,1,0:T(8,128)(2,1)S(1)} %pad_maximum_fusion.1.refs_0_), channel_id=1, source_target_pairs={{0,4},{4,0},{8,12},{12,8},{16,20},{20,16},{24,28},{28,24},{1,5},{5... | collective-permute-start | bytes 393224 | tf_op jit(solution)/shard_map/ppermute | solution.py:179
  41.5 12.0 %collective-permute-start.2 = (bf16[2,128,256]{2,1,0:T(8,128)(2,1)S(1)}, bf16[2,128,256]{2,1,0:T(8,128)(2,1)S(1)}, u32[]{:S(2)}, u32[]{:S(2)}) collective-permute-start(bf16[2,128,256]{2,1,0:T(8,128)(2,1)S(1)} %pad_maximum_fusion.1.refs_0_), channel_id=1, source_target_pairs={{0,8},{4,12},{8,0},{12,4},{16,24},{20,28},{24,16},{28,20},{1,9},{5... | collective-permute-start | bytes 393224 | tf_op jit(solution)/shard_map/ppermute | solution.py:179
  48.2 8.0 %collective-permute-start.3 = (bf16[2,128,256]{2,1,0:T(8,128)(2,1)S(1)}, bf16[2,128,256]{2,1,0:T(8,128)(2,1)S(1)}, u32[]{:S(2)}, u32[]{:S(2)}) collective-permute-start(bf16[2,128,256]{2,1,0:T(8,128)(2,1)S(1)} %pad_maximum_fusion.1.refs_0_), channel_id=1, source_target_pairs={{0,12},{4,8},{8,4},{12,0},{16,28},{20,24},{24,20},{28,16},{1,13},{... | collective-permute-start | bytes 393224 | tf_op jit(solution)/shard_map/ppermute | solution.py:179
  81.4 10.4 %collective-permute-start.8 = (bf16[2,128,256]{2,1,0:T(8,128)(2,1)S(1)}, bf16[2,128,256]{2,1,0:T(8,128)(2,1)S(1)}, u32[]{:S(2)}, u32[]{:S(2)}) collective-permute-start(bf16[2,128,256]{2,1,0:T(8,128)(2,1)S(1)} %get-tuple-element.22), channel_id=1, source_target_pairs={{0,12},{4,8},{8,4},{12,0},{16,28},{20,24},{24,20},{28,16},{1,13},{... | collective-permute-start | bytes 393224 | tf_op jit(solution)/shard_map/ppermute | solution.py:179
  87.7 10.4 %collective-permute-start.7 = (bf16[2,128,256]{2,1,0:T(8,128)(2,1)S(1)}, bf16[2,128,256]{2,1,0:T(8,128)(2,1)S(1)}, u32[]{:S(2)}, u32[]{:S(2)}) collective-permute-start(bf16[2,128,256]{2,1,0:T(8,128)(2,1)S(1)} %get-tuple-element.21), channel_id=1, source_target_pairs={{0,8},{4,12},{8,0},{12,4},{16,24},{20,28},{24,16},{28,20},{1,9},{5... | collective-permute-start | bytes 393224 | tf_op jit(solution)/shard_map/ppermute | solution.py:179
  89.6 8.5 %collective-permute-start.6 = (bf16[2,128,256]{2,1,0:T(8,128)(2,1)S(1)}, bf16[2,128,256]{2,1,0:T(8,128)(2,1)S(1)}, u32[]{:S(2)}, u32[]{:S(2)}) collective-permute-start(bf16[2,128,256]{2,1,0:T(8,128)(2,1)S(1)} %get-tuple-element.20), channel_id=1, source_target_pairs={{0,4},{4,0},{8,12},{12,8},{16,20},{20,16},{24,28},{28,24},{1,5},{5... | collective-permute-start | bytes 393224 | tf_op jit(solution)/shard_map/ppermute | solution.py:179
  98.2 18.5 %collective-permute-start.10 = (bf16[2,128,256]{2,1,0:T(8,128)(2,1)S(1)}, bf16[2,128,256]{2,1,0:T(8,128)(2,1)S(1)}, u32[]{:S(2)}, u32[]{:S(2)}) collective-permute-start(bf16[2,128,256]{2,1,0:T(8,128)(2,1)S(1)} %fusion.7), channel_id=1, source_target_pairs={{0,496},{4,500},{8,504},{12,508},{16,480},{20,484},{24,488},{28,49... | collective-permute-start | bytes 393224 | tf_op jit(solution)/shard_map/ppermute | solution.py:196
  111.4 5.3 %collective-permute-start.9 = (bf16[2,128,256]{2,1,0:T(8,128)(2,1)S(1)}, bf16[2,128,256]{2,1,0:T(8,128)(2,1)S(1)}, u32[]{:S(2)}, u32[]{:S(2)}) collective-permute-start(bf16[2,128,256]{2,1,0:T(8,128)(2,1)S(1)} %fusion.7), channel_id=1, source_target_pairs={{0,32},{32,0},{64,96},{96,64},{128,160},{160,128},{192,224},{224,1... | collective-permute-start | bytes 393224 | tf_op jit(solution)/shard_map/ppermute | solution.py:187
  116.8 11.7 %collective-permute-start.11 = (bf16[128,256]{1,0:T(8,128)(2,1)S(1)}, bf16[128,256]{1,0:T(8,128)(2,1)S(1)}, u32[]{:S(2)}, u32[]{:S(2)}) collective-permute-start(bf16[128,256]{1,0:T(8,128)(2,1)S(1)} %fusion.8), channel_id=1, source_target_pairs={{0,16},{4,20},{8,24},{12,28},{16,0},{20,4},{24,8},{28,12},{1,17},{... | collective-permute-start | bytes 196616 | tf_op jit(solution)/shard_map/ppermute | solution.py:179

commit v5 on v4

v5 whole, which is shorter than its diff:
```python
import jax
import jax.numpy as jnp
from jax import lax
from jax.experimental import pallas as pl
from jax.experimental.pallas import tpu as pltpu
from jax.sharding import Mesh
from jax.sharding import PartitionSpec as P

D = 8192
R = 64
TOKENS = 4096
GROUPS = 16
NX = 4
NZ = 8
TOK = TOKENS // (NX * NZ)
OWN = D // (NX * NZ)
QUAD = NZ // 2
FEAT = D // NX

learning_rate = 4.0
epsilon = 1e-05

inv_width = D ** (-0.5)
inv_rank = R ** (-0.5)
step_size = learning_rate / TOKENS**0.5

ROWS = 32
CHUNKS = TOK // ROWS

LAST = (((1,), (1,)), ((), ()))
VMEM_LIMIT = 32 * 1024 * 1024
DIRECT_LIMIT = 60 * 1024 * 1024


def prep_kernel(tok_ref, gain_ref, up_ref, out_ref, raw_ref, done_ref, in_sem, out_sem):
    sources = (up_ref, tok_ref)
    loads = {}
    for c in range(CHUNKS):
        rows = pl.ds(c * ROWS, ROWS)
        for h in range(2):
            loads[c, h] = pltpu.make_async_copy(
                sources[h].at[rows], raw_ref.at[c, h], in_sem.at[c, h]
            )
            loads[c, h].start()
    stores = []
    for c in range(CHUNKS):
        rows = pl.ds(c * ROWS, ROWS)
        for h in range(2):
            loads[c, h].wait()
            if h == 1:
                wide = raw_ref[c, h].astype(jnp.float32)
                scale = lax.rsqrt(jnp.mean(wide * wide, axis=-1, keepdims=True) + epsilon)
            for x in range(NX):
                for z in range(NZ):
                    at = slice((z * NX + x) * OWN, (z * NX + x + 1) * OWN)
                    part = raw_ref[c, h, :, at]
                    if h == 1:
                        part = part.astype(jnp.float32) * scale * gain_ref[:, at]
                    part = part.astype(jnp.bfloat16)
                    done_ref[c, x, h, z] = part
                dst = out_ref.at[x, :, h, rows]
                stores.append(
                    pltpu.make_async_copy(done_ref.at[c, x, h], dst, out_sem.at[c, x, h])
                )
                stores[-1].start()
    for copy in stores:
        copy.wait()


def prep(tokens, gain, upstream):
    return pl.pallas_call(
        prep_kernel,
        in_specs=[
            pl.BlockSpec(memory_space=pl.ANY),
            pl.BlockSpec(memory_space=pltpu.VMEM),
            pl.BlockSpec(memory_space=pl.ANY),
        ],
        out_specs=pl.BlockSpec(memory_space=pl.ANY),
        out_shape=jax.ShapeDtypeStruct((NX, NZ, 2, TOK, OWN), jnp.bfloat16),
        scratch_shapes=[
            pltpu.VMEM((CHUNKS, 2, ROWS, D), jnp.bfloat16),
            pltpu.VMEM((CHUNKS, NX, 2, NZ, ROWS, OWN), jnp.bfloat16),
            pltpu.SemaphoreType.DMA((CHUNKS, 2)),
            pltpu.SemaphoreType.DMA((CHUNKS, NX, 2)),
        ],
        compiler_params=pltpu.CompilerParams(vmem_limit_bytes=DIRECT_LIMIT),
        cost_estimate=pl.CostEstimate(
            flops=6 * TOK * D, bytes_accessed=8 * TOK * D, transcendentals=0
        ),
    )(tokens, gain, upstream)


def project_kernel(feat_ref, *refs):
    low_refs, (out_ref, held_ref, low_ref, sem) = refs[:QUAD], refs[QUAD:]
    loads = []
    for s in range(NX):
        loads.append(pltpu.make_async_copy(feat_ref.at[s], held_ref.at[s], sem.at[s]))
        loads[-1].start()
    me = lax.axis_index("z")
    for near in range(QUAD):
        for far in range(2):
            low_ref[me ^ (near + QUAD * far)] = low_refs[near][far]
    for s in range(NX):
        loads[s].wait()
        for half in range(2):
            rows = slice(half * R, (half + 1) * R)
            part = jnp.zeros((R, TOK), jnp.float32)
            for z in range(NZ):
                part += lax.dot_general(
                    low_ref[z, rows],
                    held_ref[s, z, 1 - half],
                    LAST,
                    preferred_element_type=jnp.float32,
                )
            for x in range(NX):
                out_ref[x, s, rows] = part


def project(feat, lows):
    return pl.pallas_call(
        project_kernel,
        in_specs=[pl.BlockSpec(memory_space=pl.ANY)]
        + [pl.BlockSpec(memory_space=pltpu.VMEM) for _ in lows],
        out_specs=[pl.BlockSpec(memory_space=pltpu.VMEM) for _ in range(2)],
        out_shape=[jax.ShapeDtypeStruct((NX, NX, 2 * R, TOK), jnp.float32), feat],
        scratch_shapes=[
            pltpu.VMEM((NZ, 2 * R, OWN), jnp.bfloat16),
            pltpu.SemaphoreType.DMA((NX,)),
        ],
        compiler_params=pltpu.CompilerParams(vmem_limit_bytes=VMEM_LIMIT),
        cost_estimate=pl.CostEstimate(
            flops=4 * NX * TOK * FEAT * R, bytes_accessed=6 * 1024 * 1024, transcendentals=0
        ),
    )(feat, *lows)


def block_grad(low_ref, feat_ref, piece, half):
    block = feat_ref[:, lax.axis_index("z") ^ piece, 1 - half].reshape(NX * TOK, OWN)
    grad = jnp.dot(low_ref[half], block, preferred_element_type=jnp.float32)
    return grad * (inv_rank if half else inv_width)


SENT = [near + QUAD * far for near in range(1, QUAD) for far in range(2)]
KEPT = [0, QUAD]


def sent_kernel(part_ref, feat_ref, *refs):
    out_refs, low_ref = refs[: QUAD - 1], refs[QUAD - 1]
    for s in range(NX):
        total = part_ref[0, s]
        for x in range(1, NX):
            total = total + part_ref[x, s]
        at = slice(s * TOK, (s + 1) * TOK)
        low_ref[0, :, at] = (total[R:] * inv_rank).astype(jnp.bfloat16)
        low_ref[1, :, at] = (total[:R] * inv_width).astype(jnp.bfloat16)
    for piece in SENT:
        for half in range(2):
            rows = slice(half * R, (half + 1) * R)
            grad = block_grad(low_ref, feat_ref, piece, half).astype(jnp.bfloat16)
            out_refs[piece % QUAD - 1][piece // QUAD, rows] = grad


def kept_kernel(low_ref, feat_ref, out_ref):
    for i, piece in enumerate(KEPT):
        for half in range(2):
            out_ref[i, half * R : (half + 1) * R] = block_grad(low_ref, feat_ref, piece, half)


def grads(kernel, first, feat, pieces, outs):
    return pl.pallas_call(
        kernel,
        in_specs=[pl.BlockSpec(memory_space=pltpu.VMEM) for _ in range(2)],
        out_specs=[pl.BlockSpec(memory_space=pltpu.VMEM) for _ in outs],
        out_shape=outs,
        compiler_params=pltpu.CompilerParams(vmem_limit_bytes=VMEM_LIMIT),
        cost_estimate=pl.CostEstimate(
            flops=4 * NX * TOK * OWN * R * len(pieces),
            bytes_accessed=1024 * 1024 * len(pieces),
            transcendentals=0,
        ),
    )(first, feat)


def exchange(array, axis):
    return lax.all_to_all(array, axis, 0, 0, tiled=True)


def swapped(array, by):
    return lax.ppermute(array, "z", [(i, i ^ by) for i in range(NZ)])


def is_far(group):
    return group % (GROUPS // 2) in (0, GROUPS // 2 - 1)


def first_neighbour(array):
    return lax.ppermute(array, "blk", [(g, g ^ 1) for g in range(GROUPS)])


def second_neighbour(array):
    pairs = []
    for g in range(GROUPS):
        other = (g + 1 if g % 2 else g - 1) % GROUPS
        for z in range(NZ):
            pairs.append((g * NZ + z, other * NZ + (z ^ QUAD if is_far(g) else z)))
    return lax.ppermute(array, ("blk", "z"), pairs)


def local(tokens, norm_gain, adapt_in, adapt_out, upstream):
    wide, narrow = jnp.float32, jnp.bfloat16
    far = ((lax.axis_index("blk") + 1) & (GROUPS // 2 - 1)) < 2

    feat = prep(tokens[0], norm_gain[None], upstream[0])
    feat, adapt_in, adapt_out = lax.optimization_barrier((feat, adapt_in, adapt_out))
    feat = exchange(feat, "x")

    master = jnp.concatenate([adapt_in[0].T, adapt_out[0].T], axis=0)
    opposite = swapped(master, QUAD)
    pair = jnp.stack([master, opposite]).astype(narrow)
    lows = [pair] + [swapped(pair, k) for k in range(1, QUAD)]
    base = second_neighbour(jnp.where(far, opposite, master)) + master + first_neighbour(master)
    feat, lows, base = lax.optimization_barrier((feat, lows, base))

    part, feat = project(feat, lows)
    part = exchange(part, "x")
    piece = jax.ShapeDtypeStruct((2, 2 * R, OWN), narrow)
    lowered = jax.ShapeDtypeStruct((2, R, NX * TOK), narrow)
    *pieces, lowered = grads(sent_kernel, part, feat, SENT, [piece] * (QUAD - 1) + [lowered])
    pieces = [swapped(pieces[k - 1], k) for k in range(1, QUAD)]
    (quad,) = grads(kept_kernel, lowered, feat, KEPT, [jax.ShapeDtypeStruct(piece.shape, wide)])
    for got in pieces:
        quad = quad + got.astype(wide)

    sent = quad.astype(narrow)
    second = second_neighbour(sent).astype(wide)
    second = jnp.where(far, second[::-1], second)
    around = quad + first_neighbour(sent).astype(wide) + second
    total = around[0] + swapped(around[1].astype(narrow), QUAD).astype(wide)
    mixed_in = (base[:R] - step_size * total[:R]) / 3.0
    mixed_out = (base[R:] - step_size * total[R:]) / 3.0
    return (mixed_in.T[None], mixed_out.T[None])


def solution(mesh):
    mesh = Mesh(mesh.devices.reshape(GROUPS, NZ, NX), ("blk", "z", "x"))
    split = P("blk", ("z", "x"), None)
    in_specs = (split, P(), split, split, split)
    return jax.shard_map(
        local, mesh=mesh, in_specs=in_specs, out_specs=(split, split), check_vma=False
    )
```

time: 130 us -> 127 us (0.977)
  the two profiles are of different devices: /device:TPU:25 before, /device:TPU:2 now
where the time goes in v5:
time: 127 us; the launch traced here: 126 us
  starting transfers between devices  76.6 us (60%)
  waiting for transfers between devices  26 us (20%)
  blocking collectives  13.2 us (10%)
  Pallas kernels  8.69 us (7%)
    ppermute x8, starting transfers between devices, swapped(): return lax.ppermute(array, 'z', [(i, i ^ by) for i in range(NZ)])  42.6 us
    ppermute x8, waiting for transfers between devices, swapped(): return lax.ppermute(array, 'z', [(i, i ^ by) for i in range(NZ)])  23.7 us
    ppermute x2, starting transfers between devices, second_neighbour(): return lax.ppermute(array, ('blk', 'z'), pairs)  19.3 us
    all_to_all x1, blocking collectives, exchange(): return lax.all_to_all(array, axis, 0, 0, tiled=True)  13.2 us
    all_to_all x1, starting transfers between devices, exchange(): return lax.all_to_all(array, axis, 0, 0, tiled=True)  10.9 us
    pallas_call x1, Pallas kernels, prep(): pl.pallas_call(prep_kernel, in_specs=[pl.BlockSpec(memory_space=pl.ANY),...  4.53 us
    ppermute x2, starting transfers between devices, first_neighbour(): return lax.ppermute(array, 'blk', [(g, g ^ 1) for g in range(GROUPS)])  3.84 us
    pallas_call x1, Pallas kernels, project(): pl.pallas_call(project_kernel, in_specs=[pl.BlockSpec(memory_space=pl.ANY...  3.18 us
  transfers between devices with their start and end apart: 13, of which 9 were waited for; matrix products, arithmetic and copies ran while one was open for 0% of the time, Pallas kernels for 0%

profile of v5, /device:TPU:2, one launch (start us, length us, event | category | flops | bytes accessed | tf_op | source)
XLA Modules:
  0.0 126.4 jit_solution(11256972241865856128)
XLA Ops:
  0.6 4.5 %shard_map.68 = bf16[4,8,2,128,256]{4,3,2,1,0:T(8,128)(2,1)} custom-call(bf16[128,8192]{1,0:T(8,128)(2,1)} %bitcast.27, f32[1,8192]{1,0:T(1,128)} %bitcast.37, bf16[128,8192]{1,0:T(8,128)(2,1)} %bitcast.28), custom_call_target="tpu_custom_call" | custom-call | flops 6291456 | bytes 8388608 | tf_op jit(solution)/shard_map/pallas_call | solution.py:71
  5.2 0.0 copy-start
  5.2 0.0 copy-start.1
  5.2 10.9 %all-to-all-start = ((bf16[4,8,2,128,256]{4,3,2,1,0:T(8,128)(2,1)}), bf16[4,8,2,128,256]{4,3,2,1,0:T(8,128)(2,1)}, u32[]{:S(2)}, u32[]{:S(2)}) async-start(bf16[4,8,2,128,256]{4,3,2,1,0:T(8,128)(2,1)} %shard_map.68), calls=%async_computation | async-start | bytes 8388608 | tf_op jit(solution)/shard_map/all_to_all | solution.py:185
  16.0 0.0 copy-done
  16.0 0.0 copy-done.1
  16.1 3.7 %collective-permute-start = (f32[128,256]{1,0:T(8,128)S(1)}, f32[128,256]{1,0:T(8,128)S(1)}, u32[]{:S(2)}, u32[]{:S(2)}) collective-permute-start(f32[128,256]{1,0:T(8,128)S(1)} %pad_maximum_fusion), channel_id=1, source_target_pairs={{0,16},{4,20},{8,24},{12,28},{16,0},{20,4},{24,8},{28,12},{1,17},{... | collective-permute-start | bytes 393224 | tf_op jit(solution)/shard_map/ppermute | solution.py:189
  19.8 1.9 %collective-permute-start.5 = (f32[128,256]{1,0:T(8,128)S(1)}, f32[128,256]{1,0:T(8,128)S(1)}, u32[]{:S(2)}, u32[]{:S(2)}) collective-permute-start(f32[128,256]{1,0:T(8,128)S(1)} %pad_maximum_fusion), channel_id=1, source_target_pairs={{0,32},{32,0},{64,96},{96,64},{128,160},{160,128},{192,224},{224,1... | collective-permute-start | bytes 393224 | tf_op jit(solution)/shard_map/ppermute | solution.py:197
  21.7 9.7 %collective-permute-done = f32[128,256]{1,0:T(8,128)S(1)} collective-permute-done((f32[128,256]{1,0:T(8,128)S(1)}, f32[128,256]{1,0:T(8,128)S(1)}, u32[]{:S(2)}, u32[]{:S(2)}) %collective-permute-start) | collective-permute-done | bytes 131104 | tf_op jit(solution)/shard_map/ppermute | solution.py:189
  31.4 9.9 %collective-permute-start.4 = (f32[128,256]{1,0:T(8,128)S(1)}, f32[128,256]{1,0:T(8,128)S(1)}, u32[]{:S(2)}, u32[]{:S(2)}) collective-permute-start(f32[128,256]{1,0:T(8,128)S(1)} %get-tuple-element.34), channel_id=1, source_target_pairs={{0,496},{4,500},{8,504},{12,508},{16,480},{20,484},{24,488},{28,49... | collective-permute-start | bytes 393224 | tf_op jit(solution)/shard_map/ppermute | solution.py:206
  41.4 6.7 %collective-permute-start.3 = (bf16[2,128,256]{2,1,0:T(8,128)(2,1)S(1)}, bf16[2,128,256]{2,1,0:T(8,128)(2,1)S(1)}, u32[]{:S(2)}, u32[]{:S(2)}) collective-permute-start(bf16[2,128,256]{2,1,0:T(8,128)(2,1)S(1)} %pad_maximum_fusion.1.refs_0_), channel_id=1, source_target_pairs={{0,12},{4,8},{8,4},{12,0},{16,28},{20,24},{24,20},{28,16},{1,13},{... | collective-permute-start | bytes 393224 | tf_op jit(solution)/shard_map/ppermute | solution.py:189
  48.1 1.9 %collective-permute-start.2 = (bf16[2,128,256]{2,1,0:T(8,128)(2,1)S(1)}, bf16[2,128,256]{2,1,0:T(8,128)(2,1)S(1)}, u32[]{:S(2)}, u32[]{:S(2)}) collective-permute-start(bf16[2,128,256]{2,1,0:T(8,128)(2,1)S(1)} %pad_maximum_fusion.1.refs_0_), channel_id=1, source_target_pairs={{0,8},{4,12},{8,0},{12,4},{16,24},{20,28},{24,16},{28,20},{1,9},{5... | collective-permute-start | bytes 393224 | tf_op jit(solution)/shard_map/ppermute | solution.py:189
  50.0 2.5 %collective-permute-start.1 = (bf16[2,128,256]{2,1,0:T(8,128)(2,1)S(1)}, bf16[2,128,256]{2,1,0:T(8,128)(2,1)S(1)}, u32[]{:S(2)}, u32[]{:S(2)}) collective-permute-start(bf16[2,128,256]{2,1,0:T(8,128)(2,1)S(1)} %pad_maximum_fusion.1.refs_0_), channel_id=1, source_target_pairs={{0,4},{4,0},{8,12},{12,8},{16,20},{20,16},{24,28},{28,24},{1,5},{5... | collective-permute-start | bytes 393224 | tf_op jit(solution)/shard_map/ppermute | solution.py:189
  52.5 0.0 collective-permute-done.5
  52.5 0.0 collective-permute-done.4
  52.6 0.0 collective-permute-done.3.refs_3_
  52.6 3.3 %collective-permute-done.2.refs_2_ = bf16[2,128,256]{2,1,0:T(8,128)(2,1)S(1)} collective-permute-done((bf16[2,128,256]{2,1,0:T(8,128)(2,1)S(1)}, bf16[2,128,256]{2,1,0:T(8,128)(2,1)S(1)}, u32[]{:S(2)}, u32[]{:S(2)}) %collective-permute-start.2) | collective-permute-done | bytes 131104 | tf_op jit(solution)/shard_map/ppermute | solution.py:189
  55.9 1.4 %collective-permute-done.1.refs_1_ = bf16[2,128,256]{2,1,0:T(8,128)(2,1)S(1)} collective-permute-done((bf16[2,128,256]{2,1,0:T(8,128)(2,1)S(1)}, bf16[2,128,256]{2,1,0:T(8,128)(2,1)S(1)}, u32[]{:S(2)}, u32[]{:S(2)}) %collective-permute-start.1) | collective-permute-done | bytes 131104 | tf_op jit(solution)/shard_map/ppermute | solution.py:189
  57.3 1.0 all-to-all-done.feat_ref
  58.2 3.2 %shard_map.69 = (f32[4,4,128,128]{3,2,1,0:T(8,128)S(1)}, bf16[4,8,2,128,256]{4,3,2,1,0:T(8,128)(2,1)S(1)}) custom-call(bf16[4,8,2,128,256]{4,3,2,1,0:T(8,128)(2,1)} %all-to-all-done.feat_ref, bf16[2,128,256]{2,1,0:T(8,128)(2,1)S(1)} %pad_maximum_fusion.1.refs_0_, bf16[2,128,256]{2,1,0:T(8,128)(2,1)S(1)} %collective-permute-done.1.refs_1_, ...), custom_call_target="tpu_custom_call" | custom-call | flops 268435456 | bytes 6291456 | tf_op jit(solution)/shard_map/pallas_call | solution.py:120
  61.4 13.2 %all_to_all.10.part_ref = f32[4,4,128,128]{3,2,1,0:T(8,128)S(1)} all-to-all(f32[4,4,128,128]{3,2,1,0:T(8,128)S(1)} %get-tuple-element.26), channel_id=1, replica_groups=mesh['blk'=16,'z'=8,'x'=4] {'x'}, dimensions={0} | all-to-all | bytes 2097152 | tf_op jit(solution)/shard_map/all_to_all | solution.py:185
  74.7 0.7 shard_map.70
  75.4 7.7 %collective-permute-start.6 = (bf16[2,128,256]{2,1,0:T(8,128)(2,1)S(1)}, bf16[2,128,256]{2,1,0:T(8,128)(2,1)S(1)}, u32[]{:S(2)}, u32[]{:S(2)}) collective-permute-start(bf16[2,128,256]{2,1,0:T(8,128)(2,1)S(1)} %get-tuple-element.29), channel_id=1, source_target_pairs={{0,4},{4,0},{8,12},{12,8},{16,20},{20,16},{24,28},{28,24},{1,5},{5... | collective-permute-start | bytes 393224 | tf_op jit(solution)/shard_map/ppermute | solution.py:189
  83.0 5.2 %collective-permute-start.7 = (bf16[2,128,256]{2,1,0:T(8,128)(2,1)S(1)}, bf16[2,128,256]{2,1,0:T(8,128)(2,1)S(1)}, u32[]{:S(2)}, u32[]{:S(2)}) collective-permute-start(bf16[2,128,256]{2,1,0:T(8,128)(2,1)S(1)} %get-tuple-element.30), channel_id=1, source_target_pairs={{0,8},{4,12},{8,0},{12,4},{16,24},{20,28},{24,16},{28,20},{1,9},{5... | collective-permute-start | bytes 393224 | tf_op jit(solution)/shard_map/ppermute | solution.py:189
  88.2 1.9 %collective-permute-start.8 = (bf16[2,128,256]{2,1,0:T(8,128)(2,1)S(1)}, bf16[2,128,256]{2,1,0:T(8,128)(2,1)S(1)}, u32[]{:S(2)}, u32[]{:S(2)}) collective-permute-start(bf16[2,128,256]{2,1,0:T(8,128)(2,1)S(1)} %get-tuple-element.31), channel_id=1, source_target_pairs={{0,12},{4,8},{8,4},{12,0},{16,28},{20,24},{24,20},{28,16},{1,13},{... | collective-permute-start | bytes 393224 | tf_op jit(solution)/shard_map/ppermute | solution.py:189
  90.1 0.3 shard_map.71
  90.5 0.0 collective-permute-done.6
  90.5 4.4 %collective-permute-done.7 = bf16[2,128,256]{2,1,0:T(8,128)(2,1)S(1)} collective-permute-done((bf16[2,128,256]{2,1,0:T(8,128)(2,1)S(1)}, bf16[2,128,256]{2,1,0:T(8,128)(2,1)S(1)}, u32[]{:S(2)}, u32[]{:S(2)}) %collective-permute-start.7) | collective-permute-done | bytes 131104 | tf_op jit(solution)/shard_map/ppermute | solution.py:189
  94.9 2.1 %collective-permute-done.8 = bf16[2,128,256]{2,1,0:T(8,128)(2,1)S(1)} collective-permute-done((bf16[2,128,256]{2,1,0:T(8,128)(2,1)S(1)}, bf16[2,128,256]{2,1,0:T(8,128)(2,1)S(1)}, u32[]{:S(2)}, u32[]{:S(2)}) %collective-permute-start.8) | collective-permute-done | bytes 131104 | tf_op jit(solution)/shard_map/ppermute | solution.py:189
  97.0 0.1 fusion.9
  97.0 9.4 %collective-permute-start.10 = (bf16[2,128,256]{2,1,0:T(8,128)(2,1)S(1)}, bf16[2,128,256]{2,1,0:T(8,128)(2,1)S(1)}, u32[]{:S(2)}, u32[]{:S(2)}) collective-permute-start(bf16[2,128,256]{2,1,0:T(8,128)(2,1)S(1)} %fusion.9), channel_id=1, source_target_pairs={{0,496},{4,500},{8,504},{12,508},{16,480},{20,484},{24,488},{28,49... | collective-permute-start | bytes 393224 | tf_op jit(solution)/shard_map/ppermute | solution.py:206
  106.4 1.9 %collective-permute-start.9 = (bf16[2,128,256]{2,1,0:T(8,128)(2,1)S(1)}, bf16[2,128,256]{2,1,0:T(8,128)(2,1)S(1)}, u32[]{:S(2)}, u32[]{:S(2)}) collective-permute-start(bf16[2,128,256]{2,1,0:T(8,128)(2,1)S(1)} %fusion.9), channel_id=1, source_target_pairs={{0,32},{32,0},{64,96},{96,64},{128,160},{160,128},{192,224},{224,1... | collective-permute-start | bytes 393224 | tf_op jit(solution)/shard_map/ppermute | solution.py:197
  108.3 1.1 collective-permute-done.10
  109.5 0.2 collective-permute-done.9
  109.7 0.1 fusion
  109.8 13.0 %collective-permute-start.11 = (bf16[128,256]{1,0:T(8,128)(2,1)S(1)}, bf16[128,256]{1,0:T(8,128)(2,1)S(1)}, u32[]{:S(2)}, u32[]{:S(2)}) collective-permute-start(bf16[128,256]{1,0:T(8,128)(2,1)S(1)} %fusion.2), channel_id=1, source_target_pairs={{0,16},{4,20},{8,24},{12,28},{16,0},{20,4},{24,8},{28,12},{1,17},{... | collective-permute-start | bytes 196616 | tf_op jit(solution)/shard_map/ppermute | solution.py:189
  122.8 2.8 %collective-permute-done.11 = bf16[128,256]{1,0:T(8,128)(2,1)S(1)} collective-permute-done((bf16[128,256]{1,0:T(8,128)(2,1)S(1)}, bf16[128,256]{1,0:T(8,128)(2,1)S(1)}, u32[]{:S(2)}, u32[]{:S(2)}) %collective-permute-start.11) | collective-permute-done | bytes 65568 | tf_op jit(solution)/shard_map/ppermute | solution.py:189
  125.7 0.7 fusion.5
  (8 shorter events, 0.1 us)
Async XLA Ops:
  5.2 10.9 %copy-start = (f32[1,256,64]{1,2,0:T(8,128)S(1)}, f32[1,256,64]{1,2,0:T(8,128)}, u32[]{:S(2)}) copy-start(f32[1,256,64]{1,2,0:T(8,128)} %param.8) | copy-start | bytes 196612
  5.2 10.9 %copy-start.1 = (f32[1,256,64]{1,2,0:T(8,128)S(1)}, f32[1,256,64]{1,2,0:T(8,128)}, u32[]{:S(2)}) copy-start(f32[1,256,64]{1,2,0:T(8,128)} %param.7) | copy-start | bytes 196612
  5.2 53.0 %all-to-all-start = ((bf16[4,8,2,128,256]{4,3,2,1,0:T(8,128)(2,1)}), bf16[4,8,2,128,256]{4,3,2,1,0:T(8,128)(2,1)}, u32[]{:S(2)}, u32[]{:S(2)}) async-start(bf16[4,8,2,128,256]{4,3,2,1,0:T(8,128)(2,1)} %shard_map.68), calls=%async_computation | async-start | bytes 8388608 | tf_op jit(solution)/shard_map/all_to_all | solution.py:185
  16.1 15.4 %collective-permute-start = (f32[128,256]{1,0:T(8,128)S(1)}, f32[128,256]{1,0:T(8,128)S(1)}, u32[]{:S(2)}, u32[]{:S(2)}) collective-permute-start(f32[128,256]{1,0:T(8,128)S(1)} %pad_maximum_fusion), channel_id=1, source_target_pairs={{0,16},{4,20},{8,24},{12,28},{16,0},{20,4},{24,8},{28,12},{1,17},{... | collective-permute-start | bytes 393224 | tf_op jit(solution)/shard_map/ppermute | solution.py:189
  19.8 32.7 %collective-permute-start.5 = (f32[128,256]{1,0:T(8,128)S(1)}, f32[128,256]{1,0:T(8,128)S(1)}, u32[]{:S(2)}, u32[]{:S(2)}) collective-permute-start(f32[128,256]{1,0:T(8,128)S(1)} %pad_maximum_fusion), channel_id=1, source_target_pairs={{0,32},{32,0},{64,96},{96,64},{128,160},{160,128},{192,224},{224,1... | collective-permute-start | bytes 393224 | tf_op jit(solution)/shard_map/ppermute | solution.py:197
  31.4 21.1 %collective-permute-start.4 = (f32[128,256]{1,0:T(8,128)S(1)}, f32[128,256]{1,0:T(8,128)S(1)}, u32[]{:S(2)}, u32[]{:S(2)}) collective-permute-start(f32[128,256]{1,0:T(8,128)S(1)} %get-tuple-element.34), channel_id=1, source_target_pairs={{0,496},{4,500},{8,504},{12,508},{16,480},{20,484},{24,488},{28,49... | collective-permute-start | bytes 393224 | tf_op jit(solution)/shard_map/ppermute | solution.py:206
  41.4 11.2 %collective-permute-start.3 = (bf16[2,128,256]{2,1,0:T(8,128)(2,1)S(1)}, bf16[2,128,256]{2,1,0:T(8,128)(2,1)S(1)}, u32[]{:S(2)}, u32[]{:S(2)}) collective-permute-start(bf16[2,128,256]{2,1,0:T(8,128)(2,1)S(1)} %pad_maximum_fusion.1.refs_0_), channel_id=1, source_target_pairs={{0,12},{4,8},{8,4},{12,0},{16,28},{20,24},{24,20},{28,16},{1,13},{... | collective-permute-start | bytes 393224 | tf_op jit(solution)/shard_map/ppermute | solution.py:189
  48.1 7.8 %collective-permute-start.2 = (bf16[2,128,256]{2,1,0:T(8,128)(2,1)S(1)}, bf16[2,128,256]{2,1,0:T(8,128)(2,1)S(1)}, u32[]{:S(2)}, u32[]{:S(2)}) collective-permute-start(bf16[2,128,256]{2,1,0:T(8,128)(2,1)S(1)} %pad_maximum_fusion.1.refs_0_), channel_id=1, source_target_pairs={{0,8},{4,12},{8,0},{12,4},{16,24},{20,28},{24,16},{28,20},{1,9},{5... | collective-permute-start | bytes 393224 | tf_op jit(solution)/shard_map/ppermute | solution.py:189
  50.0 7.2 %collective-permute-start.1 = (bf16[2,128,256]{2,1,0:T(8,128)(2,1)S(1)}, bf16[2,128,256]{2,1,0:T(8,128)(2,1)S(1)}, u32[]{:S(2)}, u32[]{:S(2)}) collective-permute-start(bf16[2,128,256]{2,1,0:T(8,128)(2,1)S(1)} %pad_maximum_fusion.1.refs_0_), channel_id=1, source_target_pairs={{0,4},{4,0},{8,12},{12,8},{16,20},{20,16},{24,28},{28,24},{1,5},{5... | collective-permute-start | bytes 393224 | tf_op jit(solution)/shard_map/ppermute | solution.py:189
  75.4 15.1 %collective-permute-start.6 = (bf16[2,128,256]{2,1,0:T(8,128)(2,1)S(1)}, bf16[2,128,256]{2,1,0:T(8,128)(2,1)S(1)}, u32[]{:S(2)}, u32[]{:S(2)}) collective-permute-start(bf16[2,128,256]{2,1,0:T(8,128)(2,1)S(1)} %get-tuple-element.29), channel_id=1, source_target_pairs={{0,4},{4,0},{8,12},{12,8},{16,20},{20,16},{24,28},{28,24},{1,5},{5... | collective-permute-start | bytes 393224 | tf_op jit(solution)/shard_map/ppermute | solution.py:189
  83.0 11.9 %collective-permute-start.7 = (bf16[2,128,256]{2,1,0:T(8,128)(2,1)S(1)}, bf16[2,128,256]{2,1,0:T(8,128)(2,1)S(1)}, u32[]{:S(2)}, u32[]{:S(2)}) collective-permute-start(bf16[2,128,256]{2,1,0:T(8,128)(2,1)S(1)} %get-tuple-element.30), channel_id=1, source_target_pairs={{0,8},{4,12},{8,0},{12,4},{16,24},{20,28},{24,16},{28,20},{1,9},{5... | collective-permute-start | bytes 393224 | tf_op jit(solution)/shard_map/ppermute | solution.py:189
  88.2 8.8 %collective-permute-start.8 = (bf16[2,128,256]{2,1,0:T(8,128)(2,1)S(1)}, bf16[2,128,256]{2,1,0:T(8,128)(2,1)S(1)}, u32[]{:S(2)}, u32[]{:S(2)}) collective-permute-start(bf16[2,128,256]{2,1,0:T(8,128)(2,1)S(1)} %get-tuple-element.31), channel_id=1, source_target_pairs={{0,12},{4,8},{8,4},{12,0},{16,28},{20,24},{24,20},{28,16},{1,13},{... | collective-permute-start | bytes 393224 | tf_op jit(solution)/shard_map/ppermute | solution.py:189
  97.0 12.4 %collective-permute-start.10 = (bf16[2,128,256]{2,1,0:T(8,128)(2,1)S(1)}, bf16[2,128,256]{2,1,0:T(8,128)(2,1)S(1)}, u32[]{:S(2)}, u32[]{:S(2)}) collective-permute-start(bf16[2,128,256]{2,1,0:T(8,128)(2,1)S(1)} %fusion.9), channel_id=1, source_target_pairs={{0,496},{4,500},{8,504},{12,508},{16,480},{20,484},{24,488},{28,49... | collective-permute-start | bytes 393224 | tf_op jit(solution)/shard_map/ppermute | solution.py:206
  106.4 3.2 %collective-permute-start.9 = (bf16[2,128,256]{2,1,0:T(8,128)(2,1)S(1)}, bf16[2,128,256]{2,1,0:T(8,128)(2,1)S(1)}, u32[]{:S(2)}, u32[]{:S(2)}) collective-permute-start(bf16[2,128,256]{2,1,0:T(8,128)(2,1)S(1)} %fusion.9), channel_id=1, source_target_pairs={{0,32},{32,0},{64,96},{96,64},{128,160},{160,128},{192,224},{224,1... | collective-permute-start | bytes 393224 | tf_op jit(solution)/shard_map/ppermute | solution.py:197
  109.8 15.9 %collective-permute-start.11 = (bf16[128,256]{1,0:T(8,128)(2,1)S(1)}, bf16[128,256]{1,0:T(8,128)(2,1)S(1)}, u32[]{:S(2)}, u32[]{:S(2)}) collective-permute-start(bf16[128,256]{1,0:T(8,128)(2,1)S(1)} %fusion.2), channel_id=1, source_target_pairs={{0,16},{4,20},{8,24},{12,28},{16,0},{20,4},{24,8},{28,12},{1,17},{... | collective-permute-start | bytes 196616 | tf_op jit(solution)/shard_map/ppermute | solution.py:189

commit v6 on v5

v6 whole, which is shorter than its diff:
```python
import jax
import jax.numpy as jnp
from jax import lax
from jax.experimental import pallas as pl
from jax.experimental.pallas import tpu as pltpu
from jax.sharding import Mesh
from jax.sharding import PartitionSpec as P

D = 8192
R = 64
TOKENS = 4096
GROUPS = 16
NX = 4
NZ = 8
TOK = TOKENS // (NX * NZ)
OWN = D // (NX * NZ)
QUAD = NZ // 2

learning_rate = 4.0
epsilon = 1e-05

inv_width = D ** (-0.5)
inv_rank = R ** (-0.5)
step_size = learning_rate / TOKENS**0.5

ROWS = 32
CHUNKS = TOK // ROWS

LAST = (((1,), (1,)), ((), ()))
VMEM_LIMIT = 32 * 1024 * 1024
DIRECT_LIMIT = 60 * 1024 * 1024


def prep_kernel(tok_ref, gain_ref, up_ref, keep_ref, send_ref, raw_ref, done_ref, in_sem, out_sem):
    sources = (up_ref, tok_ref)
    loads = {}
    for c in range(CHUNKS):
        rows = pl.ds(c * ROWS, ROWS)
        for h in range(2):
            loads[c, h] = pltpu.make_async_copy(
                sources[h].at[rows], raw_ref.at[c, h], in_sem.at[c, h]
            )
            loads[c, h].start()
    me = lax.axis_index("x")
    pair, mate = steps(lax.axis_index("blk"))
    columns = (me, me ^ mate, me ^ pair, me ^ pair ^ mate)
    stores = []
    for c in range(CHUNKS):
        rows = pl.ds(c * ROWS, ROWS)
        for h in range(2):
            loads[c, h].wait()
            if h == 1:
                wide = raw_ref[c, h].astype(jnp.float32)
                scale = lax.rsqrt(jnp.mean(wide * wide, axis=-1, keepdims=True) + epsilon)
            for i, column in enumerate(columns):
                for z in range(NZ):
                    at = pl.ds(pl.multiple_of((z * NX + column) * OWN, OWN), OWN)
                    part = raw_ref[c, h, :, at]
                    if h == 1:
                        part = part.astype(jnp.float32) * scale * gain_ref[:, at]
                    done_ref[c, h, i, z] = part.astype(jnp.bfloat16)
            for i, ref in enumerate((keep_ref, send_ref)):
                src = done_ref.at[c, h, pl.ds(2 * i, 2)]
                stores.append(
                    pltpu.make_async_copy(src, ref.at[:, :, h, rows], out_sem.at[c, h, i])
                )
                stores[-1].start()
    for copy in stores:
        copy.wait()


def prep(tokens, gain, upstream):
    out = jax.ShapeDtypeStruct((2, NZ, 2, TOK, OWN), jnp.bfloat16)
    return pl.pallas_call(
        prep_kernel,
        in_specs=[
            pl.BlockSpec(memory_space=pl.ANY),
            pl.BlockSpec(memory_space=pltpu.VMEM),
            pl.BlockSpec(memory_space=pl.ANY),
        ],
        out_specs=[pl.BlockSpec(memory_space=pl.ANY) for _ in range(2)],
        out_shape=[out, out],
        scratch_shapes=[
            pltpu.VMEM((CHUNKS, 2, ROWS, D), jnp.bfloat16),
            pltpu.VMEM((CHUNKS, 2, 4, NZ, ROWS, OWN), jnp.bfloat16),
            pltpu.SemaphoreType.DMA((CHUNKS, 2)),
            pltpu.SemaphoreType.DMA((CHUNKS, 2, 2)),
        ],
        compiler_params=pltpu.CompilerParams(vmem_limit_bytes=DIRECT_LIMIT),
        cost_estimate=pl.CostEstimate(
            flops=6 * TOK * D, bytes_accessed=8 * TOK * D, transcendentals=0
        ),
    )(tokens, gain, upstream)


def project_kernel(keep_ref, got_ref, *refs):
    piece_refs, (out_ref, held_ref, low_ref, sem) = refs[: 2 * QUAD], refs[2 * QUAD :]
    loads = []
    for t, ref in enumerate((keep_ref, got_ref)):
        loads.append(pltpu.make_async_copy(ref, held_ref.at[t], sem.at[t]))
        loads[-1].start()
    me = lax.axis_index("z")
    for c in range(2):
        for near in range(QUAD):
            for far in range(2):
                low_ref[c, me ^ (near + QUAD * far)] = piece_refs[QUAD * c + near][far]
    for t in range(2):
        loads[t].wait()
        for half in range(2):
            rows = slice(half * R, (half + 1) * R)
            part = jnp.zeros((R, TOK), jnp.float32)
            for c in range(2):
                for z in range(NZ):
                    part += lax.dot_general(
                        low_ref[c, z, rows],
                        held_ref[t, c, z, 1 - half],
                        LAST,
                        preferred_element_type=jnp.float32,
                    )
            out_ref[t, rows] = part


def project(keep, got, lows):
    return pl.pallas_call(
        project_kernel,
        in_specs=[pl.BlockSpec(memory_space=pl.ANY) for _ in range(2)]
        + [pl.BlockSpec(memory_space=pltpu.VMEM) for _ in lows],
        out_specs=[pl.BlockSpec(memory_space=pltpu.VMEM) for _ in range(2)],
        out_shape=[
            jax.ShapeDtypeStruct((2, 2 * R, TOK), jnp.float32),
            jax.ShapeDtypeStruct((2,) + keep.shape, keep.dtype),
        ],
        scratch_shapes=[
            pltpu.VMEM((2, NZ, 2 * R, OWN), jnp.bfloat16),
            pltpu.SemaphoreType.DMA((2,)),
        ],
        compiler_params=pltpu.CompilerParams(vmem_limit_bytes=VMEM_LIMIT),
        cost_estimate=pl.CostEstimate(
            flops=8 * TOK * D * R, bytes_accessed=6 * 1024 * 1024, transcendentals=0
        ),
    )(keep, got, *lows)


EARLY, LATE = (3, 2), (1, 0)


def column_grads(low_ref, feat_ref, out_refs, column):
    me = lax.axis_index("z")
    for nears, out_ref in zip((EARLY, LATE), out_refs, strict=True):
        for i, near in enumerate(nears):
            for far in range(2):
                for half, scale in enumerate((inv_width, inv_rank)):
                    block = feat_ref[:, column, me ^ (near + QUAD * far), 1 - half]
                    block = block.reshape(2 * TOK, OWN)
                    grad = jnp.dot(low_ref[half], block, preferred_element_type=jnp.float32)
                    rows = slice(half * R, (half + 1) * R)
                    out_ref[i, far, rows] = (grad * scale).astype(out_ref.dtype)


def other_kernel(part_ref, got_ref, feat_ref, early_ref, late_ref, low_ref):
    for t in range(2):
        total = part_ref[t] + got_ref[1 - t]
        at = slice(t * TOK, (t + 1) * TOK)
        low_ref[0, :, at] = (total[R:] * inv_rank).astype(jnp.bfloat16)
        low_ref[1, :, at] = (total[:R] * inv_width).astype(jnp.bfloat16)
    column_grads(low_ref, feat_ref, (early_ref, late_ref), 1)


def own_kernel(low_ref, feat_ref, early_ref, late_ref):
    column_grads(low_ref, feat_ref, (early_ref, late_ref), 0)


def early_kernel(own_ref, got_ref, first_ref, second_ref):
    for i, ref in enumerate((first_ref, second_ref)):
        ref[...] = (own_ref[i] + got_ref[i].astype(jnp.float32)).astype(ref.dtype)


def late_kernel(master_ref, own_ref, got_ref, sent_ref, kept_ref):
    sent_ref[...] = (own_ref[0] + got_ref[0].astype(jnp.float32)).astype(sent_ref.dtype)
    kept_ref[0] = own_ref[1, 0] + got_ref[1, 0].astype(jnp.float32) - master_ref[...] / step_size
    kept_ref[1] = own_ref[1, 1] + got_ref[1, 1].astype(jnp.float32)


def small(kernel, outs, *args):
    return pl.pallas_call(
        kernel,
        in_specs=[pl.BlockSpec(memory_space=pltpu.VMEM) for _ in args],
        out_specs=[pl.BlockSpec(memory_space=pltpu.VMEM) for _ in outs],
        out_shape=outs,
        compiler_params=pltpu.CompilerParams(vmem_limit_bytes=VMEM_LIMIT),
        cost_estimate=pl.CostEstimate(
            flops=2 * TOK * D * R, bytes_accessed=1024 * 1024, transcendentals=0
        ),
    )(*args)


def steps(group):
    odd = group % 2
    return 1 + 2 * odd, 3 - 2 * odd


def along_x(array, which):
    pairs = []
    for g in range(GROUPS):
        for x in range(NX):
            pairs.append((g * NX + x, g * NX + (x ^ steps(g)[which])))
    return lax.ppermute(array, ("blk", "x"), pairs)


def swapped(array, by):
    return lax.ppermute(array, "z", [(i, i ^ by) for i in range(NZ)])


def is_far(group):
    return group % (GROUPS // 2) in (0, GROUPS // 2 - 1)


def first_neighbour(array):
    return lax.ppermute(array, "blk", [(g, g ^ 1) for g in range(GROUPS)])


def second_neighbour(array):
    pairs = []
    for g in range(GROUPS):
        other = (g + 1 if g % 2 else g - 1) % GROUPS
        for z in range(NZ):
            pairs.append((g * NZ + z, other * NZ + (z ^ QUAD if is_far(g) else z)))
    return lax.ppermute(array, ("blk", "z"), pairs)


def local(tokens, norm_gain, adapt_in, adapt_out, upstream):
    wide, narrow = jnp.float32, jnp.bfloat16
    far = ((lax.axis_index("blk") + 1) & (GROUPS // 2 - 1)) < 2

    master = jnp.concatenate([adapt_in[0].T, adapt_out[0].T], axis=0)
    own = master.astype(narrow)
    pair = jnp.stack([own, swapped(own, QUAD)])
    lows = [pair] + [swapped(pair, k) for k in range(1, QUAD)]
    lows += [along_x(low, 1) for low in lows]

    keep, send = prep(tokens[0], norm_gain[None], upstream[0])
    got = along_x(send, 0)
    part, feat = project(keep, got, lows)
    part_got = along_x(part, 0)

    narrow_pieces = jax.ShapeDtypeStruct((2, 2, 2 * R, OWN), narrow)
    wide_pieces = jax.ShapeDtypeStruct(narrow_pieces.shape, wide)
    lowered = jax.ShapeDtypeStruct((2, R, 2 * TOK), narrow)
    *theirs, lowered = small(
        other_kernel, [narrow_pieces, narrow_pieces, lowered], part, part_got, feat
    )
    theirs = [along_x(pieces, 1) for pieces in theirs]
    mine = small(own_kernel, [wide_pieces, wide_pieces], lowered, feat)
    piece = jax.ShapeDtypeStruct((2, 2 * R, OWN), narrow)
    kept = jax.ShapeDtypeStruct(piece.shape, wide)
    sent = small(early_kernel, [piece, piece], mine[0], theirs[0])
    early = [swapped(array, near) for array, near in zip(sent, EARLY, strict=True)]
    sent, quad = small(late_kernel, [piece, kept], master, mine[1], theirs[1])
    for got in early + [swapped(sent, LATE[0])]:
        quad = quad + got.astype(wide)

    sent = quad.astype(narrow)
    second = second_neighbour(sent).astype(wide)
    second = jnp.where(far, second[::-1], second)
    around = quad + first_neighbour(sent).astype(wide) + second
    total = around[0] + swapped(around[1].astype(narrow), QUAD).astype(wide)
    mixed = [total[half * R : (half + 1) * R] * (-step_size / 3.0) for half in range(2)]
    return (mixed[0].T[None], mixed[1].T[None])


def solution(mesh):
    mesh = Mesh(mesh.devices.reshape(GROUPS, NZ, NX), ("blk", "z", "x"))
    split = P("blk", ("z", "x"), None)
    in_specs = (split, P(), split, split, split)
    return jax.shard_map(
        local, mesh=mesh, in_specs=in_specs, out_specs=(split, split), check_vma=False
    )
```

time: 127 us -> 118 us (0.929)
  the two profiles are of different devices: /device:TPU:2 before, /device:TPU:25 now
where the time goes in v6:
time: 118 us; the launch traced here: 117 us
  starting transfers between devices  80.1 us (68%)
  waiting for transfers between devices  25.7 us (22%)
  Pallas kernels  7.56 us (6%)
  local copies, waits for them, and re-layouts  1.61 us (1%)
    ppermute x8, starting transfers between devices, swapped(): return lax.ppermute(array, 'z', [(i, i ^ by) for i in range(NZ)])  36.9 us
    ppermute x8, starting transfers between devices, along_x(): return lax.ppermute(array, ('blk', 'x'), pairs)  22.6 us
    ppermute x1, starting transfers between devices, second_neighbour(): return lax.ppermute(array, ('blk', 'z'), pairs)  18.7 us
    ppermute x8, waiting for transfers between devices, swapped(): return lax.ppermute(array, 'z', [(i, i ^ by) for i in range(NZ)])  11.7 us
    ppermute x8, waiting for transfers between devices, along_x(): return lax.ppermute(array, ('blk', 'x'), pairs)  9.88 us
    pallas_call x1, Pallas kernels, prep(): pl.pallas_call(prep_kernel, in_specs=[pl.BlockSpec(memory_space=pl.ANY),...  4.45 us
    ppermute x1, waiting for transfers between devices, second_neighbour(): return lax.ppermute(array, ('blk', 'z'), pairs)  4.17 us
  transfers between devices with their start and end apart: 18, of which 9 were waited for; matrix products, arithmetic and copies ran while one was open for 0% of the time, Pallas kernels for 1%

profile of v6, /device:TPU:25, one launch (start us, length us, event | category | flops | bytes accessed | tf_op | source)
XLA Modules:
  0.0 116.9 jit_solution(1723846670277871896)
XLA Ops:
  0.6 0.0 copy-start.1
  0.6 0.0 copy-start.2
  0.7 4.5 %shard_map.68 = (bf16[2,8,2,128,256]{4,3,2,1,0:T(8,128)(2,1)}, bf16[2,8,2,128,256]{4,3,2,1,0:T(8,128)(2,1)}) custom-call(bf16[128,8192]{1,0:T(8,128)(2,1)} %bitcast.30, f32[1,8192]{1,0:T(1,128)} %bitcast.37, bf16[128,8192]{1,0:T(8,128)(2,1)} %bitcast.31), custom_call_target="tpu_custom_call" | custom-call | flops 6291456 | bytes 8388608 | tf_op jit(solution)/shard_map/pallas_call | solution.py:74
  5.1 4.4 %collective-permute-start = (bf16[2,8,2,128,256]{4,3,2,1,0:T(8,128)(2,1)}, bf16[2,8,2,128,256]{4,3,2,1,0:T(8,128)(2,1)S(1)}, u32[]{:S(2)}, u32[]{:S(2)}) collective-permute-start(bf16[2,8,2,128,256]{4,3,2,1,0:T(8,128)(2,1)} %get-tuple-element.16), channel_id=1, source_target_pairs={{0,1},{1,0},{2,3},{3,2},{32,35},{33,34},{34,33},{35,32},{64,65},{6... | collective-permute-start | bytes 6291464 | tf_op jit(solution)/shard_map/ppermute | solution.py:207
  9.5 0.0 copy-done.1
  9.5 0.0 copy-done.2
  9.5 8.8 %collective-permute-start.1 = (bf16[128,256]{1,0:T(8,128)(2,1)S(1)}, bf16[128,256]{1,0:T(8,128)(2,1)S(1)}, u32[]{:S(2)}, u32[]{:S(2)}) collective-permute-start(bf16[128,256]{1,0:T(8,128)(2,1)S(1)} %fusion.6), channel_id=1, source_target_pairs={{0,16},{4,20},{8,24},{12,28},{16,0},{20,4},{24,8},{28,12},{1,17},{... | collective-permute-start | bytes 196616 | tf_op jit(solution)/shard_map/ppermute | solution.py:211
  18.4 2.3 %collective-permute-done.1 = bf16[128,256]{1,0:T(8,128)(2,1)S(1)} collective-permute-done((bf16[128,256]{1,0:T(8,128)(2,1)S(1)}, bf16[128,256]{1,0:T(8,128)(2,1)S(1)}, u32[]{:S(2)}, u32[]{:S(2)}) %collective-permute-start.1) | collective-permute-done | bytes 65568 | tf_op jit(solution)/shard_map/ppermute | solution.py:211
  20.7 4.1 %collective-permute-start.2 = (bf16[2,128,256]{2,1,0:T(8,128)(2,1)S(1)}, bf16[2,128,256]{2,1,0:T(8,128)(2,1)S(1)}, u32[]{:S(2)}, u32[]{:S(2)}) collective-permute-start(bf16[2,128,256]{2,1,0:T(8,128)(2,1)S(1)} %pad_maximum_fusion.1.refs_0_), channel_id=1, source_target_pairs={{0,4},{4,0},{8,12},{12,8},{16,20},{20,16},{24,28},{28,24},{1,5},{5... | collective-permute-start | bytes 393224 | tf_op jit(solution)/shard_map/ppermute | solution.py:211
  24.8 6.6 %collective-permute-start.3 = (bf16[2,128,256]{2,1,0:T(8,128)(2,1)S(1)}, bf16[2,128,256]{2,1,0:T(8,128)(2,1)S(1)}, u32[]{:S(2)}, u32[]{:S(2)}) collective-permute-start(bf16[2,128,256]{2,1,0:T(8,128)(2,1)S(1)} %pad_maximum_fusion.1.refs_0_), channel_id=1, source_target_pairs={{0,8},{4,12},{8,0},{12,4},{16,24},{20,28},{24,16},{28,20},{1,9},{5... | collective-permute-start | bytes 393224 | tf_op jit(solution)/shard_map/ppermute | solution.py:211
  31.4 1.9 %collective-permute-start.4 = (bf16[2,128,256]{2,1,0:T(8,128)(2,1)S(1)}, bf16[2,128,256]{2,1,0:T(8,128)(2,1)S(1)}, u32[]{:S(2)}, u32[]{:S(2)}) collective-permute-start(bf16[2,128,256]{2,1,0:T(8,128)(2,1)S(1)} %pad_maximum_fusion.1.refs_0_), channel_id=1, source_target_pairs={{0,12},{4,8},{8,4},{12,0},{16,28},{20,24},{24,20},{28,16},{1,13},{... | collective-permute-start | bytes 393224 | tf_op jit(solution)/shard_map/ppermute | solution.py:211
  33.4 1.9 %collective-permute-start.5 = (bf16[2,128,256]{2,1,0:T(8,128)(2,1)S(1)}, bf16[2,128,256]{2,1,0:T(8,128)(2,1)S(1)}, u32[]{:S(2)}, u32[]{:S(2)}) collective-permute-start(bf16[2,128,256]{2,1,0:T(8,128)(2,1)S(1)} %pad_maximum_fusion.1.refs_0_), channel_id=1, source_target_pairs={{0,3},{1,2},{2,1},{3,0},{32,33},{33,32},{34,35},{35,34},{64,67},{6... | collective-permute-start | bytes 393224 | tf_op jit(solution)/shard_map/ppermute | solution.py:207
  35.3 0.0 collective-permute-done.2.refs_1_
  35.3 3.4 %collective-permute-start.6 = (bf16[2,128,256]{2,1,0:T(8,128)(2,1)S(1)}, bf16[2,128,256]{2,1,0:T(8,128)(2,1)S(1)}, u32[]{:S(2)}, u32[]{:S(2)}) collective-permute-start(bf16[2,128,256]{2,1,0:T(8,128)(2,1)S(1)} %collective-permute-done.2.refs_1_), channel_id=1, source_target_pairs={{0,3},{1,2},{2,1},{3,0},{32,33},{33,32},{34,35},{35,34},{64,67},{6... | collective-permute-start | bytes 393224 | tf_op jit(solution)/shard_map/ppermute | solution.py:207
  38.7 0.0 collective-permute-done.3.refs_2_
  38.7 1.9 %collective-permute-start.7 = (bf16[2,128,256]{2,1,0:T(8,128)(2,1)S(1)}, bf16[2,128,256]{2,1,0:T(8,128)(2,1)S(1)}, u32[]{:S(2)}, u32[]{:S(2)}) collective-permute-start(bf16[2,128,256]{2,1,0:T(8,128)(2,1)S(1)} %collective-permute-done.3.refs_2_), channel_id=1, source_target_pairs={{0,3},{1,2},{2,1},{3,0},{32,33},{33,32},{34,35},{35,34},{64,67},{6... | collective-permute-start | bytes 393224 | tf_op jit(solution)/shard_map/ppermute | solution.py:207
  40.6 0.0 collective-permute-done.4.refs_3_
  40.6 3.4 %collective-permute-start.8 = (bf16[2,128,256]{2,1,0:T(8,128)(2,1)S(1)}, bf16[2,128,256]{2,1,0:T(8,128)(2,1)S(1)}, u32[]{:S(2)}, u32[]{:S(2)}) collective-permute-start(bf16[2,128,256]{2,1,0:T(8,128)(2,1)S(1)} %collective-permute-done.4.refs_3_), channel_id=1, source_target_pairs={{0,3},{1,2},{2,1},{3,0},{32,33},{33,32},{34,35},{35,34},{64,67},{6... | collective-permute-start | bytes 393224 | tf_op jit(solution)/shard_map/ppermute | solution.py:207
  44.0 0.0 collective-permute-done.5.refs_4_
  44.0 0.0 collective-permute-done.6.refs_5_
  44.0 0.4 collective-permute-done.7.refs_6_
  44.4 2.2 %collective-permute-done.8.refs_7_ = bf16[2,128,256]{2,1,0:T(8,128)(2,1)S(1)} collective-permute-done((bf16[2,128,256]{2,1,0:T(8,128)(2,1)S(1)}, bf16[2,128,256]{2,1,0:T(8,128)(2,1)S(1)}, u32[]{:S(2)}, u32[]{:S(2)}) %collective-permute-start.8) | collective-permute-done | bytes 131104 | tf_op jit(solution)/shard_map/ppermute | solution.py:207
  46.6 0.0 collective-permute-done.got_ref
  46.6 0.0 copy-start
  46.6 1.6 %copy-done = bf16[2,8,2,128,256]{4,3,2,1,0:T(8,128)(2,1)S(1)} copy-done((bf16[2,8,2,128,256]{4,3,2,1,0:T(8,128)(2,1)S(1)}, bf16[2,8,2,128,256]{4,3,2,1,0:T(8,128)(2,1)}, u32[]{:S(2)}) %copy-start) | copy-done | bytes 2097176
  48.2 2.0 %shard_map.69 = (f32[2,128,128]{2,1,0:T(8,128)S(1)}, bf16[2,2,8,2,128,256]{5,4,3,2,1,0:T(8,128)(2,1)S(1)}) custom-call(bf16[2,8,2,128,256]{4,3,2,1,0:T(8,128)(2,1)S(1)} %copy-done, bf16[2,8,2,128,256]{4,3,2,1,0:T(8,128)(2,1)S(1)} %collective-permute-done.got_ref, bf16[2,128,256]{2,1,0:T(8,128)(2,1)S(1)} %pad_maximum_fusion.1.refs_0_, ...), custom_call_target="tpu_custom_call" | custom-call | flops 536870912 | bytes 6291456 | tf_op jit(solution)/shard_map/pallas_call | solution.py:124
  50.2 2.3 %collective-permute-start.9 = (f32[2,128,128]{2,1,0:T(8,128)S(1)}, f32[2,128,128]{2,1,0:T(8,128)S(1)}, u32[]{:S(2)}, u32[]{:S(2)}) collective-permute-start(f32[2,128,128]{2,1,0:T(8,128)S(1)} %get-tuple-element.17.part_ref), channel_id=1, source_target_pairs={{0,1},{1,0},{2,3},{3,2},{32,35},{33,34},{34,33},{35,32},{64,65},{6... | collective-permute-start | bytes 393224 | tf_op jit(solution)/shard_map/ppermute | solution.py:207
  52.6 4.6 %collective-permute-done.9.got_ref = f32[2,128,128]{2,1,0:T(8,128)S(1)} collective-permute-done((f32[2,128,128]{2,1,0:T(8,128)S(1)}, f32[2,128,128]{2,1,0:T(8,128)S(1)}, u32[]{:S(2)}, u32[]{:S(2)}) %collective-permute-start.9) | collective-permute-done | bytes 131104 | tf_op jit(solution)/shard_map/ppermute | solution.py:207
  57.1 0.5 shard_map.70
  57.6 2.2 %collective-permute-start.11 = (bf16[2,2,128,256]{3,2,1,0:T(8,128)(2,1)S(1)}, bf16[2,2,128,256]{3,2,1,0:T(8,128)(2,1)S(1)}, u32[]{:S(2)}, u32[]{:S(2)}) collective-permute-start(bf16[2,2,128,256]{3,2,1,0:T(8,128)(2,1)S(1)} %get-tuple-element.24), channel_id=1, source_target_pairs={{0,3},{1,2},{2,1},{3,0},{32,33},{33,32},{34,35},{35,34},{64,67},{6... | collective-permute-start | bytes 786440 | tf_op jit(solution)/shard_map/ppermute | solution.py:207
  59.8 3.1 %collective-permute-start.10 = (bf16[2,2,128,256]{3,2,1,0:T(8,128)(2,1)S(1)}, bf16[2,2,128,256]{3,2,1,0:T(8,128)(2,1)S(1)}, u32[]{:S(2)}, u32[]{:S(2)}) collective-permute-start(bf16[2,2,128,256]{3,2,1,0:T(8,128)(2,1)S(1)} %get-tuple-element.21), channel_id=1, source_target_pairs={{0,3},{1,2},{2,1},{3,0},{32,33},{33,32},{34,35},{35,34},{64,67},{6... | collective-permute-start | bytes 786440 | tf_op jit(solution)/shard_map/ppermute | solution.py:207
  63.0 0.5 shard_map.71
  63.5 2.7 %collective-permute-done.11.got_ref = bf16[2,2,128,256]{3,2,1,0:T(8,128)(2,1)S(1)} collective-permute-done((bf16[2,2,128,256]{3,2,1,0:T(8,128)(2,1)S(1)}, bf16[2,2,128,256]{3,2,1,0:T(8,128)(2,1)S(1)}, u32[]{:S(2)}, u32[]{:S(2)}) %collective-permute-start.11) | collective-permute-done | bytes 262176 | tf_op jit(solution)/shard_map/ppermute | solution.py:207
  66.2 3.9 %collective-permute-start.12 = (bf16[2,128,256]{2,1,0:T(8,128)(2,1)S(1)}, bf16[2,128,256]{2,1,0:T(8,128)(2,1)S(1)}, u32[]{:S(2)}, u32[]{:S(2)}) collective-permute-start(bf16[2,128,256]{2,1,0:T(8,128)(2,1)S(1)} %get-tuple-element.25), channel_id=1, source_target_pairs={{0,12},{4,8},{8,4},{12,0},{16,28},{20,24},{24,20},{28,16},{1,13},{... | collective-permute-start | bytes 393224 | tf_op jit(solution)/shard_map/ppermute | solution.py:211
  70.1 2.6 %collective-permute-start.13 = (bf16[2,128,256]{2,1,0:T(8,128)(2,1)S(1)}, bf16[2,128,256]{2,1,0:T(8,128)(2,1)S(1)}, u32[]{:S(2)}, u32[]{:S(2)}) collective-permute-start(bf16[2,128,256]{2,1,0:T(8,128)(2,1)S(1)} %get-tuple-element.26), channel_id=1, source_target_pairs={{0,8},{4,12},{8,0},{12,4},{16,24},{20,28},{24,16},{28,20},{1,9},{5... | collective-permute-start | bytes 393224 | tf_op jit(solution)/shard_map/ppermute | solution.py:211
  72.8 0.0 collective-permute-done.10.got_ref
  72.8 0.1 shard_map.72
  72.8 2.8 %collective-permute-start.14 = (bf16[2,128,256]{2,1,0:T(8,128)(2,1)S(1)}, bf16[2,128,256]{2,1,0:T(8,128)(2,1)S(1)}, u32[]{:S(2)}, u32[]{:S(2)}) collective-permute-start(bf16[2,128,256]{2,1,0:T(8,128)(2,1)S(1)} %get-tuple-element.27), channel_id=1, source_target_pairs={{0,4},{4,0},{8,12},{12,8},{16,20},{20,16},{24,28},{28,24},{1,5},{5... | collective-permute-start | bytes 393224 | tf_op jit(solution)/shard_map/ppermute | solution.py:211
  75.6 0.0 collective-permute-done.12
  75.6 2.9 %collective-permute-done.13 = bf16[2,128,256]{2,1,0:T(8,128)(2,1)S(1)} collective-permute-done((bf16[2,128,256]{2,1,0:T(8,128)(2,1)S(1)}, bf16[2,128,256]{2,1,0:T(8,128)(2,1)S(1)}, u32[]{:S(2)}, u32[]{:S(2)}) %collective-permute-start.13) | collective-permute-done | bytes 131104 | tf_op jit(solution)/shard_map/ppermute | solution.py:211
  78.5 1.0 collective-permute-done.14
  79.6 0.1 fusion.5
  79.6 18.7 %collective-permute-start.16 = (bf16[2,128,256]{2,1,0:T(8,128)(2,1)S(1)}, bf16[2,128,256]{2,1,0:T(8,128)(2,1)S(1)}, u32[]{:S(2)}, u32[]{:S(2)}) collective-permute-start(bf16[2,128,256]{2,1,0:T(8,128)(2,1)S(1)} %fusion.5), channel_id=1, source_target_pairs={{0,496},{4,500},{8,504},{12,508},{16,480},{20,484},{24,488},{28,49... | collective-permute-start | bytes 393224 | tf_op jit(solution)/shard_map/ppermute | solution.py:228
  98.3 1.9 %collective-permute-start.15 = (bf16[2,128,256]{2,1,0:T(8,128)(2,1)S(1)}, bf16[2,128,256]{2,1,0:T(8,128)(2,1)S(1)}, u32[]{:S(2)}, u32[]{:S(2)}) collective-permute-start(bf16[2,128,256]{2,1,0:T(8,128)(2,1)S(1)} %fusion.5), channel_id=1, source_target_pairs={{0,32},{32,0},{64,96},{96,64},{128,160},{160,128},{192,224},{224,1... | collective-permute-start | bytes 393224 | tf_op jit(solution)/shard_map/ppermute | solution.py:219
  100.2 4.2 %collective-permute-done.16 = bf16[2,128,256]{2,1,0:T(8,128)(2,1)S(1)} collective-permute-done((bf16[2,128,256]{2,1,0:T(8,128)(2,1)S(1)}, bf16[2,128,256]{2,1,0:T(8,128)(2,1)S(1)}, u32[]{:S(2)}, u32[]{:S(2)}) %collective-permute-start.16) | collective-permute-done | bytes 131104 | tf_op jit(solution)/shard_map/ppermute | solution.py:228
  104.4 0.0 collective-permute-done.15
  104.4 0.1 fusion
  104.6 6.3 %collective-permute-start.17 = (bf16[128,256]{1,0:T(8,128)(2,1)S(1)}, bf16[128,256]{1,0:T(8,128)(2,1)S(1)}, u32[]{:S(2)}, u32[]{:S(2)}) collective-permute-start(bf16[128,256]{1,0:T(8,128)(2,1)S(1)} %fusion.2), channel_id=1, source_target_pairs={{0,16},{4,20},{8,24},{12,28},{16,0},{20,4},{24,8},{28,12},{1,17},{... | collective-permute-start | bytes 196616 | tf_op jit(solution)/shard_map/ppermute | solution.py:211
  110.8 5.4 %collective-permute-done.17 = bf16[128,256]{1,0:T(8,128)(2,1)S(1)} collective-permute-done((bf16[128,256]{1,0:T(8,128)(2,1)S(1)}, bf16[128,256]{1,0:T(8,128)(2,1)S(1)}, u32[]{:S(2)}, u32[]{:S(2)}) %collective-permute-start.17) | collective-permute-done | bytes 65568 | tf_op jit(solution)/shard_map/ppermute | solution.py:211
  116.2 0.7 fusion.3
  (8 shorter events, 0.1 us)
Async XLA Ops:
  0.6 8.9 %copy-start.1 = (f32[1,256,64]{1,2,0:T(8,128)S(1)}, f32[1,256,64]{1,2,0:T(8,128)}, u32[]{:S(2)}) copy-start(f32[1,256,64]{1,2,0:T(8,128)} %param.8) | copy-start | bytes 196612
  0.6 8.9 %copy-start.2 = (f32[1,256,64]{1,2,0:T(8,128)S(1)}, f32[1,256,64]{1,2,0:T(8,128)}, u32[]{:S(2)}) copy-start(f32[1,256,64]{1,2,0:T(8,128)} %param.7) | copy-start | bytes 196612
  5.1 41.5 %collective-permute-start = (bf16[2,8,2,128,256]{4,3,2,1,0:T(8,128)(2,1)}, bf16[2,8,2,128,256]{4,3,2,1,0:T(8,128)(2,1)S(1)}, u32[]{:S(2)}, u32[]{:S(2)}) collective-permute-start(bf16[2,8,2,128,256]{4,3,2,1,0:T(8,128)(2,1)} %get-tuple-element.16), channel_id=1, source_target_pairs={{0,1},{1,0},{2,3},{3,2},{32,35},{33,34},{34,33},{35,32},{64,65},{6... | collective-permute-start | bytes 6291464 | tf_op jit(solution)/shard_map/ppermute | solution.py:207
  9.5 11.2 %collective-permute-start.1 = (bf16[128,256]{1,0:T(8,128)(2,1)S(1)}, bf16[128,256]{1,0:T(8,128)(2,1)S(1)}, u32[]{:S(2)}, u32[]{:S(2)}) collective-permute-start(bf16[128,256]{1,0:T(8,128)(2,1)S(1)} %fusion.6), channel_id=1, source_target_pairs={{0,16},{4,20},{8,24},{12,28},{16,0},{20,4},{24,8},{28,12},{1,17},{... | collective-permute-start | bytes 196616 | tf_op jit(solution)/shard_map/ppermute | solution.py:211
  20.7 14.5 %collective-permute-start.2 = (bf16[2,128,256]{2,1,0:T(8,128)(2,1)S(1)}, bf16[2,128,256]{2,1,0:T(8,128)(2,1)S(1)}, u32[]{:S(2)}, u32[]{:S(2)}) collective-permute-start(bf16[2,128,256]{2,1,0:T(8,128)(2,1)S(1)} %pad_maximum_fusion.1.refs_0_), channel_id=1, source_target_pairs={{0,4},{4,0},{8,12},{12,8},{16,20},{20,16},{24,28},{28,24},{1,5},{5... | collective-permute-start | bytes 393224 | tf_op jit(solution)/shard_map/ppermute | solution.py:211
  24.8 13.9 %collective-permute-start.3 = (bf16[2,128,256]{2,1,0:T(8,128)(2,1)S(1)}, bf16[2,128,256]{2,1,0:T(8,128)(2,1)S(1)}, u32[]{:S(2)}, u32[]{:S(2)}) collective-permute-start(bf16[2,128,256]{2,1,0:T(8,128)(2,1)S(1)} %pad_maximum_fusion.1.refs_0_), channel_id=1, source_target_pairs={{0,8},{4,12},{8,0},{12,4},{16,24},{20,28},{24,16},{28,20},{1,9},{5... | collective-permute-start | bytes 393224 | tf_op jit(solution)/shard_map/ppermute | solution.py:211
  31.4 9.2 %collective-permute-start.4 = (bf16[2,128,256]{2,1,0:T(8,128)(2,1)S(1)}, bf16[2,128,256]{2,1,0:T(8,128)(2,1)S(1)}, u32[]{:S(2)}, u32[]{:S(2)}) collective-permute-start(bf16[2,128,256]{2,1,0:T(8,128)(2,1)S(1)} %pad_maximum_fusion.1.refs_0_), channel_id=1, source_target_pairs={{0,12},{4,8},{8,4},{12,0},{16,28},{20,24},{24,20},{28,16},{1,13},{... | collective-permute-start | bytes 393224 | tf_op jit(solution)/shard_map/ppermute | solution.py:211
  33.4 10.6 %collective-permute-start.5 = (bf16[2,128,256]{2,1,0:T(8,128)(2,1)S(1)}, bf16[2,128,256]{2,1,0:T(8,128)(2,1)S(1)}, u32[]{:S(2)}, u32[]{:S(2)}) collective-permute-start(bf16[2,128,256]{2,1,0:T(8,128)(2,1)S(1)} %pad_maximum_fusion.1.refs_0_), channel_id=1, source_target_pairs={{0,3},{1,2},{2,1},{3,0},{32,33},{33,32},{34,35},{35,34},{64,67},{6... | collective-permute-start | bytes 393224 | tf_op jit(solution)/shard_map/ppermute | solution.py:207
  35.3 8.7 %collective-permute-start.6 = (bf16[2,128,256]{2,1,0:T(8,128)(2,1)S(1)}, bf16[2,128,256]{2,1,0:T(8,128)(2,1)S(1)}, u32[]{:S(2)}, u32[]{:S(2)}) collective-permute-start(bf16[2,128,256]{2,1,0:T(8,128)(2,1)S(1)} %collective-permute-done.2.refs_1_), channel_id=1, source_target_pairs={{0,3},{1,2},{2,1},{3,0},{32,33},{33,32},{34,35},{35,34},{64,67},{6... | collective-permute-start | bytes 393224 | tf_op jit(solution)/shard_map/ppermute | solution.py:207
  38.7 5.7 %collective-permute-start.7 = (bf16[2,128,256]{2,1,0:T(8,128)(2,1)S(1)}, bf16[2,128,256]{2,1,0:T(8,128)(2,1)S(1)}, u32[]{:S(2)}, u32[]{:S(2)}) collective-permute-start(bf16[2,128,256]{2,1,0:T(8,128)(2,1)S(1)} %collective-permute-done.3.refs_2_), channel_id=1, source_target_pairs={{0,3},{1,2},{2,1},{3,0},{32,33},{33,32},{34,35},{35,34},{64,67},{6... | collective-permute-start | bytes 393224 | tf_op jit(solution)/shard_map/ppermute | solution.py:207
  40.6 6.0 %collective-permute-start.8 = (bf16[2,128,256]{2,1,0:T(8,128)(2,1)S(1)}, bf16[2,128,256]{2,1,0:T(8,128)(2,1)S(1)}, u32[]{:S(2)}, u32[]{:S(2)}) collective-permute-start(bf16[2,128,256]{2,1,0:T(8,128)(2,1)S(1)} %collective-permute-done.4.refs_3_), channel_id=1, source_target_pairs={{0,3},{1,2},{2,1},{3,0},{32,33},{33,32},{34,35},{35,34},{64,67},{6... | collective-permute-start | bytes 393224 | tf_op jit(solution)/shard_map/ppermute | solution.py:207
  46.6 1.6 %copy-start = (bf16[2,8,2,128,256]{4,3,2,1,0:T(8,128)(2,1)S(1)}, bf16[2,8,2,128,256]{4,3,2,1,0:T(8,128)(2,1)}, u32[]{:S(2)}) copy-start(bf16[2,8,2,128,256]{4,3,2,1,0:T(8,128)(2,1)} %get-tuple-element.15.keep_ref) | copy-start | bytes 6291460
  50.2 6.9 %collective-permute-start.9 = (f32[2,128,128]{2,1,0:T(8,128)S(1)}, f32[2,128,128]{2,1,0:T(8,128)S(1)}, u32[]{:S(2)}, u32[]{:S(2)}) collective-permute-start(f32[2,128,128]{2,1,0:T(8,128)S(1)} %get-tuple-element.17.part_ref), channel_id=1, source_target_pairs={{0,1},{1,0},{2,3},{3,2},{32,35},{33,34},{34,33},{35,32},{64,65},{6... | collective-permute-start | bytes 393224 | tf_op jit(solution)/shard_map/ppermute | solution.py:207
  57.6 8.5 %collective-permute-start.11 = (bf16[2,2,128,256]{3,2,1,0:T(8,128)(2,1)S(1)}, bf16[2,2,128,256]{3,2,1,0:T(8,128)(2,1)S(1)}, u32[]{:S(2)}, u32[]{:S(2)}) collective-permute-start(bf16[2,2,128,256]{3,2,1,0:T(8,128)(2,1)S(1)} %get-tuple-element.24), channel_id=1, source_target_pairs={{0,3},{1,2},{2,1},{3,0},{32,33},{33,32},{34,35},{35,34},{64,67},{6... | collective-permute-start | bytes 786440 | tf_op jit(solution)/shard_map/ppermute | solution.py:207
  59.8 12.9 %collective-permute-start.10 = (bf16[2,2,128,256]{3,2,1,0:T(8,128)(2,1)S(1)}, bf16[2,2,128,256]{3,2,1,0:T(8,128)(2,1)S(1)}, u32[]{:S(2)}, u32[]{:S(2)}) collective-permute-start(bf16[2,2,128,256]{3,2,1,0:T(8,128)(2,1)S(1)} %get-tuple-element.21), channel_id=1, source_target_pairs={{0,3},{1,2},{2,1},{3,0},{32,33},{33,32},{34,35},{35,34},{64,67},{6... | collective-permute-start | bytes 786440 | tf_op jit(solution)/shard_map/ppermute | solution.py:207
  66.2 9.4 %collective-permute-start.12 = (bf16[2,128,256]{2,1,0:T(8,128)(2,1)S(1)}, bf16[2,128,256]{2,1,0:T(8,128)(2,1)S(1)}, u32[]{:S(2)}, u32[]{:S(2)}) collective-permute-start(bf16[2,128,256]{2,1,0:T(8,128)(2,1)S(1)} %get-tuple-element.25), channel_id=1, source_target_pairs={{0,12},{4,8},{8,4},{12,0},{16,28},{20,24},{24,20},{28,16},{1,13},{... | collective-permute-start | bytes 393224 | tf_op jit(solution)/shard_map/ppermute | solution.py:211
  70.1 8.4 %collective-permute-start.13 = (bf16[2,128,256]{2,1,0:T(8,128)(2,1)S(1)}, bf16[2,128,256]{2,1,0:T(8,128)(2,1)S(1)}, u32[]{:S(2)}, u32[]{:S(2)}) collective-permute-start(bf16[2,128,256]{2,1,0:T(8,128)(2,1)S(1)} %get-tuple-element.26), channel_id=1, source_target_pairs={{0,8},{4,12},{8,0},{12,4},{16,24},{20,28},{24,16},{28,20},{1,9},{5... | collective-permute-start | bytes 393224 | tf_op jit(solution)/shard_map/ppermute | solution.py:211
  72.8 6.7 %collective-permute-start.14 = (bf16[2,128,256]{2,1,0:T(8,128)(2,1)S(1)}, bf16[2,128,256]{2,1,0:T(8,128)(2,1)S(1)}, u32[]{:S(2)}, u32[]{:S(2)}) collective-permute-start(bf16[2,128,256]{2,1,0:T(8,128)(2,1)S(1)} %get-tuple-element.27), channel_id=1, source_target_pairs={{0,4},{4,0},{8,12},{12,8},{16,20},{20,16},{24,28},{28,24},{1,5},{5... | collective-permute-start | bytes 393224 | tf_op jit(solution)/shard_map/ppermute | solution.py:211
  79.6 24.8 %collective-permute-start.16 = (bf16[2,128,256]{2,1,0:T(8,128)(2,1)S(1)}, bf16[2,128,256]{2,1,0:T(8,128)(2,1)S(1)}, u32[]{:S(2)}, u32[]{:S(2)}) collective-permute-start(bf16[2,128,256]{2,1,0:T(8,128)(2,1)S(1)} %fusion.5), channel_id=1, source_target_pairs={{0,496},{4,500},{8,504},{12,508},{16,480},{20,484},{24,488},{28,49... | collective-permute-start | bytes 393224 | tf_op jit(solution)/shard_map/ppermute | solution.py:228
  98.3 6.1 %collective-permute-start.15 = (bf16[2,128,256]{2,1,0:T(8,128)(2,1)S(1)}, bf16[2,128,256]{2,1,0:T(8,128)(2,1)S(1)}, u32[]{:S(2)}, u32[]{:S(2)}) collective-permute-start(bf16[2,128,256]{2,1,0:T(8,128)(2,1)S(1)} %fusion.5), channel_id=1, source_target_pairs={{0,32},{32,0},{64,96},{96,64},{128,160},{160,128},{192,224},{224,1... | collective-permute-start | bytes 393224 | tf_op jit(solution)/shard_map/ppermute | solution.py:219
  104.6 11.6 %collective-permute-start.17 = (bf16[128,256]{1,0:T(8,128)(2,1)S(1)}, bf16[128,256]{1,0:T(8,128)(2,1)S(1)}, u32[]{:S(2)}, u32[]{:S(2)}) collective-permute-start(bf16[128,256]{1,0:T(8,128)(2,1)S(1)} %fusion.2), channel_id=1, source_target_pairs={{0,16},{4,20},{8,24},{12,28},{16,0},{20,4},{24,8},{28,12},{1,17},{... | collective-permute-start | bytes 196616 | tf_op jit(solution)/shard_map/ppermute | solution.py:211

commit v7 on v6

--- a/solution.py
+++ b/solution.py
@@ -94,16 +94,16 @@
 
 
 def project_kernel(keep_ref, got_ref, *refs):
-    piece_refs, (out_ref, held_ref, low_ref, sem) = refs[: 2 * QUAD], refs[2 * QUAD :]
+    piece_refs, (out_ref, held_ref, low_ref, sem) = refs[:2], refs[2:]
     loads = []
     for t, ref in enumerate((keep_ref, got_ref)):
         loads.append(pltpu.make_async_copy(ref, held_ref.at[t], sem.at[t]))
         loads[-1].start()
-    me = lax.axis_index("z")
-    for c in range(2):
+    half = lax.axis_index("half")
+    for c, ref in enumerate(piece_refs):
         for near in range(QUAD):
             for far in range(2):
-                low_ref[c, me ^ (near + QUAD * far)] = piece_refs[QUAD * c + near][far]
+                low_ref[c, QUAD * (half ^ far) + near] = ref[near, far]
     for t in range(2):
         loads[t].wait()
         for half in range(2):
@@ -145,7 +145,7 @@
 
 
 def column_grads(low_ref, feat_ref, out_refs, column):
-    me = lax.axis_index("z")
+    me = my_z()
     for nears, out_ref in zip((EARLY, LATE), out_refs, strict=True):
         for i, near in enumerate(nears):
             for far in range(2):
@@ -208,7 +208,11 @@
 
 
 def swapped(array, by):
-    return lax.ppermute(array, "z", [(i, i ^ by) for i in range(NZ)])
+    return lax.ppermute(array, ("half", "near"), [(i, i ^ by) for i in range(NZ)])
+
+
+def my_z():
+    return QUAD * lax.axis_index("half") + lax.axis_index("near")
 
 
 def is_far(group):
@@ -225,7 +229,7 @@
         other = (g + 1 if g % 2 else g - 1) % GROUPS
         for z in range(NZ):
             pairs.append((g * NZ + z, other * NZ + (z ^ QUAD if is_far(g) else z)))
-    return lax.ppermute(array, ("blk", "z"), pairs)
+    return lax.ppermute(array, ("blk", "half", "near"), pairs)
 
 
 def local(tokens, norm_gain, adapt_in, adapt_out, upstream):
@@ -235,8 +239,8 @@
     master = jnp.concatenate([adapt_in[0].T, adapt_out[0].T], axis=0)
     own = master.astype(narrow)
     pair = jnp.stack([own, swapped(own, QUAD)])
-    lows = [pair] + [swapped(pair, k) for k in range(1, QUAD)]
-    lows += [along_x(low, 1) for low in lows]
+    low = lax.all_to_all(jnp.broadcast_to(pair, (QUAD,) + pair.shape), "near", 0, 0, tiled=True)
+    lows = [low, along_x(low, 1)]
 
     keep, send = prep(tokens[0], norm_gain[None], upstream[0])
     got = along_x(send, 0)
@@ -269,8 +273,9 @@
 
 
 def solution(mesh):
-    mesh = Mesh(mesh.devices.reshape(GROUPS, NZ, NX), ("blk", "z", "x"))
-    split = P("blk", ("z", "x"), None)
+    axes = ("blk", "half", "near", "x")
+    mesh = Mesh(mesh.devices.reshape(GROUPS, 2, QUAD, NX), axes)
+    split = P("blk", axes[1:], None)
     in_specs = (split, P(), split, split, split)
     return jax.shard_map(
         local, mesh=mesh, in_specs=in_specs, out_specs=(split, split), check_vma=False

time: 118 us -> 110 us (0.932)
  starting transfers between devices: 80.1 us -> 50.9 us
  blocking collectives: 0 us -> 19.7 us
  waiting for transfers between devices: 25.7 us -> 28.9 us
  local copies, waits for them, and re-layouts: 1.61 us -> 0.06 us
    ppermute x9 -> x6, starting transfers between devices: 55.6 us -> 33 us  [the longest x5 24 us: swapped(): lax.ppermute(array, ('half', 'near'), [(i, i ^ by) for i in range(NZ)])]
    all_to_all x0 -> x1, blocking collectives: none -> 19.7 us  [local(): lax.all_to_all(jnp.broadcast_to(pair, (QUAD,) + pair.shape), 'near', 0, 0...]
    ppermute x8 -> x5, starting transfers between devices: 22.6 us -> 16 us  [along_x(): return lax.ppermute(array, ('blk', 'x'), pairs)]
    ppermute x8 -> x5, waiting for transfers between devices: 9.88 us -> 12.2 us  [along_x(): return lax.ppermute(array, ('blk', 'x'), pairs)]
    unnamed x6, local copies, waits for them, and re-layouts: 1.6 us -> 0.02 us
    ppermute x9 -> x6, waiting for transfers between devices: 15.9 us -> 16.7 us  [the longest x5 13.3 us: swapped(): lax.ppermute(array, ('half', 'near'), [(i, i ^ by) for i in range(NZ)])]
  transfers between devices with their start and end apart: 18 -> 12, of which waited for: 9 -> 7; matrix products, arithmetic and copies ran while one was open for 0% -> 0% of each run, Pallas kernels for 1% -> 5%
where the time goes in v7:
time: 110 us
  starting transfers between devices  50.9 us (46%)
  waiting for transfers between devices  28.9 us (26%)
  blocking collectives  19.7 us (18%)
  Pallas kernels  7.58 us (7%)
  other arithmetic  1.77 us (2%)
    ppermute x5, starting transfers between devices, swapped(): lax.ppermute(array, ('half', 'near'), [(i, i ^ by) for i in range(NZ)])  24 us
    all_to_all x1, blocking collectives, local(): lax.all_to_all(jnp.broadcast_to(pair, (QUAD,) + pair.shape), 'near', 0, 0...  19.7 us
    ppermute x5, starting transfers between devices, along_x(): return lax.ppermute(array, ('blk', 'x'), pairs)  16 us
    ppermute x5, waiting for transfers between devices, swapped(): lax.ppermute(array, ('half', 'near'), [(i, i ^ by) for i in range(NZ)])  13.3 us
    ppermute x5, waiting for transfers between devices, along_x(): return lax.ppermute(array, ('blk', 'x'), pairs)  12.2 us
    ppermute x1, starting transfers between devices, second_neighbour(): return lax.ppermute(array, ('blk', 'half', 'near'), pairs)  8.94 us
    pallas_call x1, Pallas kernels, prep(): pl.pallas_call(prep_kernel, in_specs=[pl.BlockSpec(memory_space=pl.ANY),...  4.46 us
    ppermute x1, waiting for transfers between devices, second_neighbour(): return lax.ppermute(array, ('blk', 'half', 'near'), pairs)  3.42 us
  transfers between devices with their start and end apart: 12, of which 7 were waited for; matrix products, arithmetic and copies ran while one was open for 0% of the time, Pallas kernels for 5%

profile of v7, /device:TPU:25, one launch (start us, length us, event | category | flops | bytes accessed | tf_op | source)
XLA Modules:
  0.0 109.8 jit_solution(4565272047662165134)
XLA Ops:
  0.6 0.9 fusion.6
  1.5 8.8 %collective-permute-start.1 = (bf16[128,256]{1,0:T(8,128)(2,1)S(1)}, bf16[128,256]{1,0:T(8,128)(2,1)S(1)}, u32[]{:S(2)}, u32[]{:S(2)}) collective-permute-start(bf16[128,256]{1,0:T(8,128)(2,1)S(1)} %fusion.6), channel_id=1, source_target_pairs={{0,16},{4,20},{8,24},{12,28},{16,0},{20,4},{24,8},{28,12},{1,17},{... | collective-permute-start | bytes 196616 | tf_op jit(solution)/shard_map/ppermute | solution.py:211
  10.3 0.0 copy-start.1
  10.4 0.0 copy-start.2
  10.4 4.5 %shard_map.68 = (bf16[2,8,2,128,256]{4,3,2,1,0:T(8,128)(2,1)}, bf16[2,8,2,128,256]{4,3,2,1,0:T(8,128)(2,1)}) custom-call(bf16[128,8192]{1,0:T(8,128)(2,1)} %bitcast.30, f32[1,8192]{1,0:T(1,128)} %bitcast.37, bf16[128,8192]{1,0:T(8,128)(2,1)} %bitcast.31), custom_call_target="tpu_custom_call" | custom-call | flops 6291456 | bytes 8388608 | tf_op jit(solution)/shard_map/pallas_call | solution.py:74
  14.8 0.0 copy-start
  14.8 4.5 %collective-permute-start = (bf16[2,8,2,128,256]{4,3,2,1,0:T(8,128)(2,1)}, bf16[2,8,2,128,256]{4,3,2,1,0:T(8,128)(2,1)S(1)}, u32[]{:S(2)}, u32[]{:S(2)}) collective-permute-start(bf16[2,8,2,128,256]{4,3,2,1,0:T(8,128)(2,1)} %get-tuple-element.16), channel_id=1, source_target_pairs={{0,1},{1,0},{2,3},{3,2},{32,35},{33,34},{34,33},{35,32},{64,65},{6... | collective-permute-start | bytes 6291464 | tf_op jit(solution)/shard_map/ppermute | solution.py:207
  19.4 0.0 copy-done.1
  19.4 0.0 copy-done.2
  19.4 0.0 collective-permute-done.1
  19.5 19.7 %all_to_all.5.refs_0_ = bf16[4,2,128,256]{3,2,1,0:T(8,128)(2,1)S(1)} all-to-all(bf16[4,2,128,256]{3,2,1,0:T(8,128)(2,1)S(1)} %broadcast_in_dim.13), channel_id=1, replica_groups=mesh['blk'=16,'half'=2,'near'=4,'x'=4] {'near'}, dimensions={0} | all-to-all | bytes 1048576 | tf_op jit(solution)/shard_map/all_to_all | solution.py:242
  39.2 1.9 %collective-permute-start.2 = (bf16[4,2,128,256]{3,2,1,0:T(8,128)(2,1)S(1)}, bf16[4,2,128,256]{3,2,1,0:T(8,128)(2,1)S(1)}, u32[]{:S(2)}, u32[]{:S(2)}) collective-permute-start(bf16[4,2,128,256]{3,2,1,0:T(8,128)(2,1)S(1)} %all_to_all.5.refs_0_), channel_id=1, source_target_pairs={{0,3},{1,2},{2,1},{3,0},{32,33},{33,32},{34,35},{35,34},{64,67},{6... | collective-permute-start | bytes 1572872 | tf_op jit(solution)/shard_map/ppermute | solution.py:207
  41.1 2.1 %collective-permute-done.got_ref = bf16[2,8,2,128,256]{4,3,2,1,0:T(8,128)(2,1)S(1)} collective-permute-done((bf16[2,8,2,128,256]{4,3,2,1,0:T(8,128)(2,1)}, bf16[2,8,2,128,256]{4,3,2,1,0:T(8,128)(2,1)S(1)}, u32[]{:S(2)}, u32[]{:S(2)}) %collective-permute-start) | collective-permute-done | bytes 2097184 | tf_op jit(solution)/shard_map/ppermute | solution.py:207
  43.2 6.2 %collective-permute-done.2.refs_1_ = bf16[4,2,128,256]{3,2,1,0:T(8,128)(2,1)S(1)} collective-permute-done((bf16[4,2,128,256]{3,2,1,0:T(8,128)(2,1)S(1)}, bf16[4,2,128,256]{3,2,1,0:T(8,128)(2,1)S(1)}, u32[]{:S(2)}, u32[]{:S(2)}) %collective-permute-start.2) | collective-permute-done | bytes 524320 | tf_op jit(solution)/shard_map/ppermute | solution.py:207
  49.4 0.0 copy-done
  49.4 2.0 %shard_map.69 = (f32[2,128,128]{2,1,0:T(8,128)S(1)}, bf16[2,2,8,2,128,256]{5,4,3,2,1,0:T(8,128)(2,1)S(1)}) custom-call(bf16[2,8,2,128,256]{4,3,2,1,0:T(8,128)(2,1)S(1)} %copy-done, bf16[2,8,2,128,256]{4,3,2,1,0:T(8,128)(2,1)S(1)} %collective-permute-done.got_ref, bf16[4,2,128,256]{3,2,1,0:T(8,128)(2,1)S(1)} %all_to_all.5.refs_0_, ...), custom_call_target="tpu_custom_call" | custom-call | flops 536870912 | bytes 6291456 | tf_op jit(solution)/shard_map/pallas_call | solution.py:124
  51.5 4.3 %collective-permute-start.3 = (f32[2,128,128]{2,1,0:T(8,128)S(1)}, f32[2,128,128]{2,1,0:T(8,128)S(1)}, u32[]{:S(2)}, u32[]{:S(2)}) collective-permute-start(f32[2,128,128]{2,1,0:T(8,128)S(1)} %get-tuple-element.17.part_ref), channel_id=1, source_target_pairs={{0,1},{1,0},{2,3},{3,2},{32,35},{33,34},{34,33},{35,32},{64,65},{6... | collective-permute-start | bytes 393224 | tf_op jit(solution)/shard_map/ppermute | solution.py:207
  55.7 2.6 %collective-permute-done.3.got_ref = f32[2,128,128]{2,1,0:T(8,128)S(1)} collective-permute-done((f32[2,128,128]{2,1,0:T(8,128)S(1)}, f32[2,128,128]{2,1,0:T(8,128)S(1)}, u32[]{:S(2)}, u32[]{:S(2)}) %collective-permute-start.3) | collective-permute-done | bytes 131104 | tf_op jit(solution)/shard_map/ppermute | solution.py:207
  58.4 0.5 shard_map.70
  58.9 1.9 %collective-permute-start.5 = (bf16[2,2,128,256]{3,2,1,0:T(8,128)(2,1)S(1)}, bf16[2,2,128,256]{3,2,1,0:T(8,128)(2,1)S(1)}, u32[]{:S(2)}, u32[]{:S(2)}) collective-permute-start(bf16[2,2,128,256]{3,2,1,0:T(8,128)(2,1)S(1)} %get-tuple-element.24), channel_id=1, source_target_pairs={{0,3},{1,2},{2,1},{3,0},{32,33},{33,32},{34,35},{35,34},{64,67},{6... | collective-permute-start | bytes 786440 | tf_op jit(solution)/shard_map/ppermute | solution.py:207
  60.8 3.4 %collective-permute-start.4 = (bf16[2,2,128,256]{3,2,1,0:T(8,128)(2,1)S(1)}, bf16[2,2,128,256]{3,2,1,0:T(8,128)(2,1)S(1)}, u32[]{:S(2)}, u32[]{:S(2)}) collective-permute-start(bf16[2,2,128,256]{3,2,1,0:T(8,128)(2,1)S(1)} %get-tuple-element.21), channel_id=1, source_target_pairs={{0,3},{1,2},{2,1},{3,0},{32,33},{33,32},{34,35},{35,34},{64,67},{6... | collective-permute-start | bytes 786440 | tf_op jit(solution)/shard_map/ppermute | solution.py:207
  64.2 0.5 shard_map.71
  64.7 1.3 %collective-permute-done.5.got_ref = bf16[2,2,128,256]{3,2,1,0:T(8,128)(2,1)S(1)} collective-permute-done((bf16[2,2,128,256]{3,2,1,0:T(8,128)(2,1)S(1)}, bf16[2,2,128,256]{3,2,1,0:T(8,128)(2,1)S(1)}, u32[]{:S(2)}, u32[]{:S(2)}) %collective-permute-start.5) | collective-permute-done | bytes 262176 | tf_op jit(solution)/shard_map/ppermute | solution.py:207
  66.0 6.2 %collective-permute-start.6 = (bf16[2,128,256]{2,1,0:T(8,128)(2,1)S(1)}, bf16[2,128,256]{2,1,0:T(8,128)(2,1)S(1)}, u32[]{:S(2)}, u32[]{:S(2)}) collective-permute-start(bf16[2,128,256]{2,1,0:T(8,128)(2,1)S(1)} %get-tuple-element.25), channel_id=1, source_target_pairs={{0,12},{4,8},{8,4},{12,0},{16,28},{20,24},{24,20},{28,16},{1,13},{... | collective-permute-start | bytes 393224 | tf_op jit(solution)/shard_map/ppermute | solution.py:211
  72.3 1.9 %collective-permute-start.7 = (bf16[2,128,256]{2,1,0:T(8,128)(2,1)S(1)}, bf16[2,128,256]{2,1,0:T(8,128)(2,1)S(1)}, u32[]{:S(2)}, u32[]{:S(2)}) collective-permute-start(bf16[2,128,256]{2,1,0:T(8,128)(2,1)S(1)} %get-tuple-element.26), channel_id=1, source_target_pairs={{0,8},{4,12},{8,0},{12,4},{16,24},{20,28},{24,16},{28,20},{1,9},{5... | collective-permute-start | bytes 393224 | tf_op jit(solution)/shard_map/ppermute | solution.py:211
  74.2 0.0 collective-permute-done.4.got_ref
  74.2 0.1 shard_map.72
  74.3 2.2 %collective-permute-start.8 = (bf16[2,128,256]{2,1,0:T(8,128)(2,1)S(1)}, bf16[2,128,256]{2,1,0:T(8,128)(2,1)S(1)}, u32[]{:S(2)}, u32[]{:S(2)}) collective-permute-start(bf16[2,128,256]{2,1,0:T(8,128)(2,1)S(1)} %get-tuple-element.27), channel_id=1, source_target_pairs={{0,4},{4,0},{8,12},{12,8},{16,20},{20,16},{24,28},{28,24},{1,5},{5... | collective-permute-start | bytes 393224 | tf_op jit(solution)/shard_map/ppermute | solution.py:211
  76.5 0.0 collective-permute-done.6
  76.5 7.1 %collective-permute-done.7 = bf16[2,128,256]{2,1,0:T(8,128)(2,1)S(1)} collective-permute-done((bf16[2,128,256]{2,1,0:T(8,128)(2,1)S(1)}, bf16[2,128,256]{2,1,0:T(8,128)(2,1)S(1)}, u32[]{:S(2)}, u32[]{:S(2)}) %collective-permute-start.7) | collective-permute-done | bytes 131104 | tf_op jit(solution)/shard_map/ppermute | solution.py:211
  83.6 0.0 collective-permute-done.8
  83.6 0.1 fusion.5
  83.7 8.9 %collective-permute-start.10 = (bf16[2,128,256]{2,1,0:T(8,128)(2,1)S(1)}, bf16[2,128,256]{2,1,0:T(8,128)(2,1)S(1)}, u32[]{:S(2)}, u32[]{:S(2)}) collective-permute-start(bf16[2,128,256]{2,1,0:T(8,128)(2,1)S(1)} %fusion.5), channel_id=1, source_target_pairs={{0,496},{4,500},{8,504},{12,508},{16,480},{20,484},{24,488},{28,49... | collective-permute-start | bytes 393224 | tf_op jit(solution)/shard_map/ppermute | solution.py:232
  92.6 1.9 %collective-permute-start.9 = (bf16[2,128,256]{2,1,0:T(8,128)(2,1)S(1)}, bf16[2,128,256]{2,1,0:T(8,128)(2,1)S(1)}, u32[]{:S(2)}, u32[]{:S(2)}) collective-permute-start(bf16[2,128,256]{2,1,0:T(8,128)(2,1)S(1)} %fusion.5), channel_id=1, source_target_pairs={{0,32},{32,0},{64,96},{96,64},{128,160},{160,128},{192,224},{224,1... | collective-permute-start | bytes 393224 | tf_op jit(solution)/shard_map/ppermute | solution.py:223
  94.6 3.4 %collective-permute-done.10 = bf16[2,128,256]{2,1,0:T(8,128)(2,1)S(1)} collective-permute-done((bf16[2,128,256]{2,1,0:T(8,128)(2,1)S(1)}, bf16[2,128,256]{2,1,0:T(8,128)(2,1)S(1)}, u32[]{:S(2)}, u32[]{:S(2)}) %collective-permute-start.10) | collective-permute-done | bytes 131104 | tf_op jit(solution)/shard_map/ppermute | solution.py:232
  98.0 0.0 collective-permute-done.9
  98.0 0.1 fusion
  98.1 4.9 %collective-permute-start.11 = (bf16[128,256]{1,0:T(8,128)(2,1)S(1)}, bf16[128,256]{1,0:T(8,128)(2,1)S(1)}, u32[]{:S(2)}, u32[]{:S(2)}) collective-permute-start(bf16[128,256]{1,0:T(8,128)(2,1)S(1)} %fusion.2), channel_id=1, source_target_pairs={{0,16},{4,20},{8,24},{12,28},{16,0},{20,4},{24,8},{28,12},{1,17},{... | collective-permute-start | bytes 196616 | tf_op jit(solution)/shard_map/ppermute | solution.py:211
  103.0 6.1 %collective-permute-done.11 = bf16[128,256]{1,0:T(8,128)(2,1)S(1)} collective-permute-done((bf16[128,256]{1,0:T(8,128)(2,1)S(1)}, bf16[128,256]{1,0:T(8,128)(2,1)S(1)}, u32[]{:S(2)}, u32[]{:S(2)}) %collective-permute-start.11) | collective-permute-done | bytes 65568 | tf_op jit(solution)/shard_map/ppermute | solution.py:211
  109.2 0.7 fusion.3
  (8 shorter events, 0.2 us)
Async XLA Ops:
  1.5 17.9 %collective-permute-start.1 = (bf16[128,256]{1,0:T(8,128)(2,1)S(1)}, bf16[128,256]{1,0:T(8,128)(2,1)S(1)}, u32[]{:S(2)}, u32[]{:S(2)}) collective-permute-start(bf16[128,256]{1,0:T(8,128)(2,1)S(1)} %fusion.6), channel_id=1, source_target_pairs={{0,16},{4,20},{8,24},{12,28},{16,0},{20,4},{24,8},{28,12},{1,17},{... | collective-permute-start | bytes 196616 | tf_op jit(solution)/shard_map/ppermute | solution.py:211
  10.3 9.0 %copy-start.1 = (f32[1,256,64]{1,2,0:T(8,128)S(1)}, f32[1,256,64]{1,2,0:T(8,128)}, u32[]{:S(2)}) copy-start(f32[1,256,64]{1,2,0:T(8,128)} %param.8) | copy-start | bytes 196612
  10.4 9.0 %copy-start.2 = (f32[1,256,64]{1,2,0:T(8,128)S(1)}, f32[1,256,64]{1,2,0:T(8,128)}, u32[]{:S(2)}) copy-start(f32[1,256,64]{1,2,0:T(8,128)} %param.7) | copy-start | bytes 196612
  14.8 34.6 %copy-start = (bf16[2,8,2,128,256]{4,3,2,1,0:T(8,128)(2,1)S(1)}, bf16[2,8,2,128,256]{4,3,2,1,0:T(8,128)(2,1)}, u32[]{:S(2)}) copy-start(bf16[2,8,2,128,256]{4,3,2,1,0:T(8,128)(2,1)} %get-tuple-element.15.keep_ref) | copy-start | bytes 6291460
  14.8 28.3 %collective-permute-start = (bf16[2,8,2,128,256]{4,3,2,1,0:T(8,128)(2,1)}, bf16[2,8,2,128,256]{4,3,2,1,0:T(8,128)(2,1)S(1)}, u32[]{:S(2)}, u32[]{:S(2)}) collective-permute-start(bf16[2,8,2,128,256]{4,3,2,1,0:T(8,128)(2,1)} %get-tuple-element.16), channel_id=1, source_target_pairs={{0,1},{1,0},{2,3},{3,2},{32,35},{33,34},{34,33},{35,32},{64,65},{6... | collective-permute-start | bytes 6291464 | tf_op jit(solution)/shard_map/ppermute | solution.py:207
  39.2 10.2 %collective-permute-start.2 = (bf16[4,2,128,256]{3,2,1,0:T(8,128)(2,1)S(1)}, bf16[4,2,128,256]{3,2,1,0:T(8,128)(2,1)S(1)}, u32[]{:S(2)}, u32[]{:S(2)}) collective-permute-start(bf16[4,2,128,256]{3,2,1,0:T(8,128)(2,1)S(1)} %all_to_all.5.refs_0_), channel_id=1, source_target_pairs={{0,3},{1,2},{2,1},{3,0},{32,33},{33,32},{34,35},{35,34},{64,67},{6... | collective-permute-start | bytes 1572872 | tf_op jit(solution)/shard_map/ppermute | solution.py:207
  51.5 6.9 %collective-permute-start.3 = (f32[2,128,128]{2,1,0:T(8,128)S(1)}, f32[2,128,128]{2,1,0:T(8,128)S(1)}, u32[]{:S(2)}, u32[]{:S(2)}) collective-permute-start(f32[2,128,128]{2,1,0:T(8,128)S(1)} %get-tuple-element.17.part_ref), channel_id=1, source_target_pairs={{0,1},{1,0},{2,3},{3,2},{32,35},{33,34},{34,33},{35,32},{64,65},{6... | collective-permute-start | bytes 393224 | tf_op jit(solution)/shard_map/ppermute | solution.py:207
  58.9 7.1 %collective-permute-start.5 = (bf16[2,2,128,256]{3,2,1,0:T(8,128)(2,1)S(1)}, bf16[2,2,128,256]{3,2,1,0:T(8,128)(2,1)S(1)}, u32[]{:S(2)}, u32[]{:S(2)}) collective-permute-start(bf16[2,2,128,256]{3,2,1,0:T(8,128)(2,1)S(1)} %get-tuple-element.24), channel_id=1, source_target_pairs={{0,3},{1,2},{2,1},{3,0},{32,33},{33,32},{34,35},{35,34},{64,67},{6... | collective-permute-start | bytes 786440 | tf_op jit(solution)/shard_map/ppermute | solution.py:207
  60.8 13.4 %collective-permute-start.4 = (bf16[2,2,128,256]{3,2,1,0:T(8,128)(2,1)S(1)}, bf16[2,2,128,256]{3,2,1,0:T(8,128)(2,1)S(1)}, u32[]{:S(2)}, u32[]{:S(2)}) collective-permute-start(bf16[2,2,128,256]{3,2,1,0:T(8,128)(2,1)S(1)} %get-tuple-element.21), channel_id=1, source_target_pairs={{0,3},{1,2},{2,1},{3,0},{32,33},{33,32},{34,35},{35,34},{64,67},{6... | collective-permute-start | bytes 786440 | tf_op jit(solution)/shard_map/ppermute | solution.py:207
  66.0 10.4 %collective-permute-start.6 = (bf16[2,128,256]{2,1,0:T(8,128)(2,1)S(1)}, bf16[2,128,256]{2,1,0:T(8,128)(2,1)S(1)}, u32[]{:S(2)}, u32[]{:S(2)}) collective-permute-start(bf16[2,128,256]{2,1,0:T(8,128)(2,1)S(1)} %get-tuple-element.25), channel_id=1, source_target_pairs={{0,12},{4,8},{8,4},{12,0},{16,28},{20,24},{24,20},{28,16},{1,13},{... | collective-permute-start | bytes 393224 | tf_op jit(solution)/shard_map/ppermute | solution.py:211
  72.3 11.3 %collective-permute-start.7 = (bf16[2,128,256]{2,1,0:T(8,128)(2,1)S(1)}, bf16[2,128,256]{2,1,0:T(8,128)(2,1)S(1)}, u32[]{:S(2)}, u32[]{:S(2)}) collective-permute-start(bf16[2,128,256]{2,1,0:T(8,128)(2,1)S(1)} %get-tuple-element.26), channel_id=1, source_target_pairs={{0,8},{4,12},{8,0},{12,4},{16,24},{20,28},{24,16},{28,20},{1,9},{5... | collective-permute-start | bytes 393224 | tf_op jit(solution)/shard_map/ppermute | solution.py:211
  74.3 9.3 %collective-permute-start.8 = (bf16[2,128,256]{2,1,0:T(8,128)(2,1)S(1)}, bf16[2,128,256]{2,1,0:T(8,128)(2,1)S(1)}, u32[]{:S(2)}, u32[]{:S(2)}) collective-permute-start(bf16[2,128,256]{2,1,0:T(8,128)(2,1)S(1)} %get-tuple-element.27), channel_id=1, source_target_pairs={{0,4},{4,0},{8,12},{12,8},{16,20},{20,16},{24,28},{28,24},{1,5},{5... | collective-permute-start | bytes 393224 | tf_op jit(solution)/shard_map/ppermute | solution.py:211
  83.7 14.3 %collective-permute-start.10 = (bf16[2,128,256]{2,1,0:T(8,128)(2,1)S(1)}, bf16[2,128,256]{2,1,0:T(8,128)(2,1)S(1)}, u32[]{:S(2)}, u32[]{:S(2)}) collective-permute-start(bf16[2,128,256]{2,1,0:T(8,128)(2,1)S(1)} %fusion.5), channel_id=1, source_target_pairs={{0,496},{4,500},{8,504},{12,508},{16,480},{20,484},{24,488},{28,49... | collective-permute-start | bytes 393224 | tf_op jit(solution)/shard_map/ppermute | solution.py:232
  92.6 5.4 %collective-permute-start.9 = (bf16[2,128,256]{2,1,0:T(8,128)(2,1)S(1)}, bf16[2,128,256]{2,1,0:T(8,128)(2,1)S(1)}, u32[]{:S(2)}, u32[]{:S(2)}) collective-permute-start(bf16[2,128,256]{2,1,0:T(8,128)(2,1)S(1)} %fusion.5), channel_id=1, source_target_pairs={{0,32},{32,0},{64,96},{96,64},{128,160},{160,128},{192,224},{224,1... | collective-permute-start | bytes 393224 | tf_op jit(solution)/shard_map/ppermute | solution.py:223
  98.1 11.0 %collective-permute-start.11 = (bf16[128,256]{1,0:T(8,128)(2,1)S(1)}, bf16[128,256]{1,0:T(8,128)(2,1)S(1)}, u32[]{:S(2)}, u32[]{:S(2)}) collective-permute-start(bf16[128,256]{1,0:T(8,128)(2,1)S(1)} %fusion.2), channel_id=1, source_target_pairs={{0,16},{4,20},{8,24},{12,28},{16,0},{20,4},{24,8},{28,12},{1,17},{... | collective-permute-start | bytes 196616 | tf_op jit(solution)/shard_map/ppermute | solution.py:211

commit v8 on v7

--- a/solution.py
+++ b/solution.py
@@ -93,52 +93,54 @@
     )(tokens, gain, upstream)
 
 
-def project_kernel(keep_ref, got_ref, *refs):
-    piece_refs, (out_ref, held_ref, low_ref, sem) = refs[:2], refs[2:]
+def column_part(low_ref, held_ref, t, half, column):
+    mine = lax.axis_index("half")
+    part = jnp.zeros((R, TOK), jnp.float32)
+    for near in range(QUAD):
+        for far in range(2):
+            part += lax.dot_general(
+                low_ref[near, far, half * R : (half + 1) * R],
+                held_ref[t, column, QUAD * (mine ^ far) + near, 1 - half],
+                LAST,
+                preferred_element_type=jnp.float32,
+            )
+    return part
+
+
+def first_project_kernel(keep_ref, got_ref, low_ref, out_ref, held_ref, sem):
     loads = []
     for t, ref in enumerate((keep_ref, got_ref)):
         loads.append(pltpu.make_async_copy(ref, held_ref.at[t], sem.at[t]))
         loads[-1].start()
-    half = lax.axis_index("half")
-    for c, ref in enumerate(piece_refs):
-        for near in range(QUAD):
-            for far in range(2):
-                low_ref[c, QUAD * (half ^ far) + near] = ref[near, far]
     for t in range(2):
         loads[t].wait()
         for half in range(2):
+            out_ref[t, half * R : (half + 1) * R] = column_part(low_ref, held_ref, t, half, 0)
+
+
+def second_project_kernel(part_ref, held_ref, low_ref, out_ref):
+    for t in range(2):
+        for half in range(2):
             rows = slice(half * R, (half + 1) * R)
-            part = jnp.zeros((R, TOK), jnp.float32)
-            for c in range(2):
-                for z in range(NZ):
-                    part += lax.dot_general(
-                        low_ref[c, z, rows],
-                        held_ref[t, c, z, 1 - half],
-                        LAST,
-                        preferred_element_type=jnp.float32,
-                    )
-            out_ref[t, rows] = part
-
-
-def project(keep, got, lows):
+            out_ref[t, rows] = part_ref[t, rows] + column_part(low_ref, held_ref, t, half, 1)
+
+
+def first_project(keep, got, low):
     return pl.pallas_call(
-        project_kernel,
+        first_project_kernel,
         in_specs=[pl.BlockSpec(memory_space=pl.ANY) for _ in range(2)]
-        + [pl.BlockSpec(memory_space=pltpu.VMEM) for _ in lows],
+        + [pl.BlockSpec(memory_space=pltpu.VMEM)],
         out_specs=[pl.BlockSpec(memory_space=pltpu.VMEM) for _ in range(2)],
         out_shape=[
             jax.ShapeDtypeStruct((2, 2 * R, TOK), jnp.float32),
             jax.ShapeDtypeStruct((2,) + keep.shape, keep.dtype),
         ],
-        scratch_shapes=[
-            pltpu.VMEM((2, NZ, 2 * R, OWN), jnp.bfloat16),
-            pltpu.SemaphoreType.DMA((2,)),
-        ],
+        scratch_shapes=[pltpu.SemaphoreType.DMA((2,))],
         compiler_params=pltpu.CompilerParams(vmem_limit_bytes=VMEM_LIMIT),
         cost_estimate=pl.CostEstimate(
-            flops=8 * TOK * D * R, bytes_accessed=6 * 1024 * 1024, transcendentals=0
+            flops=4 * TOK * D * R, bytes_accessed=4 * 1024 * 1024, transcendentals=0
         ),
-    )(keep, got, *lows)
+    )(keep, got, low)
 
 
 EARLY, LATE = (3, 2), (1, 0)
@@ -240,11 +242,14 @@
     own = master.astype(narrow)
     pair = jnp.stack([own, swapped(own, QUAD)])
     low = lax.all_to_all(jnp.broadcast_to(pair, (QUAD,) + pair.shape), "near", 0, 0, tiled=True)
-    lows = [low, along_x(low, 1)]
+    other = along_x(low, 1)
 
     keep, send = prep(tokens[0], norm_gain[None], upstream[0])
     got = along_x(send, 0)
-    part, feat = project(keep, got, lows)
+    part, feat = first_project(keep, got, low)
+    (part,) = small(
+        second_project_kernel, [jax.ShapeDtypeStruct(part.shape, wide)], part, feat, other
+    )
     part_got = along_x(part, 0)
 
     narrow_pieces = jax.ShapeDtypeStruct((2, 2, 2 * R, OWN), narrow)
@@ -267,9 +272,13 @@
     second = second_neighbour(sent).astype(wide)
     second = jnp.where(far, second[::-1], second)
     around = quad + first_neighbour(sent).astype(wide) + second
-    total = around[0] + swapped(around[1].astype(narrow), QUAD).astype(wide)
-    mixed = [total[half * R : (half + 1) * R] * (-step_size / 3.0) for half in range(2)]
-    return (mixed[0].T[None], mixed[1].T[None])
+    final = swapped(around[1].astype(narrow), QUAD)
+    mixed = []
+    for half in range(2):
+        rows = slice(half * R, (half + 1) * R)
+        total = around[0, rows] + final[rows].astype(wide)
+        mixed.append((total * (-step_size / 3.0)).T[None])
+    return tuple(mixed)
 
 
 def solution(mesh):

time: 110 us -> 110 us (level)
    ppermute x5, waiting for transfers between devices: 12.2 us -> 11 us  [along_x(): return lax.ppermute(array, ('blk', 'x'), pairs)]
  transfers between devices with their start and end apart: 12 -> 12, of which waited for: 7 -> 7; matrix products, arithmetic and copies ran while one was open for 0% -> 0% of each run, Pallas kernels for 5% -> 6%
where the time goes in v8:
time: 110 us; the launch traced here: 109 us
  starting transfers between devices  51 us (46%)
  waiting for transfers between devices  28 us (25%)
  blocking collectives  19.7 us (18%)
  Pallas kernels  7.63 us (7%)
  other arithmetic  1.77 us (2%)
    ppermute x5, starting transfers between devices, swapped(): lax.ppermute(array, ('half', 'near'), [(i, i ^ by) for i in range(NZ)])  23.8 us
    all_to_all x1, blocking collectives, local(): lax.all_to_all(jnp.broadcast_to(pair, (QUAD,) + pair.shape), 'near', 0, 0...  19.7 us
    ppermute x5, starting transfers between devices, along_x(): return lax.ppermute(array, ('blk', 'x'), pairs)  16 us
    ppermute x5, waiting for transfers between devices, swapped(): lax.ppermute(array, ('half', 'near'), [(i, i ^ by) for i in range(NZ)])  13.8 us
    ppermute x5, waiting for transfers between devices, along_x(): return lax.ppermute(array, ('blk', 'x'), pairs)  11 us
    ppermute x1, starting transfers between devices, second_neighbour(): return lax.ppermute(array, ('blk', 'half', 'near'), pairs)  9.39 us
    pallas_call x1, Pallas kernels, prep(): pl.pallas_call(prep_kernel, in_specs=[pl.BlockSpec(memory_space=pl.ANY),...  4.46 us
    ppermute x1, waiting for transfers between devices, second_neighbour(): return lax.ppermute(array, ('blk', 'half', 'near'), pairs)  3.28 us
  transfers between devices with their start and end apart: 12, of which 7 were waited for; matrix products, arithmetic and copies ran while one was open for 0% of the time, Pallas kernels for 6%

profile of v8, /device:TPU:25, one launch (start us, length us, event | category | flops | bytes accessed | tf_op | source)
XLA Modules:
  0.0 109.1 jit_solution(877288419219734063)
XLA Ops:
  0.6 0.9 fusion.9
  1.5 8.8 %collective-permute-start.1 = (bf16[128,256]{1,0:T(8,128)(2,1)S(1)}, bf16[128,256]{1,0:T(8,128)(2,1)S(1)}, u32[]{:S(2)}, u32[]{:S(2)}) collective-permute-start(bf16[128,256]{1,0:T(8,128)(2,1)S(1)} %fusion.9), channel_id=1, source_target_pairs={{0,16},{4,20},{8,24},{12,28},{16,0},{20,4},{24,8},{28,12},{1,17},{... | collective-permute-start | bytes 196616 | tf_op jit(solution)/shard_map/ppermute | solution.py:213
  10.3 0.0 copy-start.1
  10.4 0.0 copy-start.2
  10.4 4.5 %shard_map.68 = (bf16[2,8,2,128,256]{4,3,2,1,0:T(8,128)(2,1)}, bf16[2,8,2,128,256]{4,3,2,1,0:T(8,128)(2,1)}) custom-call(bf16[128,8192]{1,0:T(8,128)(2,1)} %bitcast.42, f32[1,8192]{1,0:T(1,128)} %bitcast.49, bf16[128,8192]{1,0:T(8,128)(2,1)} %bitcast.43), custom_call_target="tpu_custom_call" | custom-call | flops 6291456 | bytes 8388608 | tf_op jit(solution)/shard_map/pallas_call | solution.py:74
  14.8 0.0 copy-start
  14.8 4.5 %collective-permute-start = (bf16[2,8,2,128,256]{4,3,2,1,0:T(8,128)(2,1)}, bf16[2,8,2,128,256]{4,3,2,1,0:T(8,128)(2,1)S(1)}, u32[]{:S(2)}, u32[]{:S(2)}) collective-permute-start(bf16[2,8,2,128,256]{4,3,2,1,0:T(8,128)(2,1)} %get-tuple-element.16), channel_id=1, source_target_pairs={{0,1},{1,0},{2,3},{3,2},{32,35},{33,34},{34,33},{35,32},{64,65},{6... | collective-permute-start | bytes 6291464 | tf_op jit(solution)/shard_map/ppermute | solution.py:209
  19.4 0.0 copy-done.1
  19.4 0.0 copy-done.2
  19.4 0.0 collective-permute-done.1
  19.5 19.7 %all_to_all.5.low_ref = bf16[4,2,128,256]{3,2,1,0:T(8,128)(2,1)S(1)} all-to-all(bf16[4,2,128,256]{3,2,1,0:T(8,128)(2,1)S(1)} %broadcast_in_dim.13), channel_id=1, replica_groups=mesh['blk'=16,'half'=2,'near'=4,'x'=4] {'near'}, dimensions={0} | all-to-all | bytes 1048576 | tf_op jit(solution)/shard_map/all_to_all | solution.py:244
  39.2 1.9 %collective-permute-start.2 = (bf16[4,2,128,256]{3,2,1,0:T(8,128)(2,1)S(1)}, bf16[4,2,128,256]{3,2,1,0:T(8,128)(2,1)S(1)}, u32[]{:S(2)}, u32[]{:S(2)}) collective-permute-start(bf16[4,2,128,256]{3,2,1,0:T(8,128)(2,1)S(1)} %all_to_all.5.low_ref), channel_id=1, source_target_pairs={{0,3},{1,2},{2,1},{3,0},{32,33},{33,32},{34,35},{35,34},{64,67},{6... | collective-permute-start | bytes 1572872 | tf_op jit(solution)/shard_map/ppermute | solution.py:209
  41.1 2.1 %collective-permute-done.got_ref = bf16[2,8,2,128,256]{4,3,2,1,0:T(8,128)(2,1)S(1)} collective-permute-done((bf16[2,8,2,128,256]{4,3,2,1,0:T(8,128)(2,1)}, bf16[2,8,2,128,256]{4,3,2,1,0:T(8,128)(2,1)S(1)}, u32[]{:S(2)}, u32[]{:S(2)}) %collective-permute-start) | collective-permute-done | bytes 2097184 | tf_op jit(solution)/shard_map/ppermute | solution.py:209
  43.2 0.0 copy-done
  43.2 1.2 %shard_map.69 = (f32[2,128,128]{2,1,0:T(8,128)S(1)}, bf16[2,2,8,2,128,256]{5,4,3,2,1,0:T(8,128)(2,1)S(1)}) custom-call(bf16[2,8,2,128,256]{4,3,2,1,0:T(8,128)(2,1)S(1)} %copy-done, bf16[2,8,2,128,256]{4,3,2,1,0:T(8,128)(2,1)S(1)} %collective-permute-done.got_ref, bf16[4,2,128,256]{3,2,1,0:T(8,128)(2,1)S(1)} %all_to_all.5.low_ref), custom_call_target="tpu_custom_call" | custom-call | flops 268435456 | bytes 4194304 | tf_op jit(solution)/shard_map/pallas_call | solution.py:129
  44.4 5.0 %collective-permute-done.2.low_ref = bf16[4,2,128,256]{3,2,1,0:T(8,128)(2,1)S(1)} collective-permute-done((bf16[4,2,128,256]{3,2,1,0:T(8,128)(2,1)S(1)}, bf16[4,2,128,256]{3,2,1,0:T(8,128)(2,1)S(1)}, u32[]{:S(2)}, u32[]{:S(2)}) %collective-permute-start.2) | collective-permute-done | bytes 524320 | tf_op jit(solution)/shard_map/ppermute | solution.py:209
  49.4 0.8 shard_map.70.part_ref
  50.3 4.3 %collective-permute-start.3 = (f32[2,128,128]{2,1,0:T(8,128)S(1)}, f32[2,128,128]{2,1,0:T(8,128)S(1)}, u32[]{:S(2)}, u32[]{:S(2)}) collective-permute-start(f32[2,128,128]{2,1,0:T(8,128)S(1)} %shard_map.70.part_ref), channel_id=1, source_target_pairs={{0,1},{1,0},{2,3},{3,2},{32,35},{33,34},{34,33},{35,32},{64,65},{6... | collective-permute-start | bytes 393224 | tf_op jit(solution)/shard_map/ppermute | solution.py:209
  54.5 2.6 %collective-permute-done.3.got_ref = f32[2,128,128]{2,1,0:T(8,128)S(1)} collective-permute-done((f32[2,128,128]{2,1,0:T(8,128)S(1)}, f32[2,128,128]{2,1,0:T(8,128)S(1)}, u32[]{:S(2)}, u32[]{:S(2)}) %collective-permute-start.3) | collective-permute-done | bytes 131104 | tf_op jit(solution)/shard_map/ppermute | solution.py:209
  57.2 0.5 shard_map.71
  57.7 1.9 %collective-permute-start.5 = (bf16[2,2,128,256]{3,2,1,0:T(8,128)(2,1)S(1)}, bf16[2,2,128,256]{3,2,1,0:T(8,128)(2,1)S(1)}, u32[]{:S(2)}, u32[]{:S(2)}) collective-permute-start(bf16[2,2,128,256]{3,2,1,0:T(8,128)(2,1)S(1)} %get-tuple-element.24), channel_id=1, source_target_pairs={{0,3},{1,2},{2,1},{3,0},{32,33},{33,32},{34,35},{35,34},{64,67},{6... | collective-permute-start | bytes 786440 | tf_op jit(solution)/shard_map/ppermute | solution.py:209
  59.6 3.4 %collective-permute-start.4 = (bf16[2,2,128,256]{3,2,1,0:T(8,128)(2,1)S(1)}, bf16[2,2,128,256]{3,2,1,0:T(8,128)(2,1)S(1)}, u32[]{:S(2)}, u32[]{:S(2)}) collective-permute-start(bf16[2,2,128,256]{3,2,1,0:T(8,128)(2,1)S(1)} %get-tuple-element.21), channel_id=1, source_target_pairs={{0,3},{1,2},{2,1},{3,0},{32,33},{33,32},{34,35},{35,34},{64,67},{6... | collective-permute-start | bytes 786440 | tf_op jit(solution)/shard_map/ppermute | solution.py:209
  63.0 0.5 shard_map.72
  63.5 1.3 %collective-permute-done.5.got_ref = bf16[2,2,128,256]{3,2,1,0:T(8,128)(2,1)S(1)} collective-permute-done((bf16[2,2,128,256]{3,2,1,0:T(8,128)(2,1)S(1)}, bf16[2,2,128,256]{3,2,1,0:T(8,128)(2,1)S(1)}, u32[]{:S(2)}, u32[]{:S(2)}) %collective-permute-start.5) | collective-permute-done | bytes 262176 | tf_op jit(solution)/shard_map/ppermute | solution.py:209
  64.9 5.9 %collective-permute-start.6 = (bf16[2,128,256]{2,1,0:T(8,128)(2,1)S(1)}, bf16[2,128,256]{2,1,0:T(8,128)(2,1)S(1)}, u32[]{:S(2)}, u32[]{:S(2)}) collective-permute-start(bf16[2,128,256]{2,1,0:T(8,128)(2,1)S(1)} %get-tuple-element.25), channel_id=1, source_target_pairs={{0,12},{4,8},{8,4},{12,0},{16,28},{20,24},{24,20},{28,16},{1,13},{... | collective-permute-start | bytes 393224 | tf_op jit(solution)/shard_map/ppermute | solution.py:213
  70.8 1.9 %collective-permute-start.7 = (bf16[2,128,256]{2,1,0:T(8,128)(2,1)S(1)}, bf16[2,128,256]{2,1,0:T(8,128)(2,1)S(1)}, u32[]{:S(2)}, u32[]{:S(2)}) collective-permute-start(bf16[2,128,256]{2,1,0:T(8,128)(2,1)S(1)} %get-tuple-element.26), channel_id=1, source_target_pairs={{0,8},{4,12},{8,0},{12,4},{16,24},{20,28},{24,16},{28,20},{1,9},{5... | collective-permute-start | bytes 393224 | tf_op jit(solution)/shard_map/ppermute | solution.py:213
  72.7 0.0 collective-permute-done.4.got_ref
  72.7 0.1 shard_map.73
  72.8 2.2 %collective-permute-start.8 = (bf16[2,128,256]{2,1,0:T(8,128)(2,1)S(1)}, bf16[2,128,256]{2,1,0:T(8,128)(2,1)S(1)}, u32[]{:S(2)}, u32[]{:S(2)}) collective-permute-start(bf16[2,128,256]{2,1,0:T(8,128)(2,1)S(1)} %get-tuple-element.27), channel_id=1, source_target_pairs={{0,4},{4,0},{8,12},{12,8},{16,20},{20,16},{24,28},{28,24},{1,5},{5... | collective-permute-start | bytes 393224 | tf_op jit(solution)/shard_map/ppermute | solution.py:213
  75.0 0.0 collective-permute-done.6
  75.0 7.1 %collective-permute-done.7 = bf16[2,128,256]{2,1,0:T(8,128)(2,1)S(1)} collective-permute-done((bf16[2,128,256]{2,1,0:T(8,128)(2,1)S(1)}, bf16[2,128,256]{2,1,0:T(8,128)(2,1)S(1)}, u32[]{:S(2)}, u32[]{:S(2)}) %collective-permute-start.7) | collective-permute-done | bytes 131104 | tf_op jit(solution)/shard_map/ppermute | solution.py:213
  82.1 0.0 collective-permute-done.8
  82.1 0.1 fusion.8
  82.2 9.4 %collective-permute-start.10 = (bf16[2,128,256]{2,1,0:T(8,128)(2,1)S(1)}, bf16[2,128,256]{2,1,0:T(8,128)(2,1)S(1)}, u32[]{:S(2)}, u32[]{:S(2)}) collective-permute-start(bf16[2,128,256]{2,1,0:T(8,128)(2,1)S(1)} %fusion.8), channel_id=1, source_target_pairs={{0,496},{4,500},{8,504},{12,508},{16,480},{20,484},{24,488},{28,49... | collective-permute-start | bytes 393224 | tf_op jit(solution)/shard_map/ppermute | solution.py:234
  91.6 1.9 %collective-permute-start.9 = (bf16[2,128,256]{2,1,0:T(8,128)(2,1)S(1)}, bf16[2,128,256]{2,1,0:T(8,128)(2,1)S(1)}, u32[]{:S(2)}, u32[]{:S(2)}) collective-permute-start(bf16[2,128,256]{2,1,0:T(8,128)(2,1)S(1)} %fusion.8), channel_id=1, source_target_pairs={{0,32},{32,0},{64,96},{96,64},{128,160},{160,128},{192,224},{224,1... | collective-permute-start | bytes 393224 | tf_op jit(solution)/shard_map/ppermute | solution.py:225
  93.5 3.3 %collective-permute-done.10 = bf16[2,128,256]{2,1,0:T(8,128)(2,1)S(1)} collective-permute-done((bf16[2,128,256]{2,1,0:T(8,128)(2,1)S(1)}, bf16[2,128,256]{2,1,0:T(8,128)(2,1)S(1)}, u32[]{:S(2)}, u32[]{:S(2)}) %collective-permute-start.10) | collective-permute-done | bytes 131104 | tf_op jit(solution)/shard_map/ppermute | solution.py:234
  96.8 0.0 collective-permute-done.9
  96.8 0.1 fusion
  96.9 4.9 %collective-permute-start.11 = (bf16[128,256]{1,0:T(8,128)(2,1)S(1)}, bf16[128,256]{1,0:T(8,128)(2,1)S(1)}, u32[]{:S(2)}, u32[]{:S(2)}) collective-permute-start(bf16[128,256]{1,0:T(8,128)(2,1)S(1)} %fusion.1), channel_id=1, source_target_pairs={{0,16},{4,20},{8,24},{12,28},{16,0},{20,4},{24,8},{28,12},{1,17},{... | collective-permute-start | bytes 196616 | tf_op jit(solution)/shard_map/ppermute | solution.py:213
  101.8 6.6 %collective-permute-done.11 = bf16[128,256]{1,0:T(8,128)(2,1)S(1)} collective-permute-done((bf16[128,256]{1,0:T(8,128)(2,1)S(1)}, bf16[128,256]{1,0:T(8,128)(2,1)S(1)}, u32[]{:S(2)}, u32[]{:S(2)}) %collective-permute-start.11) | collective-permute-done | bytes 65568 | tf_op jit(solution)/shard_map/ppermute | solution.py:213
  108.5 0.7 fusion.4
  (7 shorter events, 0.1 us)
Async XLA Ops:
  1.5 17.9 %collective-permute-start.1 = (bf16[128,256]{1,0:T(8,128)(2,1)S(1)}, bf16[128,256]{1,0:T(8,128)(2,1)S(1)}, u32[]{:S(2)}, u32[]{:S(2)}) collective-permute-start(bf16[128,256]{1,0:T(8,128)(2,1)S(1)} %fusion.9), channel_id=1, source_target_pairs={{0,16},{4,20},{8,24},{12,28},{16,0},{20,4},{24,8},{28,12},{1,17},{... | collective-permute-start | bytes 196616 | tf_op jit(solution)/shard_map/ppermute | solution.py:213
  10.3 9.0 %copy-start.1 = (f32[1,256,64]{1,2,0:T(8,128)S(1)}, f32[1,256,64]{1,2,0:T(8,128)}, u32[]{:S(2)}) copy-start(f32[1,256,64]{1,2,0:T(8,128)} %param.8) | copy-start | bytes 196612
  10.4 9.0 %copy-start.2 = (f32[1,256,64]{1,2,0:T(8,128)S(1)}, f32[1,256,64]{1,2,0:T(8,128)}, u32[]{:S(2)}) copy-start(f32[1,256,64]{1,2,0:T(8,128)} %param.7) | copy-start | bytes 196612
  14.8 28.3 %copy-start = (bf16[2,8,2,128,256]{4,3,2,1,0:T(8,128)(2,1)S(1)}, bf16[2,8,2,128,256]{4,3,2,1,0:T(8,128)(2,1)}, u32[]{:S(2)}) copy-start(bf16[2,8,2,128,256]{4,3,2,1,0:T(8,128)(2,1)} %get-tuple-element.15.keep_ref) | copy-start | bytes 6291460
  14.8 28.3 %collective-permute-start = (bf16[2,8,2,128,256]{4,3,2,1,0:T(8,128)(2,1)}, bf16[2,8,2,128,256]{4,3,2,1,0:T(8,128)(2,1)S(1)}, u32[]{:S(2)}, u32[]{:S(2)}) collective-permute-start(bf16[2,8,2,128,256]{4,3,2,1,0:T(8,128)(2,1)} %get-tuple-element.16), channel_id=1, source_target_pairs={{0,1},{1,0},{2,3},{3,2},{32,35},{33,34},{34,33},{35,32},{64,65},{6... | collective-permute-start | bytes 6291464 | tf_op jit(solution)/shard_map/ppermute | solution.py:209
  39.2 10.2 %collective-permute-start.2 = (bf16[4,2,128,256]{3,2,1,0:T(8,128)(2,1)S(1)}, bf16[4,2,128,256]{3,2,1,0:T(8,128)(2,1)S(1)}, u32[]{:S(2)}, u32[]{:S(2)}) collective-permute-start(bf16[4,2,128,256]{3,2,1,0:T(8,128)(2,1)S(1)} %all_to_all.5.low_ref), channel_id=1, source_target_pairs={{0,3},{1,2},{2,1},{3,0},{32,33},{33,32},{34,35},{35,34},{64,67},{6... | collective-permute-start | bytes 1572872 | tf_op jit(solution)/shard_map/ppermute | solution.py:209
  50.3 6.9 %collective-permute-start.3 = (f32[2,128,128]{2,1,0:T(8,128)S(1)}, f32[2,128,128]{2,1,0:T(8,128)S(1)}, u32[]{:S(2)}, u32[]{:S(2)}) collective-permute-start(f32[2,128,128]{2,1,0:T(8,128)S(1)} %shard_map.70.part_ref), channel_id=1, source_target_pairs={{0,1},{1,0},{2,3},{3,2},{32,35},{33,34},{34,33},{35,32},{64,65},{6... | collective-permute-start | bytes 393224 | tf_op jit(solution)/shard_map/ppermute | solution.py:209
  57.7 7.1 %collective-permute-start.5 = (bf16[2,2,128,256]{3,2,1,0:T(8,128)(2,1)S(1)}, bf16[2,2,128,256]{3,2,1,0:T(8,128)(2,1)S(1)}, u32[]{:S(2)}, u32[]{:S(2)}) collective-permute-start(bf16[2,2,128,256]{3,2,1,0:T(8,128)(2,1)S(1)} %get-tuple-element.24), channel_id=1, source_target_pairs={{0,3},{1,2},{2,1},{3,0},{32,33},{33,32},{34,35},{35,34},{64,67},{6... | collective-permute-start | bytes 786440 | tf_op jit(solution)/shard_map/ppermute | solution.py:209
  59.6 13.1 %collective-permute-start.4 = (bf16[2,2,128,256]{3,2,1,0:T(8,128)(2,1)S(1)}, bf16[2,2,128,256]{3,2,1,0:T(8,128)(2,1)S(1)}, u32[]{:S(2)}, u32[]{:S(2)}) collective-permute-start(bf16[2,2,128,256]{3,2,1,0:T(8,128)(2,1)S(1)} %get-tuple-element.21), channel_id=1, source_target_pairs={{0,3},{1,2},{2,1},{3,0},{32,33},{33,32},{34,35},{35,34},{64,67},{6... | collective-permute-start | bytes 786440 | tf_op jit(solution)/shard_map/ppermute | solution.py:209
  64.9 10.1 %collective-permute-start.6 = (bf16[2,128,256]{2,1,0:T(8,128)(2,1)S(1)}, bf16[2,128,256]{2,1,0:T(8,128)(2,1)S(1)}, u32[]{:S(2)}, u32[]{:S(2)}) collective-permute-start(bf16[2,128,256]{2,1,0:T(8,128)(2,1)S(1)} %get-tuple-element.25), channel_id=1, source_target_pairs={{0,12},{4,8},{8,4},{12,0},{16,28},{20,24},{24,20},{28,16},{1,13},{... | collective-permute-start | bytes 393224 | tf_op jit(solution)/shard_map/ppermute | solution.py:213
  70.8 11.3 %collective-permute-start.7 = (bf16[2,128,256]{2,1,0:T(8,128)(2,1)S(1)}, bf16[2,128,256]{2,1,0:T(8,128)(2,1)S(1)}, u32[]{:S(2)}, u32[]{:S(2)}) collective-permute-start(bf16[2,128,256]{2,1,0:T(8,128)(2,1)S(1)} %get-tuple-element.26), channel_id=1, source_target_pairs={{0,8},{4,12},{8,0},{12,4},{16,24},{20,28},{24,16},{28,20},{1,9},{5... | collective-permute-start | bytes 393224 | tf_op jit(solution)/shard_map/ppermute | solution.py:213
  72.8 9.3 %collective-permute-start.8 = (bf16[2,128,256]{2,1,0:T(8,128)(2,1)S(1)}, bf16[2,128,256]{2,1,0:T(8,128)(2,1)S(1)}, u32[]{:S(2)}, u32[]{:S(2)}) collective-permute-start(bf16[2,128,256]{2,1,0:T(8,128)(2,1)S(1)} %get-tuple-element.27), channel_id=1, source_target_pairs={{0,4},{4,0},{8,12},{12,8},{16,20},{20,16},{24,28},{28,24},{1,5},{5... | collective-permute-start | bytes 393224 | tf_op jit(solution)/shard_map/ppermute | solution.py:213
  82.2 14.6 %collective-permute-start.10 = (bf16[2,128,256]{2,1,0:T(8,128)(2,1)S(1)}, bf16[2,128,256]{2,1,0:T(8,128)(2,1)S(1)}, u32[]{:S(2)}, u32[]{:S(2)}) collective-permute-start(bf16[2,128,256]{2,1,0:T(8,128)(2,1)S(1)} %fusion.8), channel_id=1, source_target_pairs={{0,496},{4,500},{8,504},{12,508},{16,480},{20,484},{24,488},{28,49... | collective-permute-start | bytes 393224 | tf_op jit(solution)/shard_map/ppermute | solution.py:234
  91.6 5.2 %collective-permute-start.9 = (bf16[2,128,256]{2,1,0:T(8,128)(2,1)S(1)}, bf16[2,128,256]{2,1,0:T(8,128)(2,1)S(1)}, u32[]{:S(2)}, u32[]{:S(2)}) collective-permute-start(bf16[2,128,256]{2,1,0:T(8,128)(2,1)S(1)} %fusion.8), channel_id=1, source_target_pairs={{0,32},{32,0},{64,96},{96,64},{128,160},{160,128},{192,224},{224,1... | collective-permute-start | bytes 393224 | tf_op jit(solution)/shard_map/ppermute | solution.py:225
  96.9 11.5 %collective-permute-start.11 = (bf16[128,256]{1,0:T(8,128)(2,1)S(1)}, bf16[128,256]{1,0:T(8,128)(2,1)S(1)}, u32[]{:S(2)}, u32[]{:S(2)}) collective-permute-start(bf16[128,256]{1,0:T(8,128)(2,1)S(1)} %fusion.1), channel_id=1, source_target_pairs={{0,16},{4,20},{8,24},{12,28},{16,0},{20,4},{24,8},{28,12},{1,17},{... | collective-permute-start | bytes 196616 | tf_op jit(solution)/shard_map/ppermute | solution.py:213

commit v9 on v8

--- a/solution.py
+++ b/solution.py
@@ -146,30 +146,34 @@
 EARLY, LATE = (3, 2), (1, 0)
 
 
-def column_grads(low_ref, feat_ref, out_refs, column):
+def column_grads(low_ref, feat_ref, out_ref, column, nears):
     me = my_z()
-    for nears, out_ref in zip((EARLY, LATE), out_refs, strict=True):
-        for i, near in enumerate(nears):
-            for far in range(2):
-                for half, scale in enumerate((inv_width, inv_rank)):
-                    block = feat_ref[:, column, me ^ (near + QUAD * far), 1 - half]
-                    block = block.reshape(2 * TOK, OWN)
-                    grad = jnp.dot(low_ref[half], block, preferred_element_type=jnp.float32)
-                    rows = slice(half * R, (half + 1) * R)
-                    out_ref[i, far, rows] = (grad * scale).astype(out_ref.dtype)
-
-
-def other_kernel(part_ref, got_ref, feat_ref, early_ref, late_ref, low_ref):
+    for i, near in enumerate(nears):
+        for far in range(2):
+            for half, scale in enumerate((inv_width, inv_rank)):
+                block = feat_ref[:, column, me ^ (near + QUAD * far), 1 - half]
+                block = block.reshape(2 * TOK, OWN)
+                grad = jnp.dot(low_ref[half], block, preferred_element_type=jnp.float32)
+                rows = slice(half * R, (half + 1) * R)
+                out_ref[i, far, rows] = (grad * scale).astype(out_ref.dtype)
+
+
+def other_early_kernel(part_ref, got_ref, feat_ref, out_ref, low_ref):
     for t in range(2):
         total = part_ref[t] + got_ref[1 - t]
         at = slice(t * TOK, (t + 1) * TOK)
         low_ref[0, :, at] = (total[R:] * inv_rank).astype(jnp.bfloat16)
         low_ref[1, :, at] = (total[:R] * inv_width).astype(jnp.bfloat16)
-    column_grads(low_ref, feat_ref, (early_ref, late_ref), 1)
+    column_grads(low_ref, feat_ref, out_ref, 1, EARLY)
+
+
+def other_late_kernel(low_ref, feat_ref, out_ref):
+    column_grads(low_ref, feat_ref, out_ref, 1, LATE)
 
 
 def own_kernel(low_ref, feat_ref, early_ref, late_ref):
-    column_grads(low_ref, feat_ref, (early_ref, late_ref), 0)
+    column_grads(low_ref, feat_ref, early_ref, 0, EARLY)
+    column_grads(low_ref, feat_ref, late_ref, 0, LATE)
 
 
 def early_kernel(own_ref, got_ref, first_ref, second_ref):
@@ -255,10 +259,9 @@
     narrow_pieces = jax.ShapeDtypeStruct((2, 2, 2 * R, OWN), narrow)
     wide_pieces = jax.ShapeDtypeStruct(narrow_pieces.shape, wide)
     lowered = jax.ShapeDtypeStruct((2, R, 2 * TOK), narrow)
-    *theirs, lowered = small(
-        other_kernel, [narrow_pieces, narrow_pieces, lowered], part, part_got, feat
-    )
-    theirs = [along_x(pieces, 1) for pieces in theirs]
+    early, lowered = small(other_early_kernel, [narrow_pieces, lowered], part, part_got, feat)
+    (late,) = small(other_late_kernel, [narrow_pieces], lowered, feat)
+    theirs = [along_x(early, 1), along_x(late, 1)]
     mine = small(own_kernel, [wide_pieces, wide_pieces], lowered, feat)
     piece = jax.ShapeDtypeStruct((2, 2 * R, OWN), narrow)
     kept = jax.ShapeDtypeStruct(piece.shape, wide)

time: 110 us -> 110 us (level)
  no operation moved by 1% of the time
where the time goes in v9:
time: 110 us; the launch traced here: 109 us
  starting transfers between devices  51 us (46%)
  waiting for transfers between devices  27.7 us (25%)
  blocking collectives  19.7 us (18%)
  Pallas kernels  7.76 us (7%)
  other arithmetic  1.77 us (2%)
    ppermute x5, starting transfers between devices, swapped(): lax.ppermute(array, ('half', 'near'), [(i, i ^ by) for i in range(NZ)])  23.8 us
    all_to_all x1, blocking collectives, local(): lax.all_to_all(jnp.broadcast_to(pair, (QUAD,) + pair.shape), 'near', 0, 0...  19.7 us
    ppermute x5, starting transfers between devices, along_x(): return lax.ppermute(array, ('blk', 'x'), pairs)  16 us
    ppermute x5, waiting for transfers between devices, swapped(): lax.ppermute(array, ('half', 'near'), [(i, i ^ by) for i in range(NZ)])  13.8 us
    ppermute x5, waiting for transfers between devices, along_x(): return lax.ppermute(array, ('blk', 'x'), pairs)  10.7 us
    ppermute x1, starting transfers between devices, second_neighbour(): return lax.ppermute(array, ('blk', 'half', 'near'), pairs)  9.39 us
    pallas_call x1, Pallas kernels, prep(): pl.pallas_call(prep_kernel, in_specs=[pl.BlockSpec(memory_space=pl.ANY),...  4.46 us
    ppermute x1, waiting for transfers between devices, second_neighbour(): return lax.ppermute(array, ('blk', 'half', 'near'), pairs)  3.28 us
  transfers between devices with their start and end apart: 12, of which 7 were waited for; matrix products, arithmetic and copies ran while one was open for 0% of the time, Pallas kernels for 6%

profile of v9, /device:TPU:25, one launch (start us, length us, event | category | flops | bytes accessed | tf_op | source)
XLA Modules:
  0.0 109.0 jit_solution(16421905702870148108)
XLA Ops:
  0.6 0.9 fusion.9
  1.5 8.8 %collective-permute-start.1 = (bf16[128,256]{1,0:T(8,128)(2,1)S(1)}, bf16[128,256]{1,0:T(8,128)(2,1)S(1)}, u32[]{:S(2)}, u32[]{:S(2)}) collective-permute-start(bf16[128,256]{1,0:T(8,128)(2,1)S(1)} %fusion.9), channel_id=1, source_target_pairs={{0,16},{4,20},{8,24},{12,28},{16,0},{20,4},{24,8},{28,12},{1,17},{... | collective-permute-start | bytes 196616 | tf_op jit(solution)/shard_map/ppermute | solution.py:217
  10.3 0.0 copy-start.1
  10.4 0.0 copy-start.2
  10.4 4.5 %shard_map.68 = (bf16[2,8,2,128,256]{4,3,2,1,0:T(8,128)(2,1)}, bf16[2,8,2,128,256]{4,3,2,1,0:T(8,128)(2,1)}) custom-call(bf16[128,8192]{1,0:T(8,128)(2,1)} %bitcast.42, f32[1,8192]{1,0:T(1,128)} %bitcast.49, bf16[128,8192]{1,0:T(8,128)(2,1)} %bitcast.43), custom_call_target="tpu_custom_call" | custom-call | flops 6291456 | bytes 8388608 | tf_op jit(solution)/shard_map/pallas_call | solution.py:74
  14.8 0.0 copy-start
  14.8 4.5 %collective-permute-start = (bf16[2,8,2,128,256]{4,3,2,1,0:T(8,128)(2,1)}, bf16[2,8,2,128,256]{4,3,2,1,0:T(8,128)(2,1)S(1)}, u32[]{:S(2)}, u32[]{:S(2)}) collective-permute-start(bf16[2,8,2,128,256]{4,3,2,1,0:T(8,128)(2,1)} %get-tuple-element.15), channel_id=1, source_target_pairs={{0,1},{1,0},{2,3},{3,2},{32,35},{33,34},{34,33},{35,32},{64,65},{6... | collective-permute-start | bytes 6291464 | tf_op jit(solution)/shard_map/ppermute | solution.py:213
  19.4 0.0 copy-done.1
  19.4 0.0 copy-done.2
  19.4 0.0 collective-permute-done.1
  19.5 19.7 %all_to_all.5.low_ref = bf16[4,2,128,256]{3,2,1,0:T(8,128)(2,1)S(1)} all-to-all(bf16[4,2,128,256]{3,2,1,0:T(8,128)(2,1)S(1)} %broadcast_in_dim.13), channel_id=1, replica_groups=mesh['blk'=16,'half'=2,'near'=4,'x'=4] {'near'}, dimensions={0} | all-to-all | bytes 1048576 | tf_op jit(solution)/shard_map/all_to_all | solution.py:248
  39.2 1.9 %collective-permute-start.2 = (bf16[4,2,128,256]{3,2,1,0:T(8,128)(2,1)S(1)}, bf16[4,2,128,256]{3,2,1,0:T(8,128)(2,1)S(1)}, u32[]{:S(2)}, u32[]{:S(2)}) collective-permute-start(bf16[4,2,128,256]{3,2,1,0:T(8,128)(2,1)S(1)} %all_to_all.5.low_ref), channel_id=1, source_target_pairs={{0,3},{1,2},{2,1},{3,0},{32,33},{33,32},{34,35},{35,34},{64,67},{6... | collective-permute-start | bytes 1572872 | tf_op jit(solution)/shard_map/ppermute | solution.py:213
  41.1 2.1 %collective-permute-done.got_ref = bf16[2,8,2,128,256]{4,3,2,1,0:T(8,128)(2,1)S(1)} collective-permute-done((bf16[2,8,2,128,256]{4,3,2,1,0:T(8,128)(2,1)}, bf16[2,8,2,128,256]{4,3,2,1,0:T(8,128)(2,1)S(1)}, u32[]{:S(2)}, u32[]{:S(2)}) %collective-permute-start) | collective-permute-done | bytes 2097184 | tf_op jit(solution)/shard_map/ppermute | solution.py:213
  43.2 0.0 copy-done
  43.2 1.2 %shard_map.69 = (f32[2,128,128]{2,1,0:T(8,128)S(1)}, bf16[2,2,8,2,128,256]{5,4,3,2,1,0:T(8,128)(2,1)S(1)}) custom-call(bf16[2,8,2,128,256]{4,3,2,1,0:T(8,128)(2,1)S(1)} %copy-done, bf16[2,8,2,128,256]{4,3,2,1,0:T(8,128)(2,1)S(1)} %collective-permute-done.got_ref, bf16[4,2,128,256]{3,2,1,0:T(8,128)(2,1)S(1)} %all_to_all.5.low_ref), custom_call_target="tpu_custom_call" | custom-call | flops 268435456 | bytes 4194304 | tf_op jit(solution)/shard_map/pallas_call | solution.py:129
  44.4 5.0 %collective-permute-done.2.low_ref = bf16[4,2,128,256]{3,2,1,0:T(8,128)(2,1)S(1)} collective-permute-done((bf16[4,2,128,256]{3,2,1,0:T(8,128)(2,1)S(1)}, bf16[4,2,128,256]{3,2,1,0:T(8,128)(2,1)S(1)}, u32[]{:S(2)}, u32[]{:S(2)}) %collective-permute-start.2) | collective-permute-done | bytes 524320 | tf_op jit(solution)/shard_map/ppermute | solution.py:213
  49.4 0.8 shard_map.70.part_ref
  50.3 4.3 %collective-permute-start.3 = (f32[2,128,128]{2,1,0:T(8,128)S(1)}, f32[2,128,128]{2,1,0:T(8,128)S(1)}, u32[]{:S(2)}, u32[]{:S(2)}) collective-permute-start(f32[2,128,128]{2,1,0:T(8,128)S(1)} %shard_map.70.part_ref), channel_id=1, source_target_pairs={{0,1},{1,0},{2,3},{3,2},{32,35},{33,34},{34,33},{35,32},{64,65},{6... | collective-permute-start | bytes 393224 | tf_op jit(solution)/shard_map/ppermute | solution.py:213
  54.5 2.6 %collective-permute-done.3.got_ref = f32[2,128,128]{2,1,0:T(8,128)S(1)} collective-permute-done((f32[2,128,128]{2,1,0:T(8,128)S(1)}, f32[2,128,128]{2,1,0:T(8,128)S(1)}, u32[]{:S(2)}, u32[]{:S(2)}) %collective-permute-start.3) | collective-permute-done | bytes 131104 | tf_op jit(solution)/shard_map/ppermute | solution.py:213
  57.2 0.3 shard_map.71
  57.5 1.9 %collective-permute-start.5 = (bf16[2,2,128,256]{3,2,1,0:T(8,128)(2,1)S(1)}, bf16[2,2,128,256]{3,2,1,0:T(8,128)(2,1)S(1)}, u32[]{:S(2)}, u32[]{:S(2)}) collective-permute-start(bf16[2,2,128,256]{3,2,1,0:T(8,128)(2,1)S(1)} %get-tuple-element.22), channel_id=1, source_target_pairs={{0,3},{1,2},{2,1},{3,0},{32,33},{33,32},{34,35},{35,34},{64,67},{6... | collective-permute-start | bytes 786440 | tf_op jit(solution)/shard_map/ppermute | solution.py:213
  59.4 0.3 shard_map.73
  59.7 3.4 %collective-permute-start.4 = (bf16[2,2,128,256]{3,2,1,0:T(8,128)(2,1)S(1)}, bf16[2,2,128,256]{3,2,1,0:T(8,128)(2,1)S(1)}, u32[]{:S(2)}, u32[]{:S(2)}) collective-permute-start(bf16[2,2,128,256]{3,2,1,0:T(8,128)(2,1)S(1)} %shard_map.73), channel_id=1, source_target_pairs={{0,3},{1,2},{2,1},{3,0},{32,33},{33,32},{34,35},{35,34},{64,67},{6... | collective-permute-start | bytes 786440 | tf_op jit(solution)/shard_map/ppermute | solution.py:213
  63.1 0.5 shard_map.72
  63.6 1.0 collective-permute-done.5.got_ref
  64.7 5.9 %collective-permute-start.6 = (bf16[2,128,256]{2,1,0:T(8,128)(2,1)S(1)}, bf16[2,128,256]{2,1,0:T(8,128)(2,1)S(1)}, u32[]{:S(2)}, u32[]{:S(2)}) collective-permute-start(bf16[2,128,256]{2,1,0:T(8,128)(2,1)S(1)} %get-tuple-element.23), channel_id=1, source_target_pairs={{0,12},{4,8},{8,4},{12,0},{16,28},{20,24},{24,20},{28,16},{1,13},{... | collective-permute-start | bytes 393224 | tf_op jit(solution)/shard_map/ppermute | solution.py:217
  70.6 1.9 %collective-permute-start.7 = (bf16[2,128,256]{2,1,0:T(8,128)(2,1)S(1)}, bf16[2,128,256]{2,1,0:T(8,128)(2,1)S(1)}, u32[]{:S(2)}, u32[]{:S(2)}) collective-permute-start(bf16[2,128,256]{2,1,0:T(8,128)(2,1)S(1)} %get-tuple-element.24), channel_id=1, source_target_pairs={{0,8},{4,12},{8,0},{12,4},{16,24},{20,28},{24,16},{28,20},{1,9},{5... | collective-permute-start | bytes 393224 | tf_op jit(solution)/shard_map/ppermute | solution.py:217
  72.5 0.0 collective-permute-done.4.got_ref
  72.5 0.1 shard_map.74
  72.6 2.2 %collective-permute-start.8 = (bf16[2,128,256]{2,1,0:T(8,128)(2,1)S(1)}, bf16[2,128,256]{2,1,0:T(8,128)(2,1)S(1)}, u32[]{:S(2)}, u32[]{:S(2)}) collective-permute-start(bf16[2,128,256]{2,1,0:T(8,128)(2,1)S(1)} %get-tuple-element.25), channel_id=1, source_target_pairs={{0,4},{4,0},{8,12},{12,8},{16,20},{20,16},{24,28},{28,24},{1,5},{5... | collective-permute-start | bytes 393224 | tf_op jit(solution)/shard_map/ppermute | solution.py:217
  74.8 0.0 collective-permute-done.6
  74.8 7.1 %collective-permute-done.7 = bf16[2,128,256]{2,1,0:T(8,128)(2,1)S(1)} collective-permute-done((bf16[2,128,256]{2,1,0:T(8,128)(2,1)S(1)}, bf16[2,128,256]{2,1,0:T(8,128)(2,1)S(1)}, u32[]{:S(2)}, u32[]{:S(2)}) %collective-permute-start.7) | collective-permute-done | bytes 131104 | tf_op jit(solution)/shard_map/ppermute | solution.py:217
  81.9 0.0 collective-permute-done.8
  81.9 0.1 fusion.8
  82.0 9.4 %collective-permute-start.10 = (bf16[2,128,256]{2,1,0:T(8,128)(2,1)S(1)}, bf16[2,128,256]{2,1,0:T(8,128)(2,1)S(1)}, u32[]{:S(2)}, u32[]{:S(2)}) collective-permute-start(bf16[2,128,256]{2,1,0:T(8,128)(2,1)S(1)} %fusion.8), channel_id=1, source_target_pairs={{0,496},{4,500},{8,504},{12,508},{16,480},{20,484},{24,488},{28,49... | collective-permute-start | bytes 393224 | tf_op jit(solution)/shard_map/ppermute | solution.py:238
  91.4 1.9 %collective-permute-start.9 = (bf16[2,128,256]{2,1,0:T(8,128)(2,1)S(1)}, bf16[2,128,256]{2,1,0:T(8,128)(2,1)S(1)}, u32[]{:S(2)}, u32[]{:S(2)}) collective-permute-start(bf16[2,128,256]{2,1,0:T(8,128)(2,1)S(1)} %fusion.8), channel_id=1, source_target_pairs={{0,32},{32,0},{64,96},{96,64},{128,160},{160,128},{192,224},{224,1... | collective-permute-start | bytes 393224 | tf_op jit(solution)/shard_map/ppermute | solution.py:229
  93.3 3.3 %collective-permute-done.10 = bf16[2,128,256]{2,1,0:T(8,128)(2,1)S(1)} collective-permute-done((bf16[2,128,256]{2,1,0:T(8,128)(2,1)S(1)}, bf16[2,128,256]{2,1,0:T(8,128)(2,1)S(1)}, u32[]{:S(2)}, u32[]{:S(2)}) %collective-permute-start.10) | collective-permute-done | bytes 131104 | tf_op jit(solution)/shard_map/ppermute | solution.py:238
  96.6 0.0 collective-permute-done.9
  96.6 0.1 fusion
  96.8 4.9 %collective-permute-start.11 = (bf16[128,256]{1,0:T(8,128)(2,1)S(1)}, bf16[128,256]{1,0:T(8,128)(2,1)S(1)}, u32[]{:S(2)}, u32[]{:S(2)}) collective-permute-start(bf16[128,256]{1,0:T(8,128)(2,1)S(1)} %fusion.1), channel_id=1, source_target_pairs={{0,16},{4,20},{8,24},{12,28},{16,0},{20,4},{24,8},{28,12},{1,17},{... | collective-permute-start | bytes 196616 | tf_op jit(solution)/shard_map/ppermute | solution.py:217
  101.7 6.6 %collective-permute-done.11 = bf16[128,256]{1,0:T(8,128)(2,1)S(1)} collective-permute-done((bf16[128,256]{1,0:T(8,128)(2,1)S(1)}, bf16[128,256]{1,0:T(8,128)(2,1)S(1)}, u32[]{:S(2)}, u32[]{:S(2)}) %collective-permute-start.11) | collective-permute-done | bytes 65568 | tf_op jit(solution)/shard_map/ppermute | solution.py:217
  108.3 0.7 fusion.4
  (7 shorter events, 0.1 us)
Async XLA Ops:
  1.5 17.9 %collective-permute-start.1 = (bf16[128,256]{1,0:T(8,128)(2,1)S(1)}, bf16[128,256]{1,0:T(8,128)(2,1)S(1)}, u32[]{:S(2)}, u32[]{:S(2)}) collective-permute-start(bf16[128,256]{1,0:T(8,128)(2,1)S(1)} %fusion.9), channel_id=1, source_target_pairs={{0,16},{4,20},{8,24},{12,28},{16,0},{20,4},{24,8},{28,12},{1,17},{... | collective-permute-start | bytes 196616 | tf_op jit(solution)/shard_map/ppermute | solution.py:217
  10.3 9.0 %copy-start.1 = (f32[1,256,64]{1,2,0:T(8,128)S(1)}, f32[1,256,64]{1,2,0:T(8,128)}, u32[]{:S(2)}) copy-start(f32[1,256,64]{1,2,0:T(8,128)} %param.8) | copy-start | bytes 196612
  10.4 9.0 %copy-start.2 = (f32[1,256,64]{1,2,0:T(8,128)S(1)}, f32[1,256,64]{1,2,0:T(8,128)}, u32[]{:S(2)}) copy-start(f32[1,256,64]{1,2,0:T(8,128)} %param.7) | copy-start | bytes 196612
  14.8 28.3 %copy-start = (bf16[2,8,2,128,256]{4,3,2,1,0:T(8,128)(2,1)S(1)}, bf16[2,8,2,128,256]{4,3,2,1,0:T(8,128)(2,1)}, u32[]{:S(2)}) copy-start(bf16[2,8,2,128,256]{4,3,2,1,0:T(8,128)(2,1)} %get-tuple-element.14.keep_ref) | copy-start | bytes 6291460
  14.8 28.3 %collective-permute-start = (bf16[2,8,2,128,256]{4,3,2,1,0:T(8,128)(2,1)}, bf16[2,8,2,128,256]{4,3,2,1,0:T(8,128)(2,1)S(1)}, u32[]{:S(2)}, u32[]{:S(2)}) collective-permute-start(bf16[2,8,2,128,256]{4,3,2,1,0:T(8,128)(2,1)} %get-tuple-element.15), channel_id=1, source_target_pairs={{0,1},{1,0},{2,3},{3,2},{32,35},{33,34},{34,33},{35,32},{64,65},{6... | collective-permute-start | bytes 6291464 | tf_op jit(solution)/shard_map/ppermute | solution.py:213
  39.2 10.2 %collective-permute-start.2 = (bf16[4,2,128,256]{3,2,1,0:T(8,128)(2,1)S(1)}, bf16[4,2,128,256]{3,2,1,0:T(8,128)(2,1)S(1)}, u32[]{:S(2)}, u32[]{:S(2)}) collective-permute-start(bf16[4,2,128,256]{3,2,1,0:T(8,128)(2,1)S(1)} %all_to_all.5.low_ref), channel_id=1, source_target_pairs={{0,3},{1,2},{2,1},{3,0},{32,33},{33,32},{34,35},{35,34},{64,67},{6... | collective-permute-start | bytes 1572872 | tf_op jit(solution)/shard_map/ppermute | solution.py:213
  50.3 6.9 %collective-permute-start.3 = (f32[2,128,128]{2,1,0:T(8,128)S(1)}, f32[2,128,128]{2,1,0:T(8,128)S(1)}, u32[]{:S(2)}, u32[]{:S(2)}) collective-permute-start(f32[2,128,128]{2,1,0:T(8,128)S(1)} %shard_map.70.part_ref), channel_id=1, source_target_pairs={{0,1},{1,0},{2,3},{3,2},{32,35},{33,34},{34,33},{35,32},{64,65},{6... | collective-permute-start | bytes 393224 | tf_op jit(solution)/shard_map/ppermute | solution.py:213
  57.5 7.1 %collective-permute-start.5 = (bf16[2,2,128,256]{3,2,1,0:T(8,128)(2,1)S(1)}, bf16[2,2,128,256]{3,2,1,0:T(8,128)(2,1)S(1)}, u32[]{:S(2)}, u32[]{:S(2)}) collective-permute-start(bf16[2,2,128,256]{3,2,1,0:T(8,128)(2,1)S(1)} %get-tuple-element.22), channel_id=1, source_target_pairs={{0,3},{1,2},{2,1},{3,0},{32,33},{33,32},{34,35},{35,34},{64,67},{6... | collective-permute-start | bytes 786440 | tf_op jit(solution)/shard_map/ppermute | solution.py:213
  59.7 12.8 %collective-permute-start.4 = (bf16[2,2,128,256]{3,2,1,0:T(8,128)(2,1)S(1)}, bf16[2,2,128,256]{3,2,1,0:T(8,128)(2,1)S(1)}, u32[]{:S(2)}, u32[]{:S(2)}) collective-permute-start(bf16[2,2,128,256]{3,2,1,0:T(8,128)(2,1)S(1)} %shard_map.73), channel_id=1, source_target_pairs={{0,3},{1,2},{2,1},{3,0},{32,33},{33,32},{34,35},{35,34},{64,67},{6... | collective-permute-start | bytes 786440 | tf_op jit(solution)/shard_map/ppermute | solution.py:213
  64.7 10.1 %collective-permute-start.6 = (bf16[2,128,256]{2,1,0:T(8,128)(2,1)S(1)}, bf16[2,128,256]{2,1,0:T(8,128)(2,1)S(1)}, u32[]{:S(2)}, u32[]{:S(2)}) collective-permute-start(bf16[2,128,256]{2,1,0:T(8,128)(2,1)S(1)} %get-tuple-element.23), channel_id=1, source_target_pairs={{0,12},{4,8},{8,4},{12,0},{16,28},{20,24},{24,20},{28,16},{1,13},{... | collective-permute-start | bytes 393224 | tf_op jit(solution)/shard_map/ppermute | solution.py:217
  70.6 11.3 %collective-permute-start.7 = (bf16[2,128,256]{2,1,0:T(8,128)(2,1)S(1)}, bf16[2,128,256]{2,1,0:T(8,128)(2,1)S(1)}, u32[]{:S(2)}, u32[]{:S(2)}) collective-permute-start(bf16[2,128,256]{2,1,0:T(8,128)(2,1)S(1)} %get-tuple-element.24), channel_id=1, source_target_pairs={{0,8},{4,12},{8,0},{12,4},{16,24},{20,28},{24,16},{28,20},{1,9},{5... | collective-permute-start | bytes 393224 | tf_op jit(solution)/shard_map/ppermute | solution.py:217
  72.6 9.3 %collective-permute-start.8 = (bf16[2,128,256]{2,1,0:T(8,128)(2,1)S(1)}, bf16[2,128,256]{2,1,0:T(8,128)(2,1)S(1)}, u32[]{:S(2)}, u32[]{:S(2)}) collective-permute-start(bf16[2,128,256]{2,1,0:T(8,128)(2,1)S(1)} %get-tuple-element.25), channel_id=1, source_target_pairs={{0,4},{4,0},{8,12},{12,8},{16,20},{20,16},{24,28},{28,24},{1,5},{5... | collective-permute-start | bytes 393224 | tf_op jit(solution)/shard_map/ppermute | solution.py:217
  82.0 14.6 %collective-permute-start.10 = (bf16[2,128,256]{2,1,0:T(8,128)(2,1)S(1)}, bf16[2,128,256]{2,1,0:T(8,128)(2,1)S(1)}, u32[]{:S(2)}, u32[]{:S(2)}) collective-permute-start(bf16[2,128,256]{2,1,0:T(8,128)(2,1)S(1)} %fusion.8), channel_id=1, source_target_pairs={{0,496},{4,500},{8,504},{12,508},{16,480},{20,484},{24,488},{28,49... | collective-permute-start | bytes 393224 | tf_op jit(solution)/shard_map/ppermute | solution.py:238
  91.4 5.2 %collective-permute-start.9 = (bf16[2,128,256]{2,1,0:T(8,128)(2,1)S(1)}, bf16[2,128,256]{2,1,0:T(8,128)(2,1)S(1)}, u32[]{:S(2)}, u32[]{:S(2)}) collective-permute-start(bf16[2,128,256]{2,1,0:T(8,128)(2,1)S(1)} %fusion.8), channel_id=1, source_target_pairs={{0,32},{32,0},{64,96},{96,64},{128,160},{160,128},{192,224},{224,1... | collective-permute-start | bytes 393224 | tf_op jit(solution)/shard_map/ppermute | solution.py:229
  96.8 11.5 %collective-permute-start.11 = (bf16[128,256]{1,0:T(8,128)(2,1)S(1)}, bf16[128,256]{1,0:T(8,128)(2,1)S(1)}, u32[]{:S(2)}, u32[]{:S(2)}) collective-permute-start(bf16[128,256]{1,0:T(8,128)(2,1)S(1)} %fusion.1), channel_id=1, source_target_pairs={{0,16},{4,20},{8,24},{12,28},{16,0},{20,4},{24,8},{28,12},{1,17},{... | collective-permute-start | bytes 196616 | tf_op jit(solution)/shard_map/ppermute | solution.py:217

commit v10 on v9

--- a/solution.py
+++ b/solution.py
@@ -23,7 +23,7 @@
 inv_rank = R ** (-0.5)
 step_size = learning_rate / TOKENS**0.5
 
-ROWS = 32
+ROWS = 64
 CHUNKS = TOK // ROWS
 
 LAST = (((1,), (1,)), ((), ()))

time: 110 us -> 110 us (level)
  no operation moved by 1% of the time
where the time goes in v10:
time: 110 us; the launch traced here: 109 us
  starting transfers between devices  51 us (46%)
  waiting for transfers between devices  27.8 us (25%)
  blocking collectives  19.7 us (18%)
  Pallas kernels  7.98 us (7%)
  other arithmetic  1.77 us (2%)
    ppermute x5, starting transfers between devices, swapped(): lax.ppermute(array, ('half', 'near'), [(i, i ^ by) for i in range(NZ)])  23.6 us
    all_to_all x1, blocking collectives, local(): lax.all_to_all(jnp.broadcast_to(pair, (QUAD,) + pair.shape), 'near', 0, 0...  19.7 us
    ppermute x5, starting transfers between devices, along_x(): return lax.ppermute(array, ('blk', 'x'), pairs)  16 us
    ppermute x5, waiting for transfers between devices, swapped(): lax.ppermute(array, ('half', 'near'), [(i, i ^ by) for i in range(NZ)])  13.9 us
    ppermute x5, waiting for transfers between devices, along_x(): return lax.ppermute(array, ('blk', 'x'), pairs)  10.7 us
    ppermute x1, starting transfers between devices, second_neighbour(): return lax.ppermute(array, ('blk', 'half', 'near'), pairs)  9.46 us
    pallas_call x1, Pallas kernels, prep(): pl.pallas_call(prep_kernel, in_specs=[pl.BlockSpec(memory_space=pl.ANY),...  4.67 us
    ppermute x1, waiting for transfers between devices, second_neighbour(): return lax.ppermute(array, ('blk', 'half', 'near'), pairs)  3.23 us
  transfers between devices with their start and end apart: 12, of which 7 were waited for; matrix products, arithmetic and copies ran while one was open for 0% of the time, Pallas kernels for 6%

profile of v10, /device:TPU:25, one launch (start us, length us, event | category | flops | bytes accessed | tf_op | source)
XLA Modules:
  0.0 109.2 jit_solution(13767026935610496899)
XLA Ops:
  0.6 0.9 fusion.9
  1.5 8.8 %collective-permute-start.1 = (bf16[128,256]{1,0:T(8,128)(2,1)S(1)}, bf16[128,256]{1,0:T(8,128)(2,1)S(1)}, u32[]{:S(2)}, u32[]{:S(2)}) collective-permute-start(bf16[128,256]{1,0:T(8,128)(2,1)S(1)} %fusion.9), channel_id=1, source_target_pairs={{0,16},{4,20},{8,24},{12,28},{16,0},{20,4},{24,8},{28,12},{1,17},{... | collective-permute-start | bytes 196616 | tf_op jit(solution)/shard_map/ppermute | solution.py:217
  10.3 0.0 copy-start.1
  10.4 0.0 copy-start.2
  10.4 4.7 %shard_map.68 = (bf16[2,8,2,128,256]{4,3,2,1,0:T(8,128)(2,1)}, bf16[2,8,2,128,256]{4,3,2,1,0:T(8,128)(2,1)}) custom-call(bf16[128,8192]{1,0:T(8,128)(2,1)} %bitcast.42, f32[1,8192]{1,0:T(1,128)} %bitcast.49, bf16[128,8192]{1,0:T(8,128)(2,1)} %bitcast.43), custom_call_target="tpu_custom_call" | custom-call | flops 6291456 | bytes 8388608 | tf_op jit(solution)/shard_map/pallas_call | solution.py:74
  15.0 0.0 copy-start
  15.0 4.5 %collective-permute-start = (bf16[2,8,2,128,256]{4,3,2,1,0:T(8,128)(2,1)}, bf16[2,8,2,128,256]{4,3,2,1,0:T(8,128)(2,1)S(1)}, u32[]{:S(2)}, u32[]{:S(2)}) collective-permute-start(bf16[2,8,2,128,256]{4,3,2,1,0:T(8,128)(2,1)} %get-tuple-element.15), channel_id=1, source_target_pairs={{0,1},{1,0},{2,3},{3,2},{32,35},{33,34},{34,33},{35,32},{64,65},{6... | collective-permute-start | bytes 6291464 | tf_op jit(solution)/shard_map/ppermute | solution.py:213
  19.6 0.0 copy-done.1
  19.6 0.0 copy-done.2
  19.6 0.0 collective-permute-done.1
  19.7 19.7 %all_to_all.5.low_ref = bf16[4,2,128,256]{3,2,1,0:T(8,128)(2,1)S(1)} all-to-all(bf16[4,2,128,256]{3,2,1,0:T(8,128)(2,1)S(1)} %broadcast_in_dim.13), channel_id=1, replica_groups=mesh['blk'=16,'half'=2,'near'=4,'x'=4] {'near'}, dimensions={0} | all-to-all | bytes 1048576 | tf_op jit(solution)/shard_map/all_to_all | solution.py:248
  39.4 1.9 %collective-permute-start.2 = (bf16[4,2,128,256]{3,2,1,0:T(8,128)(2,1)S(1)}, bf16[4,2,128,256]{3,2,1,0:T(8,128)(2,1)S(1)}, u32[]{:S(2)}, u32[]{:S(2)}) collective-permute-start(bf16[4,2,128,256]{3,2,1,0:T(8,128)(2,1)S(1)} %all_to_all.5.low_ref), channel_id=1, source_target_pairs={{0,3},{1,2},{2,1},{3,0},{32,33},{33,32},{34,35},{35,34},{64,67},{6... | collective-permute-start | bytes 1572872 | tf_op jit(solution)/shard_map/ppermute | solution.py:213
  41.3 2.1 %collective-permute-done.got_ref = bf16[2,8,2,128,256]{4,3,2,1,0:T(8,128)(2,1)S(1)} collective-permute-done((bf16[2,8,2,128,256]{4,3,2,1,0:T(8,128)(2,1)}, bf16[2,8,2,128,256]{4,3,2,1,0:T(8,128)(2,1)S(1)}, u32[]{:S(2)}, u32[]{:S(2)}) %collective-permute-start) | collective-permute-done | bytes 2097184 | tf_op jit(solution)/shard_map/ppermute | solution.py:213
  43.4 0.0 copy-done
  43.4 1.3 %shard_map.69 = (f32[2,128,128]{2,1,0:T(8,128)S(1)}, bf16[2,2,8,2,128,256]{5,4,3,2,1,0:T(8,128)(2,1)S(1)}) custom-call(bf16[2,8,2,128,256]{4,3,2,1,0:T(8,128)(2,1)S(1)} %copy-done, bf16[2,8,2,128,256]{4,3,2,1,0:T(8,128)(2,1)S(1)} %collective-permute-done.got_ref, bf16[4,2,128,256]{3,2,1,0:T(8,128)(2,1)S(1)} %all_to_all.5.low_ref), custom_call_target="tpu_custom_call" | custom-call | flops 268435456 | bytes 4194304 | tf_op jit(solution)/shard_map/pallas_call | solution.py:129
  44.7 5.0 %collective-permute-done.2.low_ref = bf16[4,2,128,256]{3,2,1,0:T(8,128)(2,1)S(1)} collective-permute-done((bf16[4,2,128,256]{3,2,1,0:T(8,128)(2,1)S(1)}, bf16[4,2,128,256]{3,2,1,0:T(8,128)(2,1)S(1)}, u32[]{:S(2)}, u32[]{:S(2)}) %collective-permute-start.2) | collective-permute-done | bytes 524320 | tf_op jit(solution)/shard_map/ppermute | solution.py:213
  49.6 0.8 shard_map.70.part_ref
  50.5 4.3 %collective-permute-start.3 = (f32[2,128,128]{2,1,0:T(8,128)S(1)}, f32[2,128,128]{2,1,0:T(8,128)S(1)}, u32[]{:S(2)}, u32[]{:S(2)}) collective-permute-start(f32[2,128,128]{2,1,0:T(8,128)S(1)} %shard_map.70.part_ref), channel_id=1, source_target_pairs={{0,1},{1,0},{2,3},{3,2},{32,35},{33,34},{34,33},{35,32},{64,65},{6... | collective-permute-start | bytes 393224 | tf_op jit(solution)/shard_map/ppermute | solution.py:213
  54.7 2.7 %collective-permute-done.3.got_ref = f32[2,128,128]{2,1,0:T(8,128)S(1)} collective-permute-done((f32[2,128,128]{2,1,0:T(8,128)S(1)}, f32[2,128,128]{2,1,0:T(8,128)S(1)}, u32[]{:S(2)}, u32[]{:S(2)}) %collective-permute-start.3) | collective-permute-done | bytes 131104 | tf_op jit(solution)/shard_map/ppermute | solution.py:213
  57.4 0.3 shard_map.71
  57.7 1.9 %collective-permute-start.5 = (bf16[2,2,128,256]{3,2,1,0:T(8,128)(2,1)S(1)}, bf16[2,2,128,256]{3,2,1,0:T(8,128)(2,1)S(1)}, u32[]{:S(2)}, u32[]{:S(2)}) collective-permute-start(bf16[2,2,128,256]{3,2,1,0:T(8,128)(2,1)S(1)} %get-tuple-element.22), channel_id=1, source_target_pairs={{0,3},{1,2},{2,1},{3,0},{32,33},{33,32},{34,35},{35,34},{64,67},{6... | collective-permute-start | bytes 786440 | tf_op jit(solution)/shard_map/ppermute | solution.py:213
  59.6 0.3 shard_map.73
  60.0 3.4 %collective-permute-start.4 = (bf16[2,2,128,256]{3,2,1,0:T(8,128)(2,1)S(1)}, bf16[2,2,128,256]{3,2,1,0:T(8,128)(2,1)S(1)}, u32[]{:S(2)}, u32[]{:S(2)}) collective-permute-start(bf16[2,2,128,256]{3,2,1,0:T(8,128)(2,1)S(1)} %shard_map.73), channel_id=1, source_target_pairs={{0,3},{1,2},{2,1},{3,0},{32,33},{33,32},{34,35},{35,34},{64,67},{6... | collective-permute-start | bytes 786440 | tf_op jit(solution)/shard_map/ppermute | solution.py:213
  63.3 0.5 shard_map.72
  63.8 1.0 collective-permute-done.5.got_ref
  64.9 5.9 %collective-permute-start.6 = (bf16[2,128,256]{2,1,0:T(8,128)(2,1)S(1)}, bf16[2,128,256]{2,1,0:T(8,128)(2,1)S(1)}, u32[]{:S(2)}, u32[]{:S(2)}) collective-permute-start(bf16[2,128,256]{2,1,0:T(8,128)(2,1)S(1)} %get-tuple-element.23), channel_id=1, source_target_pairs={{0,12},{4,8},{8,4},{12,0},{16,28},{20,24},{24,20},{28,16},{1,13},{... | collective-permute-start | bytes 393224 | tf_op jit(solution)/shard_map/ppermute | solution.py:217
  70.8 1.9 %collective-permute-start.7 = (bf16[2,128,256]{2,1,0:T(8,128)(2,1)S(1)}, bf16[2,128,256]{2,1,0:T(8,128)(2,1)S(1)}, u32[]{:S(2)}, u32[]{:S(2)}) collective-permute-start(bf16[2,128,256]{2,1,0:T(8,128)(2,1)S(1)} %get-tuple-element.24), channel_id=1, source_target_pairs={{0,8},{4,12},{8,0},{12,4},{16,24},{20,28},{24,16},{28,20},{1,9},{5... | collective-permute-start | bytes 393224 | tf_op jit(solution)/shard_map/ppermute | solution.py:217
  72.7 0.0 collective-permute-done.4.got_ref
  72.7 0.1 shard_map.74
  72.8 2.2 %collective-permute-start.8 = (bf16[2,128,256]{2,1,0:T(8,128)(2,1)S(1)}, bf16[2,128,256]{2,1,0:T(8,128)(2,1)S(1)}, u32[]{:S(2)}, u32[]{:S(2)}) collective-permute-start(bf16[2,128,256]{2,1,0:T(8,128)(2,1)S(1)} %get-tuple-element.25), channel_id=1, source_target_pairs={{0,4},{4,0},{8,12},{12,8},{16,20},{20,16},{24,28},{28,24},{1,5},{5... | collective-permute-start | bytes 393224 | tf_op jit(solution)/shard_map/ppermute | solution.py:217
  75.0 0.0 collective-permute-done.6
  75.0 7.1 %collective-permute-done.7 = bf16[2,128,256]{2,1,0:T(8,128)(2,1)S(1)} collective-permute-done((bf16[2,128,256]{2,1,0:T(8,128)(2,1)S(1)}, bf16[2,128,256]{2,1,0:T(8,128)(2,1)S(1)}, u32[]{:S(2)}, u32[]{:S(2)}) %collective-permute-start.7) | collective-permute-done | bytes 131104 | tf_op jit(solution)/shard_map/ppermute | solution.py:217
  82.1 0.0 collective-permute-done.8
  82.1 0.1 fusion.8
  82.2 9.5 %collective-permute-start.10 = (bf16[2,128,256]{2,1,0:T(8,128)(2,1)S(1)}, bf16[2,128,256]{2,1,0:T(8,128)(2,1)S(1)}, u32[]{:S(2)}, u32[]{:S(2)}) collective-permute-start(bf16[2,128,256]{2,1,0:T(8,128)(2,1)S(1)} %fusion.8), channel_id=1, source_target_pairs={{0,496},{4,500},{8,504},{12,508},{16,480},{20,484},{24,488},{28,49... | collective-permute-start | bytes 393224 | tf_op jit(solution)/shard_map/ppermute | solution.py:238
  91.6 1.9 %collective-permute-start.9 = (bf16[2,128,256]{2,1,0:T(8,128)(2,1)S(1)}, bf16[2,128,256]{2,1,0:T(8,128)(2,1)S(1)}, u32[]{:S(2)}, u32[]{:S(2)}) collective-permute-start(bf16[2,128,256]{2,1,0:T(8,128)(2,1)S(1)} %fusion.8), channel_id=1, source_target_pairs={{0,32},{32,0},{64,96},{96,64},{128,160},{160,128},{192,224},{224,1... | collective-permute-start | bytes 393224 | tf_op jit(solution)/shard_map/ppermute | solution.py:229
  93.6 3.2 %collective-permute-done.10 = bf16[2,128,256]{2,1,0:T(8,128)(2,1)S(1)} collective-permute-done((bf16[2,128,256]{2,1,0:T(8,128)(2,1)S(1)}, bf16[2,128,256]{2,1,0:T(8,128)(2,1)S(1)}, u32[]{:S(2)}, u32[]{:S(2)}) %collective-permute-start.10) | collective-permute-done | bytes 131104 | tf_op jit(solution)/shard_map/ppermute | solution.py:238
  96.8 0.0 collective-permute-done.9
  96.8 0.1 fusion
  97.0 4.8 %collective-permute-start.11 = (bf16[128,256]{1,0:T(8,128)(2,1)S(1)}, bf16[128,256]{1,0:T(8,128)(2,1)S(1)}, u32[]{:S(2)}, u32[]{:S(2)}) collective-permute-start(bf16[128,256]{1,0:T(8,128)(2,1)S(1)} %fusion.1), channel_id=1, source_target_pairs={{0,16},{4,20},{8,24},{12,28},{16,0},{20,4},{24,8},{28,12},{1,17},{... | collective-permute-start | bytes 196616 | tf_op jit(solution)/shard_map/ppermute | solution.py:217
  101.7 6.8 %collective-permute-done.11 = bf16[128,256]{1,0:T(8,128)(2,1)S(1)} collective-permute-done((bf16[128,256]{1,0:T(8,128)(2,1)S(1)}, bf16[128,256]{1,0:T(8,128)(2,1)S(1)}, u32[]{:S(2)}, u32[]{:S(2)}) %collective-permute-start.11) | collective-permute-done | bytes 65568 | tf_op jit(solution)/shard_map/ppermute | solution.py:217
  108.5 0.7 fusion.4
  (7 shorter events, 0.1 us)
Async XLA Ops:
  1.5 18.1 %collective-permute-start.1 = (bf16[128,256]{1,0:T(8,128)(2,1)S(1)}, bf16[128,256]{1,0:T(8,128)(2,1)S(1)}, u32[]{:S(2)}, u32[]{:S(2)}) collective-permute-start(bf16[128,256]{1,0:T(8,128)(2,1)S(1)} %fusion.9), channel_id=1, source_target_pairs={{0,16},{4,20},{8,24},{12,28},{16,0},{20,4},{24,8},{28,12},{1,17},{... | collective-permute-start | bytes 196616 | tf_op jit(solution)/shard_map/ppermute | solution.py:217
  10.3 9.2 %copy-start.1 = (f32[1,256,64]{1,2,0:T(8,128)S(1)}, f32[1,256,64]{1,2,0:T(8,128)}, u32[]{:S(2)}) copy-start(f32[1,256,64]{1,2,0:T(8,128)} %param.8) | copy-start | bytes 196612
  10.4 9.2 %copy-start.2 = (f32[1,256,64]{1,2,0:T(8,128)S(1)}, f32[1,256,64]{1,2,0:T(8,128)}, u32[]{:S(2)}) copy-start(f32[1,256,64]{1,2,0:T(8,128)} %param.7) | copy-start | bytes 196612
  15.0 28.3 %copy-start = (bf16[2,8,2,128,256]{4,3,2,1,0:T(8,128)(2,1)S(1)}, bf16[2,8,2,128,256]{4,3,2,1,0:T(8,128)(2,1)}, u32[]{:S(2)}) copy-start(bf16[2,8,2,128,256]{4,3,2,1,0:T(8,128)(2,1)} %get-tuple-element.14.keep_ref) | copy-start | bytes 6291460
  15.0 28.3 %collective-permute-start = (bf16[2,8,2,128,256]{4,3,2,1,0:T(8,128)(2,1)}, bf16[2,8,2,128,256]{4,3,2,1,0:T(8,128)(2,1)S(1)}, u32[]{:S(2)}, u32[]{:S(2)}) collective-permute-start(bf16[2,8,2,128,256]{4,3,2,1,0:T(8,128)(2,1)} %get-tuple-element.15), channel_id=1, source_target_pairs={{0,1},{1,0},{2,3},{3,2},{32,35},{33,34},{34,33},{35,32},{64,65},{6... | collective-permute-start | bytes 6291464 | tf_op jit(solution)/shard_map/ppermute | solution.py:213
  39.4 10.2 %collective-permute-start.2 = (bf16[4,2,128,256]{3,2,1,0:T(8,128)(2,1)S(1)}, bf16[4,2,128,256]{3,2,1,0:T(8,128)(2,1)S(1)}, u32[]{:S(2)}, u32[]{:S(2)}) collective-permute-start(bf16[4,2,128,256]{3,2,1,0:T(8,128)(2,1)S(1)} %all_to_all.5.low_ref), channel_id=1, source_target_pairs={{0,3},{1,2},{2,1},{3,0},{32,33},{33,32},{34,35},{35,34},{64,67},{6... | collective-permute-start | bytes 1572872 | tf_op jit(solution)/shard_map/ppermute | solution.py:213
  50.5 6.9 %collective-permute-start.3 = (f32[2,128,128]{2,1,0:T(8,128)S(1)}, f32[2,128,128]{2,1,0:T(8,128)S(1)}, u32[]{:S(2)}, u32[]{:S(2)}) collective-permute-start(f32[2,128,128]{2,1,0:T(8,128)S(1)} %shard_map.70.part_ref), channel_id=1, source_target_pairs={{0,1},{1,0},{2,3},{3,2},{32,35},{33,34},{34,33},{35,32},{64,65},{6... | collective-permute-start | bytes 393224 | tf_op jit(solution)/shard_map/ppermute | solution.py:213
  57.7 7.1 %collective-permute-start.5 = (bf16[2,2,128,256]{3,2,1,0:T(8,128)(2,1)S(1)}, bf16[2,2,128,256]{3,2,1,0:T(8,128)(2,1)S(1)}, u32[]{:S(2)}, u32[]{:S(2)}) collective-permute-start(bf16[2,2,128,256]{3,2,1,0:T(8,128)(2,1)S(1)} %get-tuple-element.22), channel_id=1, source_target_pairs={{0,3},{1,2},{2,1},{3,0},{32,33},{33,32},{34,35},{35,34},{64,67},{6... | collective-permute-start | bytes 786440 | tf_op jit(solution)/shard_map/ppermute | solution.py:213
  60.0 12.8 %collective-permute-start.4 = (bf16[2,2,128,256]{3,2,1,0:T(8,128)(2,1)S(1)}, bf16[2,2,128,256]{3,2,1,0:T(8,128)(2,1)S(1)}, u32[]{:S(2)}, u32[]{:S(2)}) collective-permute-start(bf16[2,2,128,256]{3,2,1,0:T(8,128)(2,1)S(1)} %shard_map.73), channel_id=1, source_target_pairs={{0,3},{1,2},{2,1},{3,0},{32,33},{33,32},{34,35},{35,34},{64,67},{6... | collective-permute-start | bytes 786440 | tf_op jit(solution)/shard_map/ppermute | solution.py:213
  64.9 10.1 %collective-permute-start.6 = (bf16[2,128,256]{2,1,0:T(8,128)(2,1)S(1)}, bf16[2,128,256]{2,1,0:T(8,128)(2,1)S(1)}, u32[]{:S(2)}, u32[]{:S(2)}) collective-permute-start(bf16[2,128,256]{2,1,0:T(8,128)(2,1)S(1)} %get-tuple-element.23), channel_id=1, source_target_pairs={{0,12},{4,8},{8,4},{12,0},{16,28},{20,24},{24,20},{28,16},{1,13},{... | collective-permute-start | bytes 393224 | tf_op jit(solution)/shard_map/ppermute | solution.py:217
  70.8 11.3 %collective-permute-start.7 = (bf16[2,128,256]{2,1,0:T(8,128)(2,1)S(1)}, bf16[2,128,256]{2,1,0:T(8,128)(2,1)S(1)}, u32[]{:S(2)}, u32[]{:S(2)}) collective-permute-start(bf16[2,128,256]{2,1,0:T(8,128)(2,1)S(1)} %get-tuple-element.24), channel_id=1, source_target_pairs={{0,8},{4,12},{8,0},{12,4},{16,24},{20,28},{24,16},{28,20},{1,9},{5... | collective-permute-start | bytes 393224 | tf_op jit(solution)/shard_map/ppermute | solution.py:217
  72.8 9.3 %collective-permute-start.8 = (bf16[2,128,256]{2,1,0:T(8,128)(2,1)S(1)}, bf16[2,128,256]{2,1,0:T(8,128)(2,1)S(1)}, u32[]{:S(2)}, u32[]{:S(2)}) collective-permute-start(bf16[2,128,256]{2,1,0:T(8,128)(2,1)S(1)} %get-tuple-element.25), channel_id=1, source_target_pairs={{0,4},{4,0},{8,12},{12,8},{16,20},{20,16},{24,28},{28,24},{1,5},{5... | collective-permute-start | bytes 393224 | tf_op jit(solution)/shard_map/ppermute | solution.py:217
  82.2 14.6 %collective-permute-start.10 = (bf16[2,128,256]{2,1,0:T(8,128)(2,1)S(1)}, bf16[2,128,256]{2,1,0:T(8,128)(2,1)S(1)}, u32[]{:S(2)}, u32[]{:S(2)}) collective-permute-start(bf16[2,128,256]{2,1,0:T(8,128)(2,1)S(1)} %fusion.8), channel_id=1, source_target_pairs={{0,496},{4,500},{8,504},{12,508},{16,480},{20,484},{24,488},{28,49... | collective-permute-start | bytes 393224 | tf_op jit(solution)/shard_map/ppermute | solution.py:238
  91.6 5.2 %collective-permute-start.9 = (bf16[2,128,256]{2,1,0:T(8,128)(2,1)S(1)}, bf16[2,128,256]{2,1,0:T(8,128)(2,1)S(1)}, u32[]{:S(2)}, u32[]{:S(2)}) collective-permute-start(bf16[2,128,256]{2,1,0:T(8,128)(2,1)S(1)} %fusion.8), channel_id=1, source_target_pairs={{0,32},{32,0},{64,96},{96,64},{128,160},{160,128},{192,224},{224,1... | collective-permute-start | bytes 393224 | tf_op jit(solution)/shard_map/ppermute | solution.py:229
  97.0 11.5 %collective-permute-start.11 = (bf16[128,256]{1,0:T(8,128)(2,1)S(1)}, bf16[128,256]{1,0:T(8,128)(2,1)S(1)}, u32[]{:S(2)}, u32[]{:S(2)}) collective-permute-start(bf16[128,256]{1,0:T(8,128)(2,1)S(1)} %fusion.1), channel_id=1, source_target_pairs={{0,16},{4,20},{8,24},{12,28},{16,0},{20,4},{24,8},{28,12},{1,17},{... | collective-permute-start | bytes 196616 | tf_op jit(solution)/shard_map/ppermute | solution.py:217
